TPU v7x, 32 devices: a whole 2x2x4 slice. The times are simulated.
32 devices in a mesh: dp: 16 (over z, y, x), fsdp: 2 (over core).
Axes of the slice: x: 2, y: 2, z: 4, core: 2. Of those that a mesh axis runs over, the one named last changes fastest.
Arguments:
- inputs: bfloat16 [9216, 1024], P(('dp', 'fsdp')), may hold values from -6 to 6
- cotangent: bfloat16 [9216, 1024], P(('dp', 'fsdp')), may hold values from -6 to 6
- lengths: int32 [32, 3], P(('dp', 'fsdp')), may hold values from 0 to 288, as said below
- ffn1_in: bfloat16 [1024, 4096], P('fsdp'), may hold values from -0.1875 to 0.1875
- ffn1_out: bfloat16 [1024, 4096], P('fsdp'), may hold values from -0.09375 to 0.09375
- attn_qkv: bfloat16 [1024, 3072], P('fsdp'), may hold values from -0.1875 to 0.1875
- attn_out: bfloat16 [1024, 1024], P('fsdp'), may hold values from -1.5 to 1.5
- rel_table: bfloat16 [8, 65], P('fsdp'), may hold values from -4 to 4
- conv_in: bfloat16 [1024, 2048], P('fsdp'), may hold values from -0.1875 to 0.1875
- depth_kernel: bfloat16 [1024, 5], P('fsdp'), may hold values from -2.5 to 2.5
- conv_out: bfloat16 [1024, 1024], P('fsdp'), may hold values from -0.1875 to 0.1875
- ffn2_in: bfloat16 [1024, 4096], P('fsdp'), may hold values from -0.1875 to 0.1875
- ffn2_out: bfloat16 [1024, 4096], P('fsdp'), may hold values from -0.09375 to 0.09375
- gains: bfloat16 [1024, 6], P('fsdp'), may hold values from 0.5 to 1.5
- biases: bfloat16 [1024, 3], P('fsdp'), may hold values from -3 to 3
- inner_biases: bfloat16 [1024, 3], P('fsdp'), may hold values from -3 to 3
Outputs:
- layer_out: bfloat16 [9216, 1024], P(('dp', 'fsdp'))
- input_grad: bfloat16 [9216, 1024], P(('dp', 'fsdp'))
- ffn1_in_grad: float32 [1024, 4096], P('fsdp')
- ffn1_out_grad: float32 [1024, 4096], P('fsdp')
- attn_qkv_grad: float32 [1024, 3072], P('fsdp')
- attn_out_grad: float32 [1024, 1024], P('fsdp')
- rel_table_grad: float32 [8, 65], P('fsdp')
- conv_in_grad: float32 [1024, 2048], P('fsdp')
- depth_kernel_grad: float32 [1024, 5], P('fsdp')
- conv_out_grad: float32 [1024, 1024], P('fsdp')
- ffn2_in_grad: float32 [1024, 4096], P('fsdp')
- ffn2_out_grad: float32 [1024, 4096], P('fsdp')
- gains_grad: float32 [1024, 6], P('fsdp')
- biases_grad: float32 [1024, 3], P('fsdp')
- inner_biases_grad: float32 [1024, 3], P('fsdp')
Inputs may be any that keep to these rules, and one draw needn't show every extreme that they name: `lengths`: row g lists the utterances of group g: its length bucket holds n = 3, 2 or 1 utterances (the other entries are 0), each of 288 // n // 2 to 288 // n frames, the first of exactly 288 // n; some group has n = 1.
All inputs are finite; a program needn't handle non-finite values.
Results may differ from a plain program's by a relative error of at most 0.035.
Values may be sent and summed in bfloat16 or wider, within the bound.
A program may use at most 320 MiB of HBM per device.

v0:
```python
import jax
import jax.numpy as jnp
from jax import lax
from jax.sharding import PartitionSpec as P

EPSILON = 1e-05
MASKED = -1000000000.0
DOWN_DIMS = (((0,), (0,)), ((), ()))
ACROSS_DIMS = (((1,), (1,)), ((), ()))


def rows_norm(values, gain_col, bias_col):
    centre = values - jnp.mean(values, axis=-1, keepdims=True)
    spread = jnp.mean(centre * centre, axis=-1, keepdims=True)
    return centre * lax.rsqrt(spread + EPSILON) * gain_col + bias_col


def frame_masks(length_row, frames):
    end_one = length_row[0]
    end_two = end_one + length_row[1]
    end_three = end_two + length_row[2]
    places = jnp.arange(frames, dtype=jnp.int32)
    segment = (
        (places >= end_one).astype(jnp.int32)
        + (places >= end_two).astype(jnp.int32)
        + (places >= end_three).astype(jnp.int32)
    )
    valid_rows = (places < end_three).astype(jnp.float32)
    return (segment, valid_rows)


def shifted_rows(values, segment, offset):
    frames = values.shape[0]
    if offset > 0:
        moved_rows = jnp.concatenate(
            [values[offset:], jnp.zeros((offset, values.shape[1]), values.dtype)], axis=0
        )
        moved_seg = jnp.concatenate([segment[offset:], jnp.full((offset,), -1, jnp.int32)])
    elif offset < 0:
        moved_rows = jnp.concatenate(
            [jnp.zeros((-offset, values.shape[1]), values.dtype), values[: frames + offset]], axis=0
        )
        moved_seg = jnp.concatenate(
            [jnp.full((-offset,), -1, jnp.int32), segment[: frames + offset]]
        )
    else:
        moved_rows, moved_seg = (values, segment)
    return (moved_rows, moved_seg)


def depthwise(gated_rows, kernel, segment):
    tap_count = kernel.shape[1]
    running = jnp.zeros_like(gated_rows)
    for tap_index in range(tap_count):
        moved_rows, moved_seg = shifted_rows(gated_rows, segment, tap_index - tap_count // 2)
        keep_rows = (moved_seg == segment).astype(jnp.float32)
        running = running + kernel[:, tap_index][None, :] * moved_rows * keep_rows[:, None]
    return running


def glu_conv(front_rows, kernel, segment):
    half_width = kernel.shape[0]
    gated_rows = front_rows[:, :half_width] * jax.nn.sigmoid(front_rows[:, half_width:])
    return depthwise(gated_rows, kernel, segment)


def project(left, right):
    return jnp.dot(left, right, preferred_element_type=jnp.float32)


def project_back(left, right):
    return lax.dot_general(left, right, ACROSS_DIMS, preferred_element_type=jnp.float32)


def weight_grad(left, right):
    return lax.dot_general(left, right, DOWN_DIMS, preferred_element_type=jnp.float32)


def norm_back(grad_out, values, gain_col, bias_col):
    _, pull_back = jax.vjp(rows_norm, values, gain_col, bias_col)
    return pull_back(grad_out)


def silu_back(grad_out, before):
    _, pull_back = jax.vjp(jax.nn.silu, before)
    return pull_back(grad_out)[0]


def join_biases(outer_cols, inner_cols):
    return jnp.concatenate(
        [outer_cols[:, 0:2], inner_cols[:, 0:2], outer_cols[:, 2:3], inner_cols[:, 2:3]], axis=1
    )


def ffn_forward(values, gain_col, bias_col, weight_in, weight_out):
    normed = rows_norm(values, gain_col, bias_col).astype(jnp.bfloat16)
    before = project(normed, weight_in)
    hidden = jax.nn.silu(before).astype(jnp.bfloat16)
    return (project_back(hidden, weight_out), (normed, before, hidden))


def ffn_backward(grad_out, values, gain_col, bias_col, weight_in, weight_out, kept):
    normed, before, hidden = kept
    grad_low = grad_out.astype(jnp.bfloat16)
    grad_weight_out = weight_grad(grad_low, hidden)
    grad_before = silu_back(project(grad_low, weight_out), before).astype(jnp.bfloat16)
    grad_weight_in = weight_grad(normed, grad_before)
    grad_values, grad_gain, grad_bias = norm_back(
        project_back(grad_before, weight_in), values, gain_col, bias_col
    )
    return (grad_values, grad_weight_in, grad_weight_out, grad_gain, grad_bias)


def attn_scores(queries, key_rows, rel_bias, onehot, same_seg, score_scale):
    product = (
        jnp.einsum("qhe,khe->hqk", queries, key_rows, preferred_element_type=jnp.float32)
        * score_scale
    )
    relative = jnp.einsum("hr,rqk->hqk", rel_bias, onehot, precision=lax.Precision.HIGHEST)
    return jnp.where(same_seg[None], product + relative, MASKED)


def attn_forward(values, gain_col, bias_col, weight_qkv, weight_out, rel_bias, onehot, same_seg):
    frames = values.shape[0]
    head_count = rel_bias.shape[0]
    head_size = weight_qkv.shape[0] // head_count
    score_scale = head_size ** (-0.5)
    normed = rows_norm(values, gain_col, bias_col).astype(jnp.bfloat16)
    packed = (
        project(normed, weight_qkv).astype(jnp.bfloat16).reshape(frames, 3, head_count, head_size)
    )
    queries = packed[:, 0]
    key_rows = packed[:, 1]
    value_rows = packed[:, 2]
    scores = attn_scores(queries, key_rows, rel_bias, onehot, same_seg, score_scale)
    top_score = jnp.max(scores, axis=-1, keepdims=True)
    log_total = top_score + jnp.log(jnp.sum(jnp.exp(scores - top_score), axis=-1, keepdims=True))
    attend = jnp.exp(scores - log_total).astype(jnp.bfloat16)
    context = jnp.einsum("hqk,khe->qhe", attend, value_rows, preferred_element_type=jnp.float32)
    context = context.astype(jnp.bfloat16).reshape(frames, head_count * head_size)
    return (
        project(context, weight_out),
        (normed, queries, key_rows, value_rows, log_total, context),
    )


def attn_backward(
    grad_out, values, gain_col, bias_col, weight_qkv, weight_out, rel_bias, onehot, same_seg, kept
):
    normed, queries, key_rows, value_rows, log_total, context = kept
    frames, head_count, head_size = queries.shape
    score_scale = head_size ** (-0.5)
    grad_low = grad_out.astype(jnp.bfloat16)
    grad_weight_out = weight_grad(context, grad_low)
    grad_context = (
        project_back(grad_low, weight_out)
        .astype(jnp.bfloat16)
        .reshape(frames, head_count, head_size)
    )
    scores = attn_scores(queries, key_rows, rel_bias, onehot, same_seg, score_scale)
    attend = jnp.exp(scores - log_total)
    grad_attend = jnp.einsum(
        "qhe,khe->hqk", grad_context, value_rows, preferred_element_type=jnp.float32
    )
    grad_value = jnp.einsum(
        "hqk,qhe->khe",
        attend.astype(jnp.bfloat16),
        grad_context,
        preferred_element_type=jnp.float32,
    )
    grad_scores = attend * (grad_attend - jnp.sum(grad_attend * attend, axis=-1, keepdims=True))
    grad_rel = jnp.einsum("hqk,rqk->hr", grad_scores, onehot, precision=lax.Precision.HIGHEST)
    scores_low = grad_scores.astype(jnp.bfloat16)
    grad_query = (
        jnp.einsum("hqk,khe->qhe", scores_low, key_rows, preferred_element_type=jnp.float32)
        * score_scale
    )
    grad_key = (
        jnp.einsum("hqk,qhe->khe", scores_low, queries, preferred_element_type=jnp.float32)
        * score_scale
    )
    grad_packed = jnp.stack([grad_query, grad_key, grad_value], axis=1)
    grad_packed = grad_packed.reshape(frames, 3 * head_count * head_size).astype(jnp.bfloat16)
    grad_weight_qkv = weight_grad(normed, grad_packed)
    grad_values, grad_gain, grad_bias = norm_back(
        project_back(grad_packed, weight_qkv), values, gain_col, bias_col
    )
    return (grad_values, grad_weight_qkv, grad_weight_out, grad_rel, grad_gain, grad_bias)


def reduce_pair(first_grad, second_grad):
    parts = (
        lax.psum_scatter(
            first_grad.astype(jnp.bfloat16), "fsdp", scatter_dimension=0, tiled=True
        ).astype(jnp.float32),
        lax.psum_scatter(
            second_grad.astype(jnp.bfloat16), "fsdp", scatter_dimension=0, tiled=True
        ).astype(jnp.float32),
    )
    return (
        lax.psum(parts[0].astype(jnp.bfloat16), "dp").astype(jnp.float32),
        lax.psum(parts[1].astype(jnp.bfloat16), "dp").astype(jnp.float32),
    )


def reduce_rest(
    first_grad, second_grad, third_grad, fourth_grad, fifth_grad, sixth_grad, seventh_grad
):
    parts = (
        lax.psum_scatter(
            first_grad.astype(jnp.bfloat16), "fsdp", scatter_dimension=0, tiled=True
        ).astype(jnp.float32),
        lax.psum_scatter(
            second_grad.astype(jnp.bfloat16), "fsdp", scatter_dimension=0, tiled=True
        ).astype(jnp.float32),
        lax.psum_scatter(
            third_grad.astype(jnp.bfloat16), "fsdp", scatter_dimension=0, tiled=True
        ).astype(jnp.float32),
        lax.psum_scatter(
            fourth_grad.astype(jnp.bfloat16), "fsdp", scatter_dimension=0, tiled=True
        ).astype(jnp.float32),
        lax.psum_scatter(
            fifth_grad.astype(jnp.bfloat16), "fsdp", scatter_dimension=0, tiled=True
        ).astype(jnp.float32),
        lax.psum_scatter(
            sixth_grad.astype(jnp.bfloat16), "fsdp", scatter_dimension=0, tiled=True
        ).astype(jnp.float32),
        lax.psum_scatter(
            seventh_grad.astype(jnp.bfloat16), "fsdp", scatter_dimension=0, tiled=True
        ).astype(jnp.float32),
    )
    return (
        lax.psum(parts[0].astype(jnp.bfloat16), "dp").astype(jnp.float32),
        lax.psum(parts[1].astype(jnp.bfloat16), "dp").astype(jnp.float32),
        lax.psum(parts[2].astype(jnp.bfloat16), "dp").astype(jnp.float32),
        lax.psum(parts[3].astype(jnp.bfloat16), "dp").astype(jnp.float32),
        lax.psum(parts[4].astype(jnp.bfloat16), "dp").astype(jnp.float32),
        lax.psum(parts[5].astype(jnp.bfloat16), "dp").astype(jnp.float32),
        lax.psum(parts[6].astype(jnp.bfloat16), "dp").astype(jnp.float32),
    )


def per_device(
    inputs,
    cotangent,
    lengths,
    ffn1_in,
    ffn1_out,
    attn_qkv,
    attn_out,
    rel_table,
    conv_in,
    depth_kernel,
    conv_out,
    ffn2_in,
    ffn2_out,
    gains,
    biases,
    inner_biases,
):
    frames = inputs.shape[0]
    segment, valid_rows = frame_masks(lengths[0], frames)
    gathered = (
        lax.all_gather(ffn1_in, "fsdp", axis=0, tiled=True),
        lax.all_gather(ffn1_out, "fsdp", axis=0, tiled=True),
        lax.all_gather(attn_qkv, "fsdp", axis=0, tiled=True),
        lax.all_gather(attn_out, "fsdp", axis=0, tiled=True),
        lax.all_gather(rel_table, "fsdp", axis=0, tiled=True),
        lax.all_gather(conv_in, "fsdp", axis=0, tiled=True),
        lax.all_gather(depth_kernel, "fsdp", axis=0, tiled=True),
        lax.all_gather(conv_out, "fsdp", axis=0, tiled=True),
        lax.all_gather(ffn2_in, "fsdp", axis=0, tiled=True),
        lax.all_gather(ffn2_out, "fsdp", axis=0, tiled=True),
        lax.all_gather(gains, "fsdp", axis=0, tiled=True),
        lax.all_gather(biases, "fsdp", axis=0, tiled=True),
        lax.all_gather(inner_biases, "fsdp", axis=0, tiled=True),
    )
    (
        full_ffn1_in,
        full_ffn1_out,
        full_qkv,
        full_attn_out,
        full_rel,
        full_conv_in,
        full_kernel,
        full_conv_out,
        full_ffn2_in,
        full_ffn2_out,
        full_gains,
        full_biases,
        full_inner,
    ) = gathered
    rel_bias = full_rel.astype(jnp.float32)
    kernel = full_kernel.astype(jnp.float32)
    gain_cols = full_gains.astype(jnp.float32)
    bias_cols = join_biases(full_biases.astype(jnp.float32), full_inner.astype(jnp.float32))
    places = jnp.arange(frames, dtype=jnp.int32)
    reach = (rel_bias.shape[1] - 1) // 2
    rel_index = jnp.clip(places[None, :] - places[:, None], -reach, reach) + reach
    onehot = (
        rel_index[None] == jnp.arange(rel_bias.shape[1], dtype=jnp.int32)[:, None, None]
    ).astype(jnp.float32)
    same_seg = segment[:, None] == segment[None, :]
    stream_in = inputs.astype(jnp.float32)
    ffn_one, kept_one = ffn_forward(
        stream_in, gain_cols[:, 0], bias_cols[:, 0], full_ffn1_in, full_ffn1_out
    )
    after_ffn = stream_in + 0.5 * ffn_one
    attn_branch, kept_attn = attn_forward(
        after_ffn,
        gain_cols[:, 1],
        bias_cols[:, 1],
        full_qkv,
        full_attn_out,
        rel_bias,
        onehot,
        same_seg,
    )
    after_attn = after_ffn + attn_branch
    normed_conv = rows_norm(after_attn, gain_cols[:, 2], bias_cols[:, 2]).astype(jnp.bfloat16)
    front_rows = project(normed_conv, full_conv_in)
    mixed_rows = glu_conv(front_rows, kernel, segment)
    weighted = valid_rows[:, None] * mixed_rows
    totals = lax.psum(
        (jnp.sum(weighted, axis=0), jnp.sum(weighted * mixed_rows, axis=0), jnp.sum(valid_rows)),
        ("dp", "fsdp"),
    )
    valid_count = totals[2]
    bn_mean = totals[0] / valid_count
    bn_var = totals[1] / valid_count - bn_mean * bn_mean
    bn_rstd = lax.rsqrt(bn_var + EPSILON)
    bn_hat = (mixed_rows - bn_mean) * bn_rstd
    bn_out = bn_hat * gain_cols[:, 5] + bias_cols[:, 5]
    swish_low = jax.nn.silu(bn_out).astype(jnp.bfloat16)
    after_conv = after_attn + project(swish_low, full_conv_out)
    ffn_two, kept_two = ffn_forward(
        after_conv, gain_cols[:, 3], bias_cols[:, 3], full_ffn2_in, full_ffn2_out
    )
    after_ffn2 = after_conv + 0.5 * ffn_two
    layer_out = (
        valid_rows[:, None] * rows_norm(after_ffn2, gain_cols[:, 4], bias_cols[:, 4])
    ).astype(jnp.bfloat16)
    gathered = (
        lax.all_gather(ffn1_in, "fsdp", axis=0, tiled=True),
        lax.all_gather(ffn1_out, "fsdp", axis=0, tiled=True),
        lax.all_gather(attn_qkv, "fsdp", axis=0, tiled=True),
        lax.all_gather(attn_out, "fsdp", axis=0, tiled=True),
        lax.all_gather(rel_table, "fsdp", axis=0, tiled=True),
        lax.all_gather(conv_in, "fsdp", axis=0, tiled=True),
        lax.all_gather(depth_kernel, "fsdp", axis=0, tiled=True),
        lax.all_gather(conv_out, "fsdp", axis=0, tiled=True),
        lax.all_gather(ffn2_in, "fsdp", axis=0, tiled=True),
        lax.all_gather(ffn2_out, "fsdp", axis=0, tiled=True),
        lax.all_gather(gains, "fsdp", axis=0, tiled=True),
        lax.all_gather(biases, "fsdp", axis=0, tiled=True),
        lax.all_gather(inner_biases, "fsdp", axis=0, tiled=True),
    )
    (
        full_ffn1_in,
        full_ffn1_out,
        full_qkv,
        full_attn_out,
        full_rel,
        full_conv_in,
        full_kernel,
        full_conv_out,
        full_ffn2_in,
        full_ffn2_out,
        full_gains,
        full_biases,
        full_inner,
    ) = gathered
    rel_bias = full_rel.astype(jnp.float32)
    kernel = full_kernel.astype(jnp.float32)
    gain_cols = full_gains.astype(jnp.float32)
    bias_cols = join_biases(full_biases.astype(jnp.float32), full_inner.astype(jnp.float32))
    grad_final = valid_rows[:, None] * cotangent.astype(jnp.float32)
    grad_after_ffn2, grad_gain_final, grad_bias_final = norm_back(
        grad_final, after_ffn2, gain_cols[:, 4], bias_cols[:, 4]
    )
    branch_grad, grad_ffn2_in, grad_ffn2_out, grad_gain_two, grad_bias_two = ffn_backward(
        0.5 * grad_after_ffn2,
        after_conv,
        gain_cols[:, 3],
        bias_cols[:, 3],
        full_ffn2_in,
        full_ffn2_out,
        kept_two,
    )
    grad_after_conv = grad_after_ffn2 + branch_grad
    sum_ffn2_in, sum_ffn2_out = reduce_pair(grad_ffn2_in, grad_ffn2_out)
    conv_low = grad_after_conv.astype(jnp.bfloat16)
    grad_conv_out = weight_grad(swish_low, conv_low)
    grad_bn_out = silu_back(project_back(conv_low, full_conv_out), bn_out)
    grad_gain_bn = jnp.sum(grad_bn_out * bn_hat, axis=0)
    grad_bias_bn = jnp.sum(grad_bn_out, axis=0)
    grad_hat = grad_bn_out * gain_cols[:, 5]
    back_sums = lax.psum(
        (jnp.sum(grad_hat, axis=0), jnp.sum(grad_hat * bn_hat, axis=0)), ("dp", "fsdp")
    )
    grad_var = -0.5 * bn_rstd * bn_rstd * back_sums[1]
    grad_mean = -bn_rstd * back_sums[0] - 2.0 * bn_mean * grad_var
    grad_mixed = (
        grad_hat * bn_rstd
        + valid_rows[:, None] * (grad_mean + 2.0 * mixed_rows * grad_var) / valid_count
    )

    def conv_local(front_in, kernel_in):
        return glu_conv(front_in, kernel_in, segment)

    _, pull_back = jax.vjp(conv_local, front_rows, kernel)
    grad_front, grad_kernel = pull_back(grad_mixed)
    front_low = grad_front.astype(jnp.bfloat16)
    grad_conv_in = weight_grad(normed_conv, front_low)
    branch_grad, grad_gain_conv, grad_bias_conv = norm_back(
        project_back(front_low, full_conv_in), after_attn, gain_cols[:, 2], bias_cols[:, 2]
    )
    grad_after_attn = grad_after_conv + branch_grad
    sum_conv_in, sum_conv_out = reduce_pair(grad_conv_in, grad_conv_out)
    branch_grad, grad_qkv, grad_attn_out, grad_rel, grad_gain_attn, grad_bias_attn = attn_backward(
        grad_after_attn,
        after_ffn,
        gain_cols[:, 1],
        bias_cols[:, 1],
        full_qkv,
        full_attn_out,
        rel_bias,
        onehot,
        same_seg,
        kept_attn,
    )
    grad_after_ffn = grad_after_attn + branch_grad
    sum_qkv, sum_attn_out = reduce_pair(grad_qkv, grad_attn_out)
    branch_grad, grad_ffn1_in, grad_ffn1_out, grad_gain_one, grad_bias_one = ffn_backward(
        0.5 * grad_after_ffn,
        stream_in,
        gain_cols[:, 0],
        bias_cols[:, 0],
        full_ffn1_in,
        full_ffn1_out,
        kept_one,
    )
    grad_stream = grad_after_ffn + branch_grad
    grad_gains = jnp.stack(
        [
            grad_gain_one,
            grad_gain_attn,
            grad_gain_conv,
            grad_gain_two,
            grad_gain_final,
            grad_gain_bn,
        ],
        axis=1,
    )
    grad_outer = jnp.stack([grad_bias_one, grad_bias_attn, grad_bias_final], axis=1)
    grad_inner = jnp.stack([grad_bias_conv, grad_bias_two, grad_bias_bn], axis=1)
    rest_sums = reduce_rest(
        grad_ffn1_in, grad_ffn1_out, grad_rel, grad_kernel, grad_gains, grad_outer, grad_inner
    )
    return (
        layer_out,
        grad_stream.astype(jnp.bfloat16),
        rest_sums[0],
        rest_sums[1],
        sum_qkv,
        sum_attn_out,
        rest_sums[2],
        sum_conv_in,
        rest_sums[3],
        sum_conv_out,
        sum_ffn2_in,
        sum_ffn2_out,
        rest_sums[4],
        rest_sums[5],
        rest_sums[6],
    )


def solution(mesh):
    in_specs = (
        P(("dp", "fsdp"), None),
        P(("dp", "fsdp"), None),
        P(("dp", "fsdp"), None),
        P("fsdp", None),
        P("fsdp", None),
        P("fsdp", None),
        P("fsdp", None),
        P("fsdp", None),
        P("fsdp", None),
        P("fsdp", None),
        P("fsdp", None),
        P("fsdp", None),
        P("fsdp", None),
        P("fsdp", None),
        P("fsdp", None),
        P("fsdp", None),
    )
    out_specs = (
        P(("dp", "fsdp"), None),
        P(("dp", "fsdp"), None),
        P("fsdp", None),
        P("fsdp", None),
        P("fsdp", None),
        P("fsdp", None),
        P("fsdp", None),
        P("fsdp", None),
        P("fsdp", None),
        P("fsdp", None),
        P("fsdp", None),
        P("fsdp", None),
        P("fsdp", None),
        P("fsdp", None),
        P("fsdp", None),
    )
    return jax.shard_map(
        per_device, mesh=mesh, in_specs=in_specs, out_specs=out_specs, check_vma=False
    )
```

profile of v0, /device:TPU:0, one launch (start us, length us, event | category | flops | bytes accessed | tf_op | source)
XLA Modules:
  0.0 1144.4 jit_solution(10707450372127261846)
XLA Ops:
  30.9 6.8 fusion.1
  40.4 9.3 fusion.94
  49.6 5.1 all-gather.12.cloned.1.call-done
  54.8 7.6 fusion.115
  62.7 11.7 %all-gather.14.cloned.1.call-done = bf16[1024,3072]{1,0:T(8,128)(2,1)} async-done(((bf16[512,3072]{1,0:T(8,128)(2,1)}), bf16[1024,3072]{1,0:T(8,128)(2,1)}) %all-gather.14.cloned.1.call-update) | async-done | bytes 6291472 | tf_op jit(solution)/shard_map/all_gather | solution.py:266
  74.4 4.9 fusion.22
  93.0 10.8 all-gather.18.cloned.1.call-done
  113.2 41.4 %all-reduce.19 = (f32[1024]{0:T(1024)}, f32[]{:T(128)}, f32[1024]{0:T(1024)}) all-reduce(f32[1024]{0:T(1024)} %get-tuple-element.29, f32[]{:T(128)} %fusion.87, f32[1024]{0:T(1024)} %get-tuple-element.28), channel_id=1, replica_groups=mesh['dp'=16,'fsdp'=2] {'dp','fsdp'}, use_global_device_ids=true, to_apply=%region_13.14 | all-reduce | flops 2049 | bytes 16392 | tf_op jit(solution)/shard_map/psum | solution.py:324
  162.9 8.7 fusion.98
  171.6 7.9 fusion.119
  183.2 4.9 fusion.6
  188.2 5.2 multiply_reduce_fusion.4
  199.1 41.1 %all-reduce.18 = (f32[1024]{0:T(1024)}, f32[1024]{0:T(1024)}) all-reduce(f32[1024]{0:T(1024)} %get-tuple-element.16, f32[1024]{0:T(1024)} %get-tuple-element.27), channel_id=1, replica_groups=mesh['dp'=16,'fsdp'=2] {'dp','fsdp'}, use_global_device_ids=true, to_apply=%region_25.26 | all-reduce | flops 2048 | bytes 16384 | tf_op jit(solution)/shard_map/psum | solution.py:398
  265.5 6.9 convolution_convert_fusion.6
  282.2 5.7 convolution_convert_fusion.4
  288.4 5.1 multiply_reduce_fusion.6
  295.3 10.0 fusion.9
  306.8 7.1 convolution_convert_fusion.3
  313.9 10.4 convolution_convert_fusion.2
  325.6 9.2 convolution_convert_fusion.1
  336.3 10.3 convolution_convert_fusion
  347.4 6.4 fusion.100
  361.1 20.8 %reduce-scatter.31.cloned.1.call-done = bf16[512,4096]{1,0:T(8,128)(2,1)} async-done(((bf16[1024,4096]{1,0:T(8,128)(2,1)}), bf16[512,4096]{1,0:T(8,128)(2,1)}) %reduce-scatter.31.cloned.1.call-update) | async-done | bytes 4194320 | tf_op jit(solution)/shard_map/reduce_scatter | solution.py:193
  381.9 20.9 %reduce-scatter.33.cloned.1.call-done = bf16[512,4096]{1,0:T(8,128)(2,1)} async-done(((bf16[1024,4096]{1,0:T(8,128)(2,1)}), bf16[512,4096]{1,0:T(8,128)(2,1)}) %reduce-scatter.33.cloned.1.call-update) | async-done | bytes 4194320 | tf_op jit(solution)/shard_map/reduce_scatter | solution.py:196
  404.9 17.5 %fusion.50 = bf16[8,65]{1,0:T(8,128)(2,1)} fusion(s32[288,288]{0,1:T(8,128)} %copy-done.48, f32[8,288,288]{1,2,0:T(8,128)S(1)} %copy-done.3), kind=kOutput, calls=%fused_computation.135 | convolution fusion | flops 522962432 | bytes 2987024 | tf_op jit(solution)/shard_map/hqk,rqk->hr/dot_general | solution.py:172
  430.8 5.4 reduce-scatter.27.cloned.1.call-done
  436.2 11.2 reduce-scatter.35.cloned.1.call-done
  447.4 80.6 %all-reduce.20 = (bf16[4,65]{1,0:T(4,128)(2,1)S(1)}, bf16[512,5]{0,1:T(8,128)(2,1)S(1)}, bf16[512,6]{0,1:T(8,128)(2,1)S(1)}, bf16[512,3]{0,1:T(4,128)(2,1)S(1)}, bf16[512,3]{0,1:T(4,128)(2,1)S(1)}) all-reduce(bf16[4,65]{1,0:T(4,128)(2,1)S(1)} %constant_dynamic-slice_fusion, ...), channel_id=1, replica_groups=mesh['dp'=16,'fsdp'=2] {'dp'}, use_global_device_ids=true, to_apply=%region_42.43 | all-reduce | flops 8964 | bytes 35856 | tf_op jit(solution)/shard_map/psum | solution.py:235
  531.0 575.8 %all-reduce.24.cloned.1.call-done = (bf16[512,4096]{1,0:T(8,128)(2,1)}, bf16[512,4096]{1,0:T(8,128)(2,1)}, bf16[512,3072]{1,0:T(8,128)(2,1)}, bf16[512,1024]{1,0...) async-done(((bf16[512,4096]{1,0:T(8,128)(2,1)}, bf16[512,4096]{1,0:T(8,128)(2,1)}, ...) | async-done | bytes 24117264 | tf_op jit(solution)/shard_map/psum | solution.py:233
  1106.8 6.8 convert_element_type.312
  1113.6 4.5 convert_element_type.314
  1132.8 4.5 convert_element_type.330
  (452 shorter events, 140.9 us)
Async XLA Ops:
  7.2 33.1 %all-gather.10.cloned.1.call-start = ((), (), s32[]{:S(2)}) async-start(), calls=%async_computation.12 | async-start | bytes 12582912 | tf_op jit(solution)/shard_map/all_gather | solution.py:264
  7.9 46.9 %all-gather.12.cloned.1.call-start = ((), (), s32[]{:S(2)}) async-start(), calls=%async_computation.13 | async-start | bytes 12582912 | tf_op jit(solution)/shard_map/all_gather | solution.py:265
  8.7 65.7 %all-gather.14.cloned.1.call-start = ((), (), s32[]{:S(2)}) async-start(), calls=%async_computation.14 | async-start | bytes 9437184 | tf_op jit(solution)/shard_map/all_gather | solution.py:266
  9.4 78.2 %all-gather.16.cloned.1.call-start = ((), (), s32[]{:S(2)}) async-start(), calls=%async_computation.15 | async-start | bytes 3145728 | tf_op jit(solution)/shard_map/all_gather | solution.py:267
  10.0 93.8 %all-gather.18.cloned.1.call-start = ((), (), s32[]{:S(2)}) async-start(), calls=%async_computation.16 | async-start | bytes 6291456 | tf_op jit(solution)/shard_map/all_gather | solution.py:269
  10.6 145.8 %all-gather.20.cloned.1.call-start = ((), (), s32[]{:S(2)}) async-start(), calls=%async_computation.17 | async-start | bytes 3145728 | tf_op jit(solution)/shard_map/all_gather | solution.py:271
  11.1 151.8 %all-gather.22.cloned.1.call-start = ((), (), s32[]{:S(2)}) async-start(), calls=%async_computation.18 | async-start | bytes 12582912 | tf_op jit(solution)/shard_map/all_gather | solution.py:272
  11.9 159.7 %all-gather.24.cloned.1.call-start = ((), (), s32[]{:S(2)}) async-start(), calls=%async_computation.19 | async-start | bytes 12582912 | tf_op jit(solution)/shard_map/all_gather | solution.py:273
  12.7 346.4 %reduce-scatter.23.cloned.1.call-start = ((), (), s32[]{:S(2)}) async-start(), calls=%async_computation.23 | async-start | bytes 3145728 | tf_op jit(solution)/shard_map/reduce_scatter | solution.py:196
  12.8 24.9 %copy-start.48 = (s32[288,288]{0,1:T(8,128)}, s32[288,288]{0,1:T(8,128)S(1)}, u32[]{:S(2)}) copy-start(s32[288,288]{0,1:T(8,128)S(1)} %clamp_add_fusion) | copy-start | bytes 995332
  20.1 20.2 %copy-start.116 = (f32[1024,1]{0,1:T(1,128)}, f32[1024,1]{0,1:T(1,128)S(1)}, u32[]{:S(2)}) copy-start(f32[1024,1]{0,1:T(1,128)S(1)} %get-tuple-element.104) | copy-start | bytes 12292
  20.1 54.2 %copy-start.118 = (f32[1024,1]{0,1:T(1,128)}, f32[1024,1]{0,1:T(1,128)S(1)}, u32[]{:S(2)}) copy-start(f32[1024,1]{0,1:T(1,128)S(1)} %get-tuple-element.103) | copy-start | bytes 12292
  22.6 17.8 %copy-start.60 = (f32[1024,1]{0,1:T(1,128)}, f32[1024,1]{0,1:T(1,128)S(1)}, u32[]{:S(2)}) copy-start(f32[1024,1]{0,1:T(1,128)S(1)} %get-tuple-element.94) | copy-start | bytes 12292
  22.6 51.8 %copy-start.98 = (f32[1024,1]{0,1:T(1,128)}, f32[1024,1]{0,1:T(1,128)S(1)}, u32[]{:S(2)}) copy-start(f32[1024,1]{0,1:T(1,128)S(1)} %get-tuple-element.93) | copy-start | bytes 12292
  22.7 17.6 %copy-start.62 = (f32[288]{0:T(512)}, f32[288]{0:T(512)S(1)}, u32[]{:S(2)}) copy-start(f32[288]{0:T(512)S(1)} %broadcast_multiply_fusion.8) | copy-start | bytes 3460
  23.1 17.3 %copy-start.79 = (f32[288]{0:T(512)}, f32[288]{0:T(512)S(1)}, u32[]{:S(2)}) copy-start(f32[288]{0:T(512)S(1)} %fusion.82) | copy-start | bytes 3460
  62.4 16.9 %copy-start.4 = (f32[288,1024]{1,0:T(8,128)}, f32[288,1024]{1,0:T(8,128)S(1)}, u32[]{:S(2)}) copy-start(f32[288,1024]{1,0:T(8,128)S(1)} %get-tuple-element.118) | copy-start | bytes 3538948
  62.4 16.9 %copy-start.64 = (f32[288]{0:T(512)}, f32[288]{0:T(512)S(1)}, u32[]{:S(2)}) copy-start(f32[288]{0:T(512)S(1)} %broadcast_multiply_fusion.7) | copy-start | bytes 3460
  62.7 16.6 %copy-start.73 = (f32[288]{0:T(512)}, f32[288]{0:T(512)S(1)}, u32[]{:S(2)}) copy-start(f32[288]{0:T(512)S(1)} %multiply_reduce_fusion.20) | copy-start | bytes 3460
  261.0 98.1 %reduce-scatter.29.cloned.1.call-start = ((), (), s32[]{:S(2)}) async-start(), calls=%async_computation.26 | async-start | bytes 3145728 | tf_op jit(solution)/shard_map/reduce_scatter | solution.py:196
  265.5 93.6 %reduce-scatter.25.cloned.1.call-start = ((), (), s32[]{:S(2)}) async-start(), calls=%async_computation.24 | async-start | bytes 6291456 | tf_op jit(solution)/shard_map/reduce_scatter | solution.py:193
  272.4 86.7 %reduce-scatter.21.cloned.1.call-start = ((), (), s32[]{:S(2)}) async-start(), calls=%async_computation.22 | async-start | bytes 9437184 | tf_op jit(solution)/shard_map/reduce_scatter | solution.py:193
  287.9 71.3 %reduce-scatter.17.cloned.1.call-start = ((), (), s32[]{:S(2)}) async-start(), calls=%async_computation.20 | async-start | bytes 12582912 | tf_op jit(solution)/shard_map/reduce_scatter | solution.py:210
  295.2 18.7 %copy-start.27 = (f32[288,1024]{1,0:T(8,128)}, f32[288,1024]{1,0:T(8,128)S(1)}, u32[]{:S(2)}) copy-start(f32[288,1024]{1,0:T(8,128)S(1)} %add_add_fusion.5) | copy-start | bytes 3538948
  313.9 47.2 %reduce-scatter.19.cloned.1.call-start = ((), (), s32[]{:S(2)}) async-start(), calls=%async_computation.21 | async-start | bytes 12582912 | tf_op jit(solution)/shard_map/reduce_scatter | solution.py:213
  324.3 57.6 %reduce-scatter.31.cloned.1.call-start = ((), (), s32[]{:S(2)}) async-start(), calls=%async_computation.27 | async-start | bytes 12582912 | tf_op jit(solution)/shard_map/reduce_scatter | solution.py:193
  334.9 68.0 %reduce-scatter.33.cloned.1.call-start = ((), (), s32[]{:S(2)}) async-start(), calls=%async_computation.28 | async-start | bytes 12582912 | tf_op jit(solution)/shard_map/reduce_scatter | solution.py:196
  346.7 82.1 %reduce-scatter.37.cloned.1.call-start = ((), (), s32[]{:S(2)}) async-start(), calls=%async_computation.30 | async-start | bytes 393216
  355.0 74.8 %reduce-scatter.39.cloned.1.call-start = ((), (), s32[]{:S(2)}) async-start(), calls=%async_computation.31 | async-start | bytes 393216
  356.0 80.2 %reduce-scatter.27.cloned.1.call-start = ((), (), s32[]{:S(2)}) async-start(), calls=%async_computation.25 | async-start | bytes 24576 | tf_op jit(solution)/shard_map/reduce_scatter | solution.py:219
  356.8 90.7 %reduce-scatter.35.cloned.1.call-start = ((), (), s32[]{:S(2)}) async-start(), calls=%async_computation.29 | async-start | bytes 24576 | tf_op jit(solution)/shard_map/reduce_scatter | solution.py:222
  358.8 748.0 %all-reduce.24.cloned.1.call-start = ((), (), s32[]{:S(2)}) async-start(), calls=%async_computation.32 | async-start | bytes 48234496 | tf_op jit(solution)/shard_map/psum | solution.py:233
  (125 other events, 486.8 us)
Sparse Core Ops, SparseCore 0:
  9.6 22.5 all-gather.9
  33.7 21.0 all-gather.11
  56.3 17.9 all-gather.13
  75.8 11.7 all-gather.15
  88.9 14.8 all-gather.17
  105.2 11.7 all-gather.19
  118.5 21.0 all-gather.21
  141.1 21.0 all-gather.23
  261.1 9.7 reduce-scatter.22
  273.7 10.7 reduce-scatter.28
  287.4 13.2 reduce-scatter.24
  303.5 15.7 reduce-scatter.20
  322.2 17.9 reduce-scatter.16
  343.0 18.0 reduce-scatter.18
  363.8 18.0 reduce-scatter.30
  384.7 18.0 reduce-scatter.32
  404.9 8.9 reduce-scatter.36
  416.0 8.8 reduce-scatter.38
  427.7 8.5 reduce-scatter.26
  438.8 8.5 reduce-scatter.34
  453.9 652.8 all-reduce.23
where the time goes:
time: 1150 us; the launch traced here: 1140 us
  waiting for transfers between devices  670 us (58%)
  matrix products  176 us (15%)
  blocking collectives  175 us (15%)
  other arithmetic  67.5 us (6%)
  local copies, waits for them, and re-layouts  34.6 us (3%)
  between operations  18.9 us (2%)
    psum x1, waiting for transfers between devices, reduce_rest(): lax.psum(parts[0].astype(jnp.bfloat16), 'dp').astype(jnp.float32)  576 us
    psum x1, blocking collectives, reduce_rest(): lax.psum(parts[2].astype(jnp.bfloat16), 'dp').astype(jnp.float32)  80.6 us
    dot_general x8, matrix products, weight_grad(): lax.dot_general(left, right, DOWN_DIMS, preferred_element_type=jnp.float32)  56.6 us
    dot_general x8, matrix products, project(): return jnp.dot(left, right, preferred_element_type=jnp.float32)  48.8 us
    psum x1, blocking collectives, per_device(): lax.psum((jnp.sum(weighted, axis=0), jnp.sum(weighted * mixed_rows, axis=...  41.4 us
    psum x1, blocking collectives, per_device(): lax.psum((jnp.sum(grad_hat, axis=0), jnp.sum(grad_hat * bn_hat, axis=0)),...  41.1 us
    dot_general x8, matrix products, project_back(): lax.dot_general(left, right, ACROSS_DIMS, preferred_element_type=jnp.floa...  40.4 us
    unnamed x279, local copies, waits for them, and re-layouts  29.2 us
  transfers between devices with their start and end apart: 21, of which 10 were waited for; matrix products, arithmetic and copies ran while one was open for 16% of the time, Pallas kernels for 0%

commit v1 on v0

v1 whole, which is shorter than its diff:
```python
import functools

import jax
import jax.numpy as jnp
from jax import lax
from jax.experimental import pallas as pl
from jax.experimental.pallas import tpu as pltpu
from jax.sharding import PartitionSpec as P

EPSILON = 1e-05
MASKED = -1000000000.0
DOWN_DIMS = (((0,), (0,)), ((), ()))
ACROSS_DIMS = (((1,), (1,)), ((), ()))


def rows_norm(values, gain_col, bias_col):
    centre = values - jnp.mean(values, axis=-1, keepdims=True)
    spread = jnp.mean(centre * centre, axis=-1, keepdims=True)
    return centre * lax.rsqrt(spread + EPSILON) * gain_col + bias_col


def frame_masks(length_row, frames):
    end_one = length_row[0]
    end_two = end_one + length_row[1]
    end_three = end_two + length_row[2]
    places = jnp.arange(frames, dtype=jnp.int32)
    segment = (
        (places >= end_one).astype(jnp.int32)
        + (places >= end_two).astype(jnp.int32)
        + (places >= end_three).astype(jnp.int32)
    )
    valid_rows = (places < end_three).astype(jnp.float32)
    return (segment, valid_rows)


def shifted_rows(values, segment, offset):
    frames = values.shape[0]
    if offset > 0:
        moved_rows = jnp.concatenate(
            [values[offset:], jnp.zeros((offset, values.shape[1]), values.dtype)], axis=0
        )
        moved_seg = jnp.concatenate([segment[offset:], jnp.full((offset,), -1, jnp.int32)])
    elif offset < 0:
        moved_rows = jnp.concatenate(
            [jnp.zeros((-offset, values.shape[1]), values.dtype), values[: frames + offset]], axis=0
        )
        moved_seg = jnp.concatenate(
            [jnp.full((-offset,), -1, jnp.int32), segment[: frames + offset]]
        )
    else:
        moved_rows, moved_seg = (values, segment)
    return (moved_rows, moved_seg)


def depthwise(gated_rows, kernel, segment):
    tap_count = kernel.shape[1]
    running = jnp.zeros_like(gated_rows)
    for tap_index in range(tap_count):
        moved_rows, moved_seg = shifted_rows(gated_rows, segment, tap_index - tap_count // 2)
        keep_rows = (moved_seg == segment).astype(jnp.float32)
        running = running + kernel[:, tap_index][None, :] * moved_rows * keep_rows[:, None]
    return running


def glu_conv(front_rows, kernel, segment):
    half_width = kernel.shape[0]
    gated_rows = front_rows[:, :half_width] * jax.nn.sigmoid(front_rows[:, half_width:])
    return depthwise(gated_rows, kernel, segment)


def project(left, right):
    return jnp.dot(left, right, preferred_element_type=jnp.float32)


def project_back(left, right):
    return lax.dot_general(left, right, ACROSS_DIMS, preferred_element_type=jnp.float32)


def weight_grad(left, right):
    return lax.dot_general(left, right, DOWN_DIMS, preferred_element_type=jnp.float32)


def norm_back(grad_out, values, gain_col, bias_col):
    _, pull_back = jax.vjp(rows_norm, values, gain_col, bias_col)
    return pull_back(grad_out)


def silu_back(grad_out, before):
    _, pull_back = jax.vjp(jax.nn.silu, before)
    return pull_back(grad_out)[0]


def pair_kernel(axes, x_ref, o_ref, slots, send_sems, recv_sems):
    partners = []
    for name, size in axes:
        me = lax.axis_index(name)
        bit = 1
        while bit < size:
            partners.append({name: me + bit * (1 - 2 * ((me // bit) % 2))})
            bit *= 2
    barrier = pltpu.get_barrier_semaphore()
    for partner in partners:
        pl.semaphore_signal(barrier, inc=1, device_id=partner, device_id_type=pl.DeviceIdType.MESH)
    pl.semaphore_wait(barrier, len(partners))
    o_ref[...] = x_ref[...]
    for stage, partner in enumerate(partners):
        copy = pltpu.make_async_remote_copy(
            src_ref=o_ref,
            dst_ref=slots.at[stage],
            send_sem=send_sems.at[stage],
            recv_sem=recv_sems.at[stage],
            device_id=partner,
            device_id_type=pl.DeviceIdType.MESH,
        )
        copy.start()
        copy.wait()
        o_ref[...] += slots[stage]


def sum_everywhere(values, axes, collective_id):
    stages = sum(size.bit_length() - 1 for _, size in axes)
    if any(size & (size - 1) for _, size in axes):
        return lax.psum(values, tuple(name for name, _ in axes))
    return pl.pallas_call(
        functools.partial(pair_kernel, axes),
        out_shape=jax.ShapeDtypeStruct(values.shape, values.dtype),
        in_specs=[pl.BlockSpec(memory_space=pltpu.VMEM)],
        out_specs=pl.BlockSpec(memory_space=pltpu.VMEM),
        scratch_shapes=[
            pltpu.VMEM((stages,) + values.shape, values.dtype),
            pltpu.SemaphoreType.DMA((stages,)),
            pltpu.SemaphoreType.DMA((stages,)),
        ],
        compiler_params=pltpu.CompilerParams(collective_id=collective_id, has_side_effects=True),
    )(values)


class Rows:
    def __init__(self, size):
        self.size = size
        self.me = lax.axis_index("fsdp")

    def owner(self, step):
        return lax.rem(self.me + step, self.size)

    def shift(self, values, step):
        return lax.ppermute(
            values, "fsdp", [(j, (j - step) % self.size) for j in range(self.size)]
        )

    def gather(self, block):
        return [(self.me, block)] + [
            (self.owner(step), self.shift(block, step)) for step in range(1, self.size)
        ]

    def columns(self, values, owner):
        width = values.shape[1] // self.size
        return lax.dynamic_slice_in_dim(values, owner * width, width, axis=1)

    def order(self, parts, axis):
        if self.size == 1:
            return parts[0]
        if self.size == 2:
            first = self.me == 0
            return jnp.concatenate(
                [jnp.where(first, parts[0], parts[1]), jnp.where(first, parts[1], parts[0])],
                axis=axis,
            )
        width = parts[0].shape[axis]
        twice = jnp.concatenate(parts + parts, axis=axis)
        start = lax.rem(self.size - self.me, self.size) * width
        return lax.dynamic_slice_in_dim(twice, start, width * self.size, axis=axis)

    def times(self, values, blocks):
        return functools.reduce(
            jnp.add, [project(self.columns(values, owner), block) for owner, block in blocks]
        )

    def times_back(self, values, blocks):
        return self.order([project_back(values, block) for _, block in blocks], 1)

    def all_frames(self, values):
        return jnp.concatenate(
            [values] + [self.shift(values, step) for step in range(1, self.size)], axis=0
        )

    def all_frames_own_columns(self, values):
        return jnp.concatenate(
            [self.columns(values, self.me)]
            + [
                self.shift(self.columns(values, self.owner(self.size - step)), step)
                for step in range(1, self.size)
            ],
            axis=0,
        )


def cube_kernel(plan, *refs):
    me = lax.axis_index("dp")
    arrays = [len(columns) for _, columns, _ in plan]
    inputs, refs = refs[: sum(arrays)], refs[sum(arrays) :]
    outputs, refs = refs[: sum(arrays)], refs[sum(arrays) :]
    kinds, all_bits, first = [], [], 0
    for bits, columns, chunk in plan:
        whole, result, refs = refs[0], refs[1], refs[2:]
        sums, refs = refs[: len(bits)], refs[len(bits) :]
        send_sems, recv_sems, refs = refs[0], refs[1], refs[2:]
        rows = whole.shape[0]
        uppers = [lax.rem(me // bit, 2) for bit in bits]
        partners = [me + bit * (1 - 2 * upper) for bit, upper in zip(bits, uppers)]
        starts, start = [], 0
        for step, upper in enumerate(uppers):
            start = start + upper * (rows >> (step + 1))
            starts.append(start)
        kinds.append(
            dict(
                bits=bits,
                columns=columns,
                chunk=chunk,
                count=sum(columns) // chunk,
                whole=whole,
                result=result,
                sums=sums,
                send=send_sems,
                recv=recv_sems,
                rows=rows,
                uppers=uppers,
                partners=partners,
                starts=starts,
                first=first,
            )
        )
        first += len(columns)
        all_bits += [bit for bit in bits if bit not in all_bits]
    io_sems = refs[0]

    def loads(kind):
        offset = 0
        for place, columns in enumerate(kind["columns"]):
            index = kind["first"] + place
            yield pltpu.make_async_copy(
                inputs[index],
                kind["whole"].at[:, pl.ds(offset, columns)],
                io_sems.at[index],
            )
            offset += columns

    def stores(kind):
        offset = 0
        for place, columns in enumerate(kind["columns"]):
            index = kind["first"] + place
            yield pltpu.make_async_copy(
                kind["result"].at[:, pl.ds(offset, columns)],
                outputs[index],
                io_sems.at[index],
            )
            offset += columns

    for kind in kinds:
        for copy in loads(kind):
            copy.start()
    barrier = pltpu.get_barrier_semaphore()
    for bit in all_bits:
        partner = me + bit * (1 - 2 * lax.rem(me // bit, 2))
        pl.semaphore_signal(
            barrier, inc=1, device_id={"dp": partner}, device_id_type=pl.DeviceIdType.MESH
        )
    pl.semaphore_wait(barrier, len(all_bits))
    for kind in kinds:
        for copy in loads(kind):
            copy.wait()

    def window(kind, index):
        return pl.ds(pl.multiple_of(index * kind["chunk"], kind["chunk"]), kind["chunk"])

    def halving(kind, step, index):
        rows = kind["rows"] >> (step + 1)
        source = kind["whole"] if step == 0 else kind["sums"][step - 1]
        given = pl.multiple_of((1 - kind["uppers"][step]) * rows, rows)
        return pltpu.make_async_remote_copy(
            src_ref=source.at[pl.ds(given, rows), window(kind, index)],
            dst_ref=kind["sums"][step].at[:, window(kind, index)],
            send_sem=kind["send"].at[step, index],
            recv_sem=kind["recv"].at[step, index],
            device_id={"dp": kind["partners"][step]},
            device_id_type=pl.DeviceIdType.MESH,
        )

    def doubling(kind, step, index):
        rows = kind["rows"] >> (step + 1)
        start = pl.multiple_of(kind["starts"][step], rows)
        block = kind["result"].at[pl.ds(start, rows), window(kind, index)]
        slot = 2 * len(kind["bits"]) - 1 - step
        return pltpu.make_async_remote_copy(
            src_ref=block,
            dst_ref=block,
            send_sem=kind["send"].at[slot, index],
            recv_sem=kind["recv"].at[slot, index],
            device_id={"dp": kind["partners"][step]},
            device_id_type=pl.DeviceIdType.MESH,
        )

    def advance(kind, stage, index):
        depth = len(kind["bits"])
        if stage == 0:
            halving(kind, 0, index).start()
        elif stage <= depth:
            step = stage - 1
            halving(kind, step, index).wait()
            rows = kind["rows"] >> (step + 1)
            source = kind["whole"] if step == 0 else kind["sums"][step - 1]
            kept = pl.multiple_of(kind["uppers"][step] * rows, rows)
            columns = window(kind, index)
            total = (
                source[pl.ds(kept, rows), columns].astype(jnp.float32)
                + kind["sums"][step][:, columns].astype(jnp.float32)
            ).astype(kind["whole"].dtype)
            if stage < depth:
                kind["sums"][step][:, columns] = total
                halving(kind, stage, index).start()
            else:
                start = pl.multiple_of(kind["starts"][step], rows)
                kind["result"][pl.ds(start, rows), columns] = total
                doubling(kind, step, index).start()
        else:
            step = 2 * depth - stage
            doubling(kind, step, index).wait()
            if step > 0:
                doubling(kind, step - 1, index).start()

    last = max(kind["count"] + 2 * len(kind["bits"]) for kind in kinds)

    @pl.loop(0, last)
    def _(tick):
        for stage in range(2 * max(len(kind["bits"]) for kind in kinds) + 1):
            for kind in kinds:
                if stage <= 2 * len(kind["bits"]):

                    @pl.when((tick >= stage) & (tick < stage + kind["count"]))
                    def _(kind=kind, stage=stage):
                        advance(kind, stage, tick - stage)

    for kind in kinds:
        for copy in stores(kind):
            copy.start()
    for kind in kinds:
        for copy in stores(kind):
            copy.wait()


def sum_cube(parts, plan, collective_id):
    flat = [part for kind in parts for part in kind]
    scratch = []
    for kind, (bits, columns, chunk) in zip(parts, plan):
        rows, total = kind[0].shape[0], sum(columns)
        scratch += [pltpu.VMEM((rows, total), kind[0].dtype)] * 2
        scratch += [
            pltpu.VMEM((rows >> (step + 1), total), kind[0].dtype) for step in range(len(bits))
        ]
        scratch += [pltpu.SemaphoreType.DMA((2 * len(bits), total // chunk))] * 2
    scratch.append(pltpu.SemaphoreType.DMA((len(flat),)))
    out = pl.pallas_call(
        functools.partial(cube_kernel, plan),
        out_shape=[jax.ShapeDtypeStruct(part.shape, part.dtype) for part in flat],
        in_specs=[pl.BlockSpec(memory_space=pl.ANY)] * len(flat),
        out_specs=[pl.BlockSpec(memory_space=pl.ANY)] * len(flat),
        scratch_shapes=scratch,
        compiler_params=pltpu.CompilerParams(
            collective_id=collective_id, has_side_effects=True, vmem_limit_bytes=60 * 2**20
        ),
    )(*flat)
    result = []
    for kind in parts:
        result.append(out[: len(kind)])
        out = out[len(kind) :]
    return result


class Groups:
    def __init__(self, size):
        self.size = size
        self.me = lax.axis_index("dp")
        bits = [1 << k for k in range(size.bit_length() - 1)]
        self.plain = size & (size - 1) != 0 or not bits
        self.orders = [
            [bits[k]] + bits[:k] + bits[k + 1 :] for k in (0, min(1, len(bits) - 1), min(2, len(bits) - 1))
        ] if bits else []

    def swap(self, values, bit):
        return lax.ppermute(values, "dp", [(j, j ^ bit) for j in range(self.size)])

    def upper(self, bit):
        return lax.rem(self.me // bit, 2)

    def give(self, kind, pieces):
        if self.plain:
            return None
        bit = self.orders[kind][0]
        return self.product(pieces, 1 - self.upper(bit), 2).astype(jnp.bfloat16)

    def product(self, pieces, part, parts):
        count = pieces[0][0].shape[1] // parts
        products = [
            weight_grad(lax.dynamic_slice_in_dim(left, part * count, count, axis=1), right)
            for left, right in pieces
        ]
        return products[0] if len(products) == 1 else jnp.concatenate(products, axis=1)

    def keep(self, kind, pieces, given):
        if self.plain:
            return self.product(pieces, 0, 1).astype(jnp.bfloat16)
        bit = self.orders[kind][0]
        other = self.swap(given, bit)
        mine = self.product(pieces, self.upper(bit), 2)
        return (mine + other.astype(jnp.float32)).astype(jnp.bfloat16)

    def middle(self, parts, collective_id):
        if self.plain:
            return parts
        plan, fits = [], True
        for order, arrays in zip(self.orders, parts):
            columns = tuple(array.shape[1] for array in arrays)
            blocks = sum(columns) // 128
            chunk = 128 * max([k for k in range(1, blocks + 1) if blocks % k == 0 and blocks // k >= 16], default=1)
            plan.append((tuple(order[1:]), columns, chunk))
            fits &= all(count % 128 == 0 for count in columns) and blocks > 0
            fits &= (arrays[0].shape[0] >> len(order[1:])) % 16 == 0 and len(order) > 1
        if fits:
            return sum_cube(parts, plan, collective_id)
        return [
            [self.rounds(order[1:], array) for array in arrays]
            for order, arrays in zip(self.orders, parts)
        ]

    def rounds(self, bits, total):
        for bit in bits:
            count = total.shape[0] // 2
            given = lax.dynamic_slice_in_dim(total, (1 - self.upper(bit)) * count, count, axis=0)
            mine = lax.dynamic_slice_in_dim(total, self.upper(bit) * count, count, axis=0)
            other = self.swap(given, bit)
            total = (mine.astype(jnp.float32) + other.astype(jnp.float32)).astype(jnp.bfloat16)
        for bit in reversed(bits):
            total = self.double(bit, total)
        return total

    def double(self, bit, total):
        other = self.swap(total, bit)
        low = self.upper(bit) == 0
        return jnp.concatenate(
            [jnp.where(low, total, other), jnp.where(low, other, total)], axis=0
        )

    def gather(self, kind, total):
        if self.plain:
            return lax.psum(total, "dp").astype(jnp.float32)
        return self.double(self.orders[kind][0], total).astype(jnp.float32)


def attn_scores(queries, key_rows, rel_bias, onehot, same_seg, score_scale):
    product = (
        jnp.einsum("qhe,khe->hqk", queries, key_rows, preferred_element_type=jnp.float32)
        * score_scale
    )
    relative = jnp.einsum("hr,rqk->hqk", rel_bias, onehot, precision=lax.Precision.HIGHEST)
    return jnp.where(same_seg[None], product + relative, MASKED)


def attn_core(packed, rel_bias, onehot, same_seg):
    frames = packed.shape[0]
    head_count = rel_bias.shape[0]
    head_size = packed.shape[1] // 3 // head_count
    score_scale = head_size ** (-0.5)
    packed = packed.reshape(frames, 3, head_count, head_size)
    queries = packed[:, 0]
    key_rows = packed[:, 1]
    value_rows = packed[:, 2]
    scores = attn_scores(queries, key_rows, rel_bias, onehot, same_seg, score_scale)
    top_score = jnp.max(scores, axis=-1, keepdims=True)
    log_total = top_score + jnp.log(jnp.sum(jnp.exp(scores - top_score), axis=-1, keepdims=True))
    attend = jnp.exp(scores - log_total).astype(jnp.bfloat16)
    context = jnp.einsum("hqk,khe->qhe", attend, value_rows, preferred_element_type=jnp.float32)
    context = context.astype(jnp.bfloat16).reshape(frames, head_count * head_size)
    return context, (queries, key_rows, value_rows, log_total)


def attn_core_back(grad_context, rel_bias, onehot, same_seg, kept):
    queries, key_rows, value_rows, log_total = kept
    frames, head_count, head_size = queries.shape
    score_scale = head_size ** (-0.5)
    grad_context = grad_context.reshape(frames, head_count, head_size)
    scores = attn_scores(queries, key_rows, rel_bias, onehot, same_seg, score_scale)
    attend = jnp.exp(scores - log_total)
    grad_attend = jnp.einsum(
        "qhe,khe->hqk", grad_context, value_rows, preferred_element_type=jnp.float32
    )
    grad_value = jnp.einsum(
        "hqk,qhe->khe",
        attend.astype(jnp.bfloat16),
        grad_context,
        preferred_element_type=jnp.float32,
    )
    grad_scores = attend * (grad_attend - jnp.sum(grad_attend * attend, axis=-1, keepdims=True))
    grad_rel = jnp.einsum("hqk,rqk->hr", grad_scores, onehot, precision=lax.Precision.HIGHEST)
    scores_low = grad_scores.astype(jnp.bfloat16)
    grad_query = (
        jnp.einsum("hqk,khe->qhe", scores_low, key_rows, preferred_element_type=jnp.float32)
        * score_scale
    )
    grad_key = (
        jnp.einsum("hqk,qhe->khe", scores_low, queries, preferred_element_type=jnp.float32)
        * score_scale
    )
    grad_packed = jnp.stack([grad_query, grad_key, grad_value], axis=1)
    grad_packed = grad_packed.reshape(frames, 3 * head_count * head_size).astype(jnp.bfloat16)
    return grad_packed, grad_rel


def per_device(
    sizes,
    inputs,
    cotangent,
    lengths,
    ffn1_in,
    ffn1_out,
    attn_qkv,
    attn_out,
    rel_table,
    conv_in,
    depth_kernel,
    conv_out,
    ffn2_in,
    ffn2_out,
    gains,
    biases,
    inner_biases,
):
    dp_size, fsdp_size = sizes
    axes = (("fsdp", fsdp_size), ("dp", dp_size))
    rows = Rows(fsdp_size)
    groups = Groups(dp_size)
    frames, width = inputs.shape
    taps = depth_kernel.shape[1]
    segment, valid_rows = frame_masks(lengths[0], frames)
    valid_col = valid_rows[:, None]

    small = jnp.concatenate([gains, biases, inner_biases, depth_kernel], axis=1).T
    small = rows.order([block for _, block in rows.gather(small)], 1).astype(jnp.float32)
    rel_bias = rows.order([block for _, block in rows.gather(rel_table)], 0).astype(jnp.float32)
    w_ffn1_in = rows.gather(ffn1_in)
    w_ffn1_out = rows.gather(ffn1_out)
    w_qkv = rows.gather(attn_qkv)
    w_attn_out = rows.gather(attn_out)
    w_conv_in = rows.gather(conv_in)
    w_conv_out = rows.gather(conv_out)
    w_ffn2_in = rows.gather(ffn2_in)
    w_ffn2_out = rows.gather(ffn2_out)
    gain = [small[k] for k in range(6)]
    bias = [small[k] for k in (6, 7, 9, 10, 8, 11)]
    kernel = small[12 : 12 + taps].T

    places = jnp.arange(frames, dtype=jnp.int32)
    reach = (rel_bias.shape[1] - 1) // 2
    rel_index = jnp.clip(places[None, :] - places[:, None], -reach, reach) + reach
    onehot = (
        rel_index[None] == jnp.arange(rel_bias.shape[1], dtype=jnp.int32)[:, None, None]
    ).astype(jnp.float32)
    same_seg = segment[:, None] == segment[None, :]

    stream_in = inputs.astype(jnp.float32)
    normed_one = rows_norm(stream_in, gain[0], bias[0]).astype(jnp.bfloat16)
    before_one = rows.times(normed_one, w_ffn1_in)
    hidden_one = jax.nn.silu(before_one).astype(jnp.bfloat16)
    after_ffn = stream_in + 0.5 * rows.times_back(hidden_one, w_ffn1_out)

    normed_attn = rows_norm(after_ffn, gain[1], bias[1]).astype(jnp.bfloat16)
    packed = rows.times(normed_attn, w_qkv).astype(jnp.bfloat16)
    context, kept_attn = attn_core(packed, rel_bias, onehot, same_seg)
    after_attn = after_ffn + rows.times(context, w_attn_out)

    normed_conv = rows_norm(after_attn, gain[2], bias[2]).astype(jnp.bfloat16)
    front_rows = rows.times(normed_conv, w_conv_in)
    mixed_rows = glu_conv(front_rows, kernel, segment)
    weighted = valid_col * mixed_rows
    totals = sum_everywhere(
        jnp.stack(
            [
                jnp.sum(weighted, axis=0),
                jnp.sum(weighted * mixed_rows, axis=0),
                jnp.full((width,), jnp.sum(valid_rows)),
            ]
            + [jnp.zeros((width,), jnp.float32)] * 5
        ),
        axes,
        0,
    )
    valid_count = totals[2]
    bn_mean = totals[0] / valid_count
    bn_var = totals[1] / valid_count - bn_mean * bn_mean
    bn_rstd = lax.rsqrt(bn_var + EPSILON)
    bn_hat = (mixed_rows - bn_mean) * bn_rstd
    bn_out = bn_hat * gain[5] + bias[5]
    swish_low = jax.nn.silu(bn_out).astype(jnp.bfloat16)
    after_conv = after_attn + rows.times(swish_low, w_conv_out)

    normed_two = rows_norm(after_conv, gain[3], bias[3]).astype(jnp.bfloat16)
    before_two = rows.times(normed_two, w_ffn2_in)
    hidden_two = jax.nn.silu(before_two).astype(jnp.bfloat16)
    after_ffn2 = after_conv + 0.5 * rows.times_back(hidden_two, w_ffn2_out)
    layer_out = (valid_col * rows_norm(after_ffn2, gain[4], bias[4])).astype(jnp.bfloat16)

    grad_final = valid_col * cotangent.astype(jnp.float32)
    grad_after_ffn2, grad_gain_final, grad_bias_final = norm_back(
        grad_final, after_ffn2, gain[4], bias[4]
    )
    low_two = (0.5 * grad_after_ffn2).astype(jnp.bfloat16)
    left_out = rows.all_frames_own_columns(low_two)
    right_out = rows.all_frames(hidden_two)
    main = right_out.shape[1] * 3 // 4
    two_a = [(left_out, right_out[:, :main])]
    give_two_a = groups.give(0, two_a)
    grad_before = silu_back(rows.times(low_two, w_ffn2_out), before_two).astype(jnp.bfloat16)
    left_in = rows.all_frames_own_columns(normed_two)
    right_in = rows.all_frames(grad_before)
    two_b = [(left_in, right_in[:, :main])]
    give_two_b = groups.give(1, two_b)
    two_c = [(left_out, right_out[:, main:]), (left_in, right_in[:, main:])]
    give_two_c = groups.give(2, two_c)
    branch_grad, grad_gain_two, grad_bias_two = norm_back(
        rows.times_back(grad_before, w_ffn2_in), after_conv, gain[3], bias[3]
    )
    grad_after_conv = grad_after_ffn2 + branch_grad
    grad_after_conv, give_two_a, give_two_b, give_two_c = lax.optimization_barrier(
        (grad_after_conv, give_two_a, give_two_b, give_two_c)
    )

    conv_low = grad_after_conv.astype(jnp.bfloat16)
    conv_c = [(rows.all_frames_own_columns(swish_low), rows.all_frames(conv_low))]
    give_conv_c = groups.give(2, conv_c)
    grad_bn_out = silu_back(rows.times_back(conv_low, w_conv_out), bn_out)
    grad_gain_bn = jnp.sum(grad_bn_out * bn_hat, axis=0)
    grad_bias_bn = jnp.sum(grad_bn_out, axis=0)
    grad_hat = grad_bn_out * gain[5]
    back_sums = sum_everywhere(
        jnp.stack(
            [jnp.sum(grad_hat, axis=0), jnp.sum(grad_hat * bn_hat, axis=0)]
            + [jnp.zeros((width,), jnp.float32)] * 6
        ),
        axes,
        1,
    )
    grad_var = -0.5 * bn_rstd * bn_rstd * back_sums[1]
    grad_mean = -bn_rstd * back_sums[0] - 2.0 * bn_mean * grad_var
    grad_mixed = (
        grad_hat * bn_rstd + valid_col * (grad_mean + 2.0 * mixed_rows * grad_var) / valid_count
    )

    def conv_local(front_in, kernel_in):
        return glu_conv(front_in, kernel_in, segment)

    _, pull_back = jax.vjp(conv_local, front_rows, kernel)
    grad_front, grad_kernel = pull_back(grad_mixed)
    front_low = grad_front.astype(jnp.bfloat16)
    left_conv = rows.all_frames_own_columns(normed_conv)
    right_conv = rows.all_frames(front_low)
    conv_a = [(left_conv, right_conv[:, :width])]
    give_conv_a = groups.give(0, conv_a)
    conv_b = [(left_conv, right_conv[:, width:])]
    give_conv_b = groups.give(1, conv_b)
    branch_grad, grad_gain_conv, grad_bias_conv = norm_back(
        rows.times_back(front_low, w_conv_in), after_attn, gain[2], bias[2]
    )
    grad_after_attn = grad_after_conv + branch_grad
    grad_after_attn, give_conv_a, give_conv_b, give_conv_c = lax.optimization_barrier(
        (grad_after_attn, give_conv_a, give_conv_b, give_conv_c)
    )

    attn_low = grad_after_attn.astype(jnp.bfloat16)
    attn_c = [(rows.all_frames_own_columns(context), rows.all_frames(attn_low))]
    give_attn_c = groups.give(2, attn_c)
    grad_context = rows.times_back(attn_low, w_attn_out).astype(jnp.bfloat16)
    grad_packed, grad_rel = attn_core_back(grad_context, rel_bias, onehot, same_seg, kept_attn)
    left_qkv = rows.all_frames_own_columns(normed_attn)
    right_qkv = rows.all_frames(grad_packed)
    half = right_qkv.shape[1] // 2
    attn_a = [(left_qkv, right_qkv[:, :half])]
    give_attn_a = groups.give(0, attn_a)
    attn_b = [(left_qkv, right_qkv[:, half:])]
    give_attn_b = groups.give(1, attn_b)
    branch_grad, grad_gain_attn, grad_bias_attn = norm_back(
        rows.times_back(grad_packed, w_qkv), after_ffn, gain[1], bias[1]
    )
    grad_after_ffn = grad_after_attn + branch_grad
    grad_after_ffn, give_attn_a, give_attn_b, give_attn_c = lax.optimization_barrier(
        (grad_after_ffn, give_attn_a, give_attn_b, give_attn_c)
    )

    low_one = (0.5 * grad_after_ffn).astype(jnp.bfloat16)
    left_out = rows.all_frames_own_columns(low_one)
    right_out = rows.all_frames(hidden_one)
    one_a = [(left_out, right_out[:, :main])]
    give_one_a = groups.give(0, one_a)
    grad_before = silu_back(rows.times(low_one, w_ffn1_out), before_one).astype(jnp.bfloat16)
    left_in = rows.all_frames_own_columns(normed_one)
    right_in = rows.all_frames(grad_before)
    one_b = [(left_in, right_in[:, :main])]
    give_one_b = groups.give(1, one_b)
    one_c = [(left_out, right_out[:, main:]), (left_in, right_in[:, main:])]
    give_one_c = groups.give(2, one_c)
    branch_grad, grad_gain_one, grad_bias_one = norm_back(
        rows.times_back(grad_before, w_ffn1_in), stream_in, gain[0], bias[0]
    )
    input_grad = (grad_after_ffn + branch_grad).astype(jnp.bfloat16)

    lines = [
        grad_gain_one,
        grad_gain_attn,
        grad_gain_conv,
        grad_gain_two,
        grad_gain_final,
        grad_gain_bn,
        grad_bias_one,
        grad_bias_attn,
        grad_bias_final,
        grad_bias_conv,
        grad_bias_two,
        grad_bias_bn,
    ] + [grad_kernel[:, k] for k in range(taps)]
    flat_rel = grad_rel.reshape(-1)
    rel_lines = -(-flat_rel.shape[0] // width)
    flat_rel = jnp.pad(flat_rel, (0, rel_lines * width - flat_rel.shape[0]))
    count = len(lines) + rel_lines
    sums = jnp.concatenate(
        [jnp.stack(lines), flat_rel.reshape(rel_lines, width)]
        + ([jnp.zeros((-count % 8, width), jnp.float32)] if count % 8 else [])
    )
    sums = sum_everywhere(sums, axes, 2)
    own = lax.dynamic_slice_in_dim(
        sums[: len(lines)], rows.me * gains.shape[0], gains.shape[0], axis=1
    )
    rel_sum = sums[len(lines) : count].reshape(-1)[: grad_rel.size].reshape(grad_rel.shape)
    rel_sum = lax.dynamic_slice_in_dim(
        rel_sum, rows.me * rel_table.shape[0], rel_table.shape[0], axis=0
    )

    middle = groups.middle(
        [
            [
                groups.keep(0, two_a, give_two_a),
                groups.keep(0, conv_a, give_conv_a),
                groups.keep(0, attn_a, give_attn_a),
                groups.keep(0, one_a, give_one_a),
            ],
            [
                groups.keep(1, two_b, give_two_b),
                groups.keep(1, conv_b, give_conv_b),
                groups.keep(1, attn_b, give_attn_b),
                groups.keep(1, one_b, give_one_b),
            ],
            [
                groups.keep(2, two_c, give_two_c),
                groups.keep(2, conv_c, give_conv_c),
                groups.keep(2, attn_c, give_attn_c),
                groups.keep(2, one_c, give_one_c),
            ],
        ],
        3,
    )
    (two_a, conv_a, attn_a, one_a), (two_b, conv_b, attn_b, one_b), (two_c, conv_c, attn_c, one_c) = [
        [groups.gather(kind, array) for array in arrays] for kind, arrays in enumerate(middle)
    ]
    rest = two_c.shape[1] // 2
    sum_ffn2_out = jnp.concatenate([two_a, two_c[:, :rest]], axis=1)
    sum_ffn2_in = jnp.concatenate([two_b, two_c[:, rest:]], axis=1)
    sum_conv_in = jnp.concatenate([conv_a, conv_b], axis=1)
    sum_conv_out = conv_c
    sum_qkv = jnp.concatenate([attn_a, attn_b], axis=1)
    sum_attn_out = attn_c
    sum_ffn1_out = jnp.concatenate([one_a, one_c[:, :rest]], axis=1)
    sum_ffn1_in = jnp.concatenate([one_b, one_c[:, rest:]], axis=1)
    return (
        layer_out,
        input_grad,
        sum_ffn1_in,
        sum_ffn1_out,
        sum_qkv,
        sum_attn_out,
        rel_sum,
        sum_conv_in,
        own[12 : 12 + taps].T,
        sum_conv_out,
        sum_ffn2_in,
        sum_ffn2_out,
        own[0:6].T,
        own[6:9].T,
        own[9:12].T,
    )


def solution(mesh):
    frame_spec = P(("dp", "fsdp"), None)
    row_spec = P("fsdp", None)
    sizes = (mesh.shape["dp"], mesh.shape["fsdp"])
    return jax.shard_map(
        functools.partial(per_device, sizes),
        mesh=mesh,
        in_specs=(frame_spec,) * 3 + (row_spec,) * 13,
        out_specs=(frame_spec,) * 2 + (row_spec,) * 13,
        check_vma=False,
    )
```

time: 1150 us -> 788 us (0.69)
  waiting for transfers between devices: 670 us -> 79.8 us
  Pallas kernels: 0 us -> 243 us
  blocking collectives: 175 us -> 0 us
  local copies, waits for them, and re-layouts: 34.6 us -> 95.2 us
  other arithmetic: 67.5 us -> 122 us
  starting transfers between devices: 1.84 us -> 34.3 us
  matrix products: 176 us -> 196 us
  between operations: 18.9 us -> 6.04 us
    psum x1 -> x0, waiting for transfers between devices: 576 us -> none  [reduce_rest(): lax.psum(parts[0].astype(jnp.bfloat16), 'dp').astype(jnp.float32)]
    pallas_call x0 -> x4, Pallas kernels: none -> 243 us  [the longest x1 185 us: sum_cube(): pl.pallas_call(functools.partial(cube_kernel, plan), out_shape=[jax.Shape...]
    psum x3 -> x0, blocking collectives: 163 us -> none  [the longest x1 80.6 us: reduce_rest(): lax.psum(parts[2].astype(jnp.bfloat16), 'dp').astype(jnp.float32)]
    ppermute x0 -> x50, waiting for transfers between devices: none -> 79.8 us  [the longest x24 79.7 us: swap(): return lax.ppermute(values, 'dp', [(j, j ^ bit) for j in range(self.size)])]
    reduce_scatter x10 -> x0, waiting for transfers between devices: 60.4 us -> none  [the longest x3 21 us: reduce_pair(): lax.psum_scatter(second_grad.astype(jnp.bfloat16), 'fsdp', scatter_dimens...]
    concatenate x0 -> x12, other arithmetic: none -> 49.5 us  [the longest x1 14 us: per_device(): sum_qkv = jnp.concatenate([attn_a, attn_b], axis=1)]
    ppermute x0 -> x50, starting transfers between devices: none -> 34.3 us  [the longest x24 27.9 us: swap(): return lax.ppermute(values, 'dp', [(j, j ^ bit) for j in range(self.size)])]
    all_gather x8 -> x0, waiting for transfers between devices: 29.1 us -> none  [the longest x1 11.7 us: per_device(): lax.all_gather(attn_qkv, 'fsdp', axis=0, tiled=True)]
  transfers between devices with their start and end apart: 21 -> 50, of which waited for: 10 -> 10; matrix products, arithmetic and copies ran while one was open for 16% -> 46% of each run, Pallas kernels for 0% -> 7%
where the time goes in v1:
time: 788 us; the launch traced here: 776 us
  Pallas kernels  243 us (31%)
  matrix products  196 us (25%)
  other arithmetic  122 us (15%)
  local copies, waits for them, and re-layouts  95.2 us (12%)
  waiting for transfers between devices  79.8 us (10%)
  starting transfers between devices  34.3 us (4%)
    pallas_call x1, Pallas kernels, sum_cube(): pl.pallas_call(functools.partial(cube_kernel, plan), out_shape=[jax.Shape...  185 us
    ppermute x24, waiting for transfers between devices, swap(): return lax.ppermute(values, 'dp', [(j, j ^ bit) for j in range(self.size)])  79.7 us
    dot_general x28, matrix products, weight_grad(): lax.dot_general(left, right, DOWN_DIMS, preferred_element_type=jnp.float32)  66.7 us
    pallas_call x3, Pallas kernels, sum_everywhere(): pl.pallas_call(functools.partial(pair_kernel, axes), out_shape=jax.ShapeD...  58.2 us
    dot_general x16, matrix products, project(): return jnp.dot(left, right, preferred_element_type=jnp.float32)  52.1 us
    dot_general x16, matrix products, project_back(): lax.dot_general(left, right, ACROSS_DIMS, preferred_element_type=jnp.floa...  46.7 us
    ppermute x24, starting transfers between devices, swap(): return lax.ppermute(values, 'dp', [(j, j ^ bit) for j in range(self.size)])  27.9 us
    eq x1, local copies, waits for them, and re-layouts, per_device(): rel_index[None]  25.2 us
  transfers between devices with their start and end apart: 50, of which 10 were waited for; matrix products, arithmetic and copies ran while one was open for 46% of the time, Pallas kernels for 7%

profile of v1, /device:TPU:0, one launch (start us, length us, event | category | flops | bytes accessed | tf_op | source)
XLA Modules:
  0.0 776.4 jit_solution(12221844404393315698)
XLA Ops:
  12.3 7.7 iota_compare_fusion
  20.6 25.2 %copy.44 = pred[65,288,288]{2,0,1:T(8,128)(4,1)} copy(pred[65,288,288]{1,0,2:T(8,128)(4,1)} %iota_compare_fusion) | data formatting | bytes 10782720 | tf_op jit(solution)/shard_map/eq | solution.py:565
  45.9 8.8 %fusion.166 = f32[8,288,288]{2,0,1:T(8,128)} fusion(pred[65,288,288]{2,0,1:T(8,128)(4,1)} %copy.44, bf16[4,65]{1,0:T(4,128)(2,1)S(1)} %get-tuple-element.219, bf16[4,65]{1,0:T(4,128)(2,1)S(1)} %get-tuple-element.218), kind=kOutput, calls=%fused_computation.447 | convolution fusion | flops 86263840 | bytes 8046608 | tf_op jit(solution)/shard_map/hr,rqk->hqk/dot_general | solution.py:464
  54.7 5.5 copy.45
  65.8 6.9 multiply_convert_fusion.1
  76.3 4.3 broadcast_select_fusion.37
  93.3 11.6 %copy.93 = bf16[8,36,8,128]{3,2,0,1:T(8,128)(2,1)S(1)} copy(bf16[8,36,8,128]{3,2,1,0:T(8,128)(2,1)S(1)} %fusion.41) | data formatting | bytes 1179648 | tf_op jit(solution)/shard_map/reshape | solution.py:482
  122.5 19.1 %shard_map.271 = f32[8,1024]{1,0:T(8,128)} custom-call(f32[8,1024]{1,0:T(8,128)} %stack.52.x_ref), custom_call_target="tpu_custom_call" | custom-call | tf_op jit(solution)/shard_map/pallas_call | solution.py:124
  158.1 4.5 fusion.250
  174.9 6.9 fusion.2
  188.0 4.4 broadcast_select_fusion.33
  203.7 4.6 convolution_convert_fusion.2
  216.4 15.3 %shard_map.272 = f32[8,1024]{1,0:T(8,128)} custom-call(f32[8,1024]{1,0:T(8,128)} %pad_maximum_fusion.25.x_ref), custom_call_target="tpu_custom_call" | custom-call | tf_op jit(solution)/shard_map/pallas_call | solution.py:124
  261.2 5.3 collective-permute-done.34
  285.9 16.6 %fusion.61 = f32[8,65]{1,0:T(8,128)} fusion(f32[8,288,288]{1,2,0:T(8,128)S(1)} %subtract_multiply_fusion.2, s32[288,288]{0,1:T(8,128)S(1)} %copy-done.74), kind=kOutput, calls=%fused_computation.213 | convolution fusion | flops 522961920 | bytes 2988064 | tf_op jit(solution)/shard_map/hqk,rqk->hr/dot_general | solution.py:503
  320.8 5.2 fusion.9.refs_4_
  349.0 6.5 fusion.5
  360.2 4.3 broadcast_select_fusion.25
  371.4 23.8 %shard_map.274 = f32[24,1024]{1,0:T(8,128)} custom-call(f32[24,1024]{1,0:T(8,128)} %concatenate.255.x_ref), custom_call_target="tpu_custom_call" | custom-call | tf_op jit(solution)/shard_map/pallas_call | solution.py:124
  428.3 15.1 %collective-permute-done.27 = bf16[256,3072]{1,0:T(8,128)(2,1)S(1)} collective-permute-done((bf16[256,3072]{1,0:T(8,128)(2,1)S(1)}, bf16[256,3072]{1,0:T(8,128)(2,1)S(1)}, u32[]{:S(2)}, u32[]{:S(2)}) %collective-permute-start.27) | collective-permute-done | bytes 1572896 | tf_op jit(solution)/shard_map/ppermute | solution.py:390
  443.4 4.7 fusion.8.refs_3_
  452.8 4.7 fusion.10.refs_7_
  457.5 185.3 %shard_map.273 = (bf16[256,3072]{1,0:T(8,128)(2,1)}, bf16[256,1024]{1,0:T(8,128)(2,1)}, bf16[256,1536]{1,0:T(8,128)(2,1)}, bf16[256,3072]{1,0:T(8,128)(2,1)}, bf...) custom-call(bf16[256,3072]{1,0:T(8,128)(2,1)} %fusion.7.refs_0_, ...), custom_call_target="tpu_custom_call" | custom-call | tf_op jit(solution)/shard_map/pallas_call | solution.py:362
  651.3 6.6 collective-permute-done.43
  660.0 9.1 %collective-permute-done.46 = bf16[256,1024]{1,0:T(8,128)(2,1)S(1)} collective-permute-done((bf16[256,1024]{1,0:T(8,128)(2,1)}, bf16[256,1024]{1,0:T(8,128)(2,1)S(1)}, u32[]{:S(2)}, u32[]{:S(2)}) %collective-permute-start.46) | collective-permute-done | bytes 524320 | tf_op jit(solution)/shard_map/ppermute | solution.py:390
  670.1 23.5 %collective-permute-done.45 = bf16[256,1024]{1,0:T(8,128)(2,1)S(1)} collective-permute-done((bf16[256,1024]{1,0:T(8,128)(2,1)}, bf16[256,1024]{1,0:T(8,128)(2,1)S(1)}, u32[]{:S(2)}, u32[]{:S(2)}) %collective-permute-start.45) | collective-permute-done | bytes 524320 | tf_op jit(solution)/shard_map/ppermute | solution.py:390
  702.3 9.6 %collective-permute-done.42 = bf16[256,1536]{1,0:T(8,128)(2,1)S(1)} collective-permute-done((bf16[256,1536]{1,0:T(8,128)(2,1)S(1)}, bf16[256,1536]{1,0:T(8,128)(2,1)S(1)}, u32[]{:S(2)}, u32[]{:S(2)}) %collective-permute-start.42) | collective-permute-done | bytes 786464 | tf_op jit(solution)/shard_map/ppermute | solution.py:390
  713.9 14.0 %maximum_convert_fusion.2 = f32[512,3072]{1,0:T(8,128)} fusion(bf16[256,1536]{1,0:T(8,128)(2,1)S(1)} %get-tuple-element.133, bf16[256,1536]{1,0:T(8,128)(2,1)S(1)} %get-tuple-element.132, bf16[256,1536]{1,0:T(8,128)(2,1)S(1)} %get-tuple-element.131, bf16[256,1536]{1,0:T(8,128)(2,1)S(1)} %get-tuple-element.130), kind=kLoop, calls=%fused_computation.56 | loop fusion | flops 12582912 | bytes 9437184 | tf_op jit(solution)/shard_map/concatenate | solution.py:776
  741.4 7.8 %pad_maximum_fusion = f32[512,4096]{1,0:T(8,128)} fusion(f32[512,1024]{1,0:T(8,128)} %get-tuple-element.114, f32[512,3072]{1,0:T(8,128)} %maximum_convert_fusion), kind=kLoop, calls=%fused_computation.1 | loop fusion | flops 2097152 | bytes 16777216 | tf_op jit(solution)/shard_map/concatenate | solution.py:779
  754.8 6.0 pad_maximum_fusion.1
  760.8 7.8 %pad_maximum_fusion.2 = f32[512,4096]{1,0:T(8,128)} fusion(f32[512,1024]{1,0:T(8,128)} %get-tuple-element.112, f32[512,3072]{1,0:T(8,128)} %maximum_convert_fusion.3), kind=kLoop, calls=%fused_computation.3 | loop fusion | flops 2097152 | bytes 16777216 | tf_op jit(solution)/shard_map/concatenate | solution.py:773
  771.5 4.4 pad_maximum_fusion.3
  (687 shorter events, 285.2 us)
Async XLA Ops:
  1.5 58.7 %collective-permute-start = (bf16[17,512]{1,0:T(8,128)(2,1)S(1)}, bf16[17,512]{1,0:T(8,128)(2,1)S(1)}, u32[]{:S(2)}, u32[]{:S(2)}) collective-permute-start(bf16[17,512]{1,0:T(8,128)(2,1)S(1)} %maximum_bitcast_fusion), channel_id=1, source_target_pairs={{0,1},{1,0},{2,3},{3,2},{4,5},{5,4},{6,7},{7,6},{8,9},{9,8},{10,11... | collective-permute-start | bytes 52232 | tf_op jit(solution)/shard_map/ppermute | solution.py:147
  2.0 63.6 %collective-permute-start.1 = (bf16[512,4096]{1,0:T(8,128)(2,1)}, bf16[512,4096]{1,0:T(8,128)(2,1)}, u32[]{:S(2)}, u32[]{:S(2)}) collective-permute-start(bf16[512,4096]{1,0:T(8,128)(2,1)} %param.19), channel_id=1, source_target_pairs={{0,1},{1,0},{2,3},{3,2},{4,5},{5,4},{6,7},{7,6},{8,9},{9,8},{10,11... | collective-permute-start | bytes 12582920 | tf_op jit(solution)/shard_map/ppermute | solution.py:147
  2.1 73.7 %collective-permute-start.2 = (bf16[512,4096]{1,0:T(8,128)(2,1)}, bf16[512,4096]{1,0:T(8,128)(2,1)}, u32[]{:S(2)}, u32[]{:S(2)}) collective-permute-start(bf16[512,4096]{1,0:T(8,128)(2,1)} %param.20), channel_id=1, source_target_pairs={{0,1},{1,0},{2,3},{3,2},{4,5},{5,4},{6,7},{7,6},{8,9},{9,8},{10,11... | collective-permute-start | bytes 12582920 | tf_op jit(solution)/shard_map/ppermute | solution.py:147
  2.5 82.0 %collective-permute-start.3 = (bf16[512,3072]{1,0:T(8,128)(2,1)}, bf16[512,3072]{1,0:T(8,128)(2,1)}, u32[]{:S(2)}, u32[]{:S(2)}) collective-permute-start(bf16[512,3072]{1,0:T(8,128)(2,1)} %param.21), channel_id=1, source_target_pairs={{0,1},{1,0},{2,3},{3,2},{4,5},{5,4},{6,7},{7,6},{8,9},{9,8},{10,11... | collective-permute-start | bytes 9437192 | tf_op jit(solution)/shard_map/ppermute | solution.py:147
  2.6 43.2 %collective-permute-start.4 = (bf16[4,65]{1,0:T(4,128)(2,1)}, bf16[4,65]{1,0:T(4,128)(2,1)S(1)}, u32[]{:S(2)}, u32[]{:S(2)}) collective-permute-start(bf16[4,65]{1,0:T(4,128)(2,1)} %param.23), channel_id=1, source_target_pairs={{0,1},{1,0},{2,3},{3,2},{4,5},{5,4},{6,7},{7,6},{8,9},{9,8},{10,11... | collective-permute-start | bytes 1568 | tf_op jit(solution)/shard_map/ppermute | solution.py:147
  45.8 61.1 %collective-permute-start.5 = (bf16[512,1024]{1,0:T(8,128)(2,1)}, bf16[512,1024]{1,0:T(8,128)(2,1)}, u32[]{:S(2)}, u32[]{:S(2)}) collective-permute-start(bf16[512,1024]{1,0:T(8,128)(2,1)} %param.22), channel_id=1, source_target_pairs={{0,1},{1,0},{2,3},{3,2},{4,5},{5,4},{6,7},{7,6},{8,9},{9,8},{10,11... | collective-permute-start | bytes 3145736 | tf_op jit(solution)/shard_map/ppermute | solution.py:147
  60.2 52.5 %collective-permute-start.6 = (bf16[512,2048]{1,0:T(8,128)(2,1)}, bf16[512,2048]{1,0:T(8,128)(2,1)S(1)}, u32[]{:S(2)}, u32[]{:S(2)}) collective-permute-start(bf16[512,2048]{1,0:T(8,128)(2,1)} %param.24), channel_id=1, source_target_pairs={{0,1},{1,0},{2,3},{3,2},{4,5},{5,4},{6,7},{7,6},{8,9},{9,8},{10,11... | collective-permute-start | bytes 6291464 | tf_op jit(solution)/shard_map/ppermute | solution.py:147
  65.6 81.7 %collective-permute-start.7 = (bf16[512,1024]{1,0:T(8,128)(2,1)}, bf16[512,1024]{1,0:T(8,128)(2,1)}, u32[]{:S(2)}, u32[]{:S(2)}) collective-permute-start(bf16[512,1024]{1,0:T(8,128)(2,1)} %param.26), channel_id=1, source_target_pairs={{0,1},{1,0},{2,3},{3,2},{4,5},{5,4},{6,7},{7,6},{8,9},{9,8},{10,11... | collective-permute-start | bytes 3145736 | tf_op jit(solution)/shard_map/ppermute | solution.py:147
  75.7 78.3 %collective-permute-start.8 = (bf16[512,4096]{1,0:T(8,128)(2,1)}, bf16[512,4096]{1,0:T(8,128)(2,1)}, u32[]{:S(2)}, u32[]{:S(2)}) collective-permute-start(bf16[512,4096]{1,0:T(8,128)(2,1)} %param.27), channel_id=1, source_target_pairs={{0,1},{1,0},{2,3},{3,2},{4,5},{5,4},{6,7},{7,6},{8,9},{9,8},{10,11... | collective-permute-start | bytes 12582920 | tf_op jit(solution)/shard_map/ppermute | solution.py:147
  84.5 78.0 %collective-permute-start.9 = (bf16[512,4096]{1,0:T(8,128)(2,1)}, bf16[512,4096]{1,0:T(8,128)(2,1)}, u32[]{:S(2)}, u32[]{:S(2)}) collective-permute-start(bf16[512,4096]{1,0:T(8,128)(2,1)} %param.28), channel_id=1, source_target_pairs={{0,1},{1,0},{2,3},{3,2},{4,5},{5,4},{6,7},{7,6},{8,9},{9,8},{10,11... | collective-permute-start | bytes 12582920 | tf_op jit(solution)/shard_map/ppermute | solution.py:147
  182.6 234.6 %collective-permute-start.31 = (bf16[288,512]{1,0:T(8,128)(2,1)}, bf16[288,512]{1,0:T(8,128)(2,1)}, u32[]{:S(2)}, u32[]{:S(2)}) collective-permute-start(bf16[288,512]{1,0:T(8,128)(2,1)} %copy-done.110), channel_id=1, source_target_pairs={{0,1},{1,0},{2,3},{3,2},{4,5},{5,4},{6,7},{7,6},{8,9},{9,8},{10,11... | collective-permute-start | bytes 884744 | tf_op jit(solution)/shard_map/ppermute | solution.py:147
  194.9 57.8 %collective-permute-start.26 = (bf16[288,4096]{1,0:T(8,128)(2,1)}, bf16[288,4096]{1,0:T(8,128)(2,1)}, u32[]{:S(2)}, u32[]{:S(2)}) collective-permute-start(bf16[288,4096]{1,0:T(8,128)(2,1)} %get-tuple-element.223), channel_id=1, source_target_pairs={{0,1},{1,0},{2,3},{3,2},{4,5},{5,4},{6,7},{7,6},{8,9},{9,8},{10,11... | collective-permute-start | bytes 7077896 | tf_op jit(solution)/shard_map/ppermute | solution.py:147
  211.2 45.9 %collective-permute-start.17 = (bf16[288,1024]{1,0:T(8,128)(2,1)}, bf16[288,1024]{1,0:T(8,128)(2,1)}, u32[]{:S(2)}, u32[]{:S(2)}) collective-permute-start(bf16[288,1024]{1,0:T(8,128)(2,1)} %convert_element_type.324), channel_id=1, source_target_pairs={{0,1},{1,0},{2,3},{3,2},{4,5},{5,4},{6,7},{7,6},{8,9},{9,8},{10,11... | collective-permute-start | bytes 1769480 | tf_op jit(solution)/shard_map/ppermute | solution.py:147
  240.9 28.5 %collective-permute-start.15 = (bf16[288,2048]{1,0:T(8,128)(2,1)S(1)}, bf16[288,2048]{1,0:T(8,128)(2,1)S(1)}, u32[]{:S(2)}, u32[]{:S(2)}) collective-permute-start(bf16[288,2048]{1,0:T(8,128)(2,1)S(1)} %add_convert_fusion), channel_id=1, source_target_pairs={{0,1},{1,0},{2,3},{3,2},{4,5},{5,4},{6,7},{7,6},{8,9},{9,8},{10,11... | collective-permute-start | bytes 3538952 | tf_op jit(solution)/shard_map/ppermute | solution.py:147
  257.0 56.3 %collective-permute-start.22 = (bf16[256,3072]{1,0:T(8,128)(2,1)}, bf16[256,3072]{1,0:T(8,128)(2,1)}, u32[]{:S(2)}, u32[]{:S(2)}) collective-permute-start(bf16[256,3072]{1,0:T(8,128)(2,1)} %convolution_convert_fusion.3), channel_id=1, source_target_pairs={{0,2},{2,0},{4,6},{6,4},{8,10},{10,8},{12,14},{14,12},{16,18},{18,... | collective-permute-start | bytes 4718600 | tf_op jit(solution)/shard_map/ppermute | solution.py:390
  266.6 53.4 %collective-permute-start.28 = (bf16[256,3072]{1,0:T(8,128)(2,1)}, bf16[256,3072]{1,0:T(8,128)(2,1)}, u32[]{:S(2)}, u32[]{:S(2)}) collective-permute-start(bf16[256,3072]{1,0:T(8,128)(2,1)} %convolution_convert_fusion.2), channel_id=1, source_target_pairs={{0,4},{2,6},{4,0},{6,2},{8,12},{10,14},{12,8},{14,10},{16,20},{18,... | collective-permute-start | bytes 4718600 | tf_op jit(solution)/shard_map/ppermute | solution.py:390
  308.1 33.1 %collective-permute-start.19 = (bf16[288,3072]{1,0:T(8,128)(2,1)}, bf16[288,3072]{1,0:T(8,128)(2,1)}, u32[]{:S(2)}, u32[]{:S(2)}) collective-permute-start(bf16[288,3072]{1,0:T(8,128)(2,1)} %bitcast.208), channel_id=1, source_target_pairs={{0,1},{1,0},{2,3},{3,2},{4,5},{5,4},{6,7},{7,6},{8,9},{9,8},{10,11... | collective-permute-start | bytes 5308424 | tf_op jit(solution)/shard_map/ppermute | solution.py:147
  308.1 28.7 %collective-permute-start.23 = (bf16[256,1024]{1,0:T(8,128)(2,1)}, bf16[256,1024]{1,0:T(8,128)(2,1)}, u32[]{:S(2)}, u32[]{:S(2)}) collective-permute-start(bf16[256,1024]{1,0:T(8,128)(2,1)} %convolution_convert_fusion.13), channel_id=1, source_target_pairs={{0,2},{2,0},{4,6},{6,4},{8,10},{10,8},{12,14},{14,12},{16,18},{18,... | collective-permute-start | bytes 1572872 | tf_op jit(solution)/shard_map/ppermute | solution.py:390
  348.9 53.2 %collective-permute-start.25 = (bf16[288,512]{1,0:T(8,128)(2,1)}, bf16[288,512]{1,0:T(8,128)(2,1)}, u32[]{:S(2)}, u32[]{:S(2)}) collective-permute-start(bf16[288,512]{1,0:T(8,128)(2,1)} %get-tuple-element.167), channel_id=1, source_target_pairs={{0,1},{1,0},{2,3},{3,2},{4,5},{5,4},{6,7},{7,6},{8,9},{9,8},{10,11... | collective-permute-start | bytes 884744 | tf_op jit(solution)/shard_map/ppermute | solution.py:147
  358.9 58.4 %collective-permute-start.32 = (bf16[288,4096]{1,0:T(8,128)(2,1)}, bf16[288,4096]{1,0:T(8,128)(2,1)}, u32[]{:S(2)}, u32[]{:S(2)}) collective-permute-start(bf16[288,4096]{1,0:T(8,128)(2,1)} %fusion.5), channel_id=1, source_target_pairs={{0,1},{1,0},{2,3},{3,2},{4,5},{5,4},{6,7},{7,6},{8,9},{9,8},{10,11... | collective-permute-start | bytes 7077896 | tf_op jit(solution)/shard_map/ppermute | solution.py:147
  359.4 55.0 %collective-permute-start.24 = (bf16[256,1536]{1,0:T(8,128)(2,1)}, bf16[256,1536]{1,0:T(8,128)(2,1)}, u32[]{:S(2)}, u32[]{:S(2)}) collective-permute-start(bf16[256,1536]{1,0:T(8,128)(2,1)} %convolution_convert_fusion.5), channel_id=1, source_target_pairs={{0,2},{2,0},{4,6},{6,4},{8,10},{10,8},{12,14},{14,12},{16,18},{18,... | collective-permute-start | bytes 2359304 | tf_op jit(solution)/shard_map/ppermute | solution.py:390
  359.7 65.7 %collective-permute-start.30 = (bf16[256,1536]{1,0:T(8,128)(2,1)}, bf16[256,1536]{1,0:T(8,128)(2,1)}, u32[]{:S(2)}, u32[]{:S(2)}) collective-permute-start(bf16[256,1536]{1,0:T(8,128)(2,1)} %convolution_convert_fusion.4), channel_id=1, source_target_pairs={{0,4},{2,6},{4,0},{6,2},{8,12},{10,14},{12,8},{14,10},{16,20},{18,... | collective-permute-start | bytes 2359304 | tf_op jit(solution)/shard_map/ppermute | solution.py:390
  411.7 31.7 %collective-permute-start.27 = (bf16[256,3072]{1,0:T(8,128)(2,1)S(1)}, bf16[256,3072]{1,0:T(8,128)(2,1)S(1)}, u32[]{:S(2)}, u32[]{:S(2)}) collective-permute-start(bf16[256,3072]{1,0:T(8,128)(2,1)S(1)} %convolution_convert_fusion.1), channel_id=1, source_target_pairs={{0,2},{2,0},{4,6},{6,4},{8,10},{10,8},{12,14},{14,12},{16,18},{18,... | collective-permute-start | bytes 4718600 | tf_op jit(solution)/shard_map/ppermute | solution.py:390
  420.8 32.0 %collective-permute-start.33 = (bf16[256,3072]{1,0:T(8,128)(2,1)S(1)}, bf16[256,3072]{1,0:T(8,128)(2,1)S(1)}, u32[]{:S(2)}, u32[]{:S(2)}) collective-permute-start(bf16[256,3072]{1,0:T(8,128)(2,1)S(1)} %convolution_convert_fusion), channel_id=1, source_target_pairs={{0,4},{2,6},{4,0},{6,2},{8,12},{10,14},{12,8},{14,10},{16,20},{18,... | collective-permute-start | bytes 4718600 | tf_op jit(solution)/shard_map/ppermute | solution.py:390
  424.9 24.7 %collective-permute-start.37 = (bf16[256,2048]{1,0:T(8,128)(2,1)S(1)}, bf16[256,2048]{1,0:T(8,128)(2,1)S(1)}, u32[]{:S(2)}, u32[]{:S(2)}) collective-permute-start(bf16[256,2048]{1,0:T(8,128)(2,1)S(1)} %pad_maximum_fusion.18), channel_id=1, source_target_pairs={{0,8},{2,10},{4,12},{6,14},{8,0},{10,2},{12,4},{14,6},{16,24},{18,... | collective-permute-start | bytes 3145736 | tf_op jit(solution)/shard_map/ppermute | solution.py:390
  646.8 81.2 %collective-permute-start.39 = (bf16[256,2048]{1,0:T(8,128)(2,1)}, bf16[256,2048]{1,0:T(8,128)(2,1)S(1)}, u32[]{:S(2)}, u32[]{:S(2)}) collective-permute-start(bf16[256,2048]{1,0:T(8,128)(2,1)} %get-tuple-element.52), channel_id=1, source_target_pairs={{0,8},{2,10},{4,12},{6,14},{8,0},{10,2},{12,4},{14,6},{16,24},{18,... | collective-permute-start | bytes 3145736 | tf_op jit(solution)/shard_map/ppermute | solution.py:390
  648.6 88.1 %collective-permute-start.38 = (bf16[256,3072]{1,0:T(8,128)(2,1)S(1)}, bf16[256,3072]{1,0:T(8,128)(2,1)S(1)}, u32[]{:S(2)}, u32[]{:S(2)}) collective-permute-start(bf16[256,3072]{1,0:T(8,128)(2,1)S(1)} %copy-done.80), channel_id=1, source_target_pairs={{0,4},{2,6},{4,0},{6,2},{8,12},{10,14},{12,8},{14,10},{16,20},{18,... | collective-permute-start | bytes 4718600 | tf_op jit(solution)/shard_map/ppermute | solution.py:390
  649.6 87.3 %collective-permute-start.40 = (bf16[256,3072]{1,0:T(8,128)(2,1)S(1)}, bf16[256,3072]{1,0:T(8,128)(2,1)S(1)}, u32[]{:S(2)}, u32[]{:S(2)}) collective-permute-start(bf16[256,3072]{1,0:T(8,128)(2,1)S(1)} %copy-done.79), channel_id=1, source_target_pairs={{0,2},{2,0},{4,6},{6,4},{8,10},{10,8},{12,14},{14,12},{16,18},{18,... | collective-permute-start | bytes 4718600 | tf_op jit(solution)/shard_map/ppermute | solution.py:390
  657.9 35.7 %collective-permute-start.45 = (bf16[256,1024]{1,0:T(8,128)(2,1)}, bf16[256,1024]{1,0:T(8,128)(2,1)S(1)}, u32[]{:S(2)}, u32[]{:S(2)}) collective-permute-start(bf16[256,1024]{1,0:T(8,128)(2,1)} %get-tuple-element.58), channel_id=1, source_target_pairs={{0,4},{2,6},{4,0},{6,2},{8,12},{10,14},{12,8},{14,10},{16,20},{18,... | collective-permute-start | bytes 1572872 | tf_op jit(solution)/shard_map/ppermute | solution.py:390
  669.2 26.3 %collective-permute-start.44 = (bf16[256,1024]{1,0:T(8,128)(2,1)S(1)}, bf16[256,1024]{1,0:T(8,128)(2,1)S(1)}, u32[]{:S(2)}, u32[]{:S(2)}) collective-permute-start(bf16[256,1024]{1,0:T(8,128)(2,1)S(1)} %copy-done.99), channel_id=1, source_target_pairs={{0,2},{2,0},{4,6},{6,4},{8,10},{10,8},{12,14},{14,12},{16,18},{18,... | collective-permute-start | bytes 1572872 | tf_op jit(solution)/shard_map/ppermute | solution.py:390
  712.0 37.2 %collective-permute-start.47 = (bf16[256,3072]{1,0:T(8,128)(2,1)}, bf16[256,3072]{1,0:T(8,128)(2,1)}, u32[]{:S(2)}, u32[]{:S(2)}) collective-permute-start(bf16[256,3072]{1,0:T(8,128)(2,1)} %get-tuple-element.60), channel_id=1, source_target_pairs={{0,4},{2,6},{4,0},{6,2},{8,12},{10,14},{12,8},{14,10},{16,20},{18,... | collective-permute-start | bytes 4718600 | tf_op jit(solution)/shard_map/ppermute | solution.py:390
  728.0 40.7 %collective-permute-start.49 = (bf16[256,3072]{1,0:T(8,128)(2,1)}, bf16[256,3072]{1,0:T(8,128)(2,1)}, u32[]{:S(2)}, u32[]{:S(2)}) collective-permute-start(bf16[256,3072]{1,0:T(8,128)(2,1)} %get-tuple-element.62), channel_id=1, source_target_pairs={{0,2},{2,0},{4,6},{6,4},{8,10},{10,8},{12,14},{14,12},{16,18},{18,... | collective-permute-start | bytes 4718600 | tf_op jit(solution)/shard_map/ppermute | solution.py:390
  (209 other events, 2241.2 us)

commit v2 on v0

v2 whole, which is shorter than its diff:
```python
import functools

import jax
import jax.numpy as jnp
from jax import lax
from jax.experimental import pallas as pl
from jax.experimental.pallas import tpu as pltpu
from jax.sharding import PartitionSpec as P

EPSILON = 1e-05
MASKED = -1000000000.0
AHEAD = 4
DOWN_DIMS = (((0,), (0,)), ((), ()))
ACROSS_DIMS = (((1,), (1,)), ((), ()))


def pair_partners(axes):
    partners = []
    for name, size in axes:
        me = lax.axis_index(name)
        bit = 1
        while bit < size:
            partners.append({name: me + bit * (1 - 2 * ((me // bit) % 2))})
            bit *= 2
    return partners


def sum_stages(axes):
    stages = []
    for name, size in axes:
        bits = [1 << k for k in range(size.bit_length() - 1)]
        stages += [(name, bits[k : k + 2]) for k in range(0, len(bits), 2)]
    return stages


def stage_partners(name, bits):
    me = lax.axis_index(name)
    low, count = bits[0], 2 ** len(bits)
    place = lax.rem(me // low, count)
    return place, [{name: me + low * (other - place)} for other in range(count)]


def pair_kernel(axes, modes, *refs):
    refs = list(refs)

    def pick(count):
        picked = refs[:count]
        del refs[:count]
        return picked

    size = dict(axes)["fsdp"]
    (x_ref,), shared, (o_ref,) = pick(1), pick(len(modes)), pick(1)
    outs = [pick(size - 1) for _ in modes]
    slots, send_sems, recv_sems, share_send, share_recv = refs
    stages = [stage_partners(name, bits) for name, bits in sum_stages(axes)]
    near = len([name for name, _ in sum_stages(axes) if name == "fsdp"])
    me = lax.axis_index("fsdp")
    peers = [{"fsdp": lax.rem(me + size - step, size)} for step in range(1, size)]
    barrier = pltpu.get_barrier_semaphore()
    greeted = 0
    for place, devices in stages:
        for other, device in enumerate(devices):

            @pl.when(other != place)
            def _(device=device):
                pl.semaphore_signal(
                    barrier, inc=1, device_id=device, device_id_type=pl.DeviceIdType.MESH
                )

        greeted += len(devices) - 1
    if modes and size > 4:
        for peer in peers:
            pl.semaphore_signal(barrier, inc=1, device_id=peer, device_id_type=pl.DeviceIdType.MESH)
        greeted += size - 1
    pl.semaphore_wait(barrier, greeted)
    copies = []
    for index, (mode, source) in enumerate(zip(modes, shared)):
        for step, peer in enumerate(peers):
            if mode == "columns":
                width = source.shape[1] // size
                start = pl.multiple_of(peer["fsdp"] * width, width)
                source_now = source.at[:, pl.ds(start, width)]
            else:
                source_now = source
            copies.append(
                pltpu.make_async_remote_copy(
                    src_ref=source_now,
                    dst_ref=outs[index][step],
                    send_sem=share_send.at[index, step],
                    recv_sem=share_recv.at[index, step],
                    device_id=peer,
                    device_id_type=pl.DeviceIdType.MESH,
                )
            )
    o_ref[...] = x_ref[...]
    started = False
    for stage, (place, devices) in enumerate(stages):

        def exchange(other, device, stage=stage, place=place):
            return pltpu.make_async_remote_copy(
                src_ref=o_ref,
                dst_ref=slots.at[stage, place],
                send_sem=send_sems.at[stage, other],
                recv_sem=recv_sems.at[stage, place],
                device_id=device,
                device_id_type=pl.DeviceIdType.MESH,
            )

        def arrival(other, device, stage=stage):
            return pltpu.make_async_remote_copy(
                src_ref=o_ref,
                dst_ref=slots.at[stage, other],
                send_sem=send_sems.at[stage, other],
                recv_sem=recv_sems.at[stage, other],
                device_id=device,
                device_id_type=pl.DeviceIdType.MESH,
            )

        for other, device in enumerate(devices):
            pl.when(other != place)(exchange(other, device).start)
        if not started and stage + 1 >= near:
            started = True
            for copy in copies:
                copy.start()
        for other, device in enumerate(devices):
            pl.when(other != place)(arrival(other, device).wait)
        slots[stage, pl.ds(place, 1)] = o_ref[...][None]
        total = slots[stage, 0]
        for other in range(1, len(devices)):
            total += slots[stage, other]
        o_ref[...] = total
    for copy in copies:
        copy.wait()


def sum_and_share(rows, axes, values, shared, collective_id):
    size = dict(axes)["fsdp"]
    stages = len(sum_stages(axes))
    if any(count & (count - 1) for _, count in axes) or stages == 0:
        total = lax.psum(values, tuple(name for name, _ in axes))
        return total, [
            (rows.all_frames if mode == "all" else rows.all_frames_own_columns)(array)[1:]
            for array, mode in shared
        ]
    shapes = [
        array.shape if mode == "all" else (array.shape[0], array.shape[1] // size)
        for array, mode in shared
    ]
    out = pl.pallas_call(
        functools.partial(pair_kernel, axes, [mode for _, mode in shared]),
        out_shape=[jax.ShapeDtypeStruct(values.shape, values.dtype)]
        + [
            jax.ShapeDtypeStruct(shape, array.dtype)
            for shape, (array, _) in zip(shapes, shared)
            for _ in range(size - 1)
        ],
        in_specs=[pl.BlockSpec(memory_space=pltpu.VMEM)]
        + [pl.BlockSpec(memory_space=pl.ANY)] * len(shared),
        out_specs=[pl.BlockSpec(memory_space=pltpu.VMEM)]
        + [pl.BlockSpec(memory_space=pl.ANY)] * (len(shared) * (size - 1)),
        scratch_shapes=[
            pltpu.VMEM((stages, 4) + values.shape, values.dtype),
            pltpu.SemaphoreType.DMA((stages, 4)),
            pltpu.SemaphoreType.DMA((stages, 4)),
            pltpu.SemaphoreType.DMA((max(len(shared), 1), max(size - 1, 1))),
            pltpu.SemaphoreType.DMA((max(len(shared), 1), max(size - 1, 1))),
        ],
        compiler_params=pltpu.CompilerParams(
            collective_id=collective_id, has_side_effects=True, vmem_limit_bytes=60 * 2**20
        ),
    )(values, *[array for array, _ in shared])
    return out[0], [
        out[1 + k * (size - 1) : 1 + (k + 1) * (size - 1)] for k in range(len(shared))
    ]


class Rows:
    def __init__(self, size):
        self.size = size
        self.me = lax.axis_index("fsdp")

    def owner(self, step):
        return lax.rem(self.me + step, self.size)

    def shift(self, values, step):
        return lax.ppermute(
            values, "fsdp", [(j, (j - step) % self.size) for j in range(self.size)]
        )

    def gather(self, block):
        return [(self.me, block)] + [
            (self.owner(step), self.shift(block, step)) for step in range(1, self.size)
        ]

    def columns(self, values, owner):
        width = values.shape[1] // self.size
        return lax.dynamic_slice_in_dim(values, owner * width, width, axis=1)

    def order(self, parts, axis):
        if self.size == 1:
            return parts[0]
        width = parts[0].shape[axis]
        twice = jnp.concatenate(parts + parts, axis=axis)
        start = lax.rem(self.size - self.me, self.size) * width
        return lax.dynamic_slice_in_dim(twice, start, width * self.size, axis=axis)

    def all_frames(self, values):
        return [values] + [self.shift(values, step) for step in range(1, self.size)]

    def all_frames_own_columns(self, values):
        return [self.columns(values, self.me)] + [
            self.shift(self.columns(values, self.owner(self.size - step)), step)
            for step in range(1, self.size)
        ]


def cube_rounds(bits):
    if len(bits) > 2 and bits[-1] == 2 * bits[-2]:
        return tuple(("swap", bit) for bit in bits[:-2]) + (("give", bits[-2]), ("mid", bits[-2]))
    return tuple(("swap", bit) for bit in bits)


def cube_kernel(axes, plan, lines, *refs):
    me = lax.axis_index("dp")
    refs = list(refs)

    def pick(count):
        picked = refs[:count]
        del refs[:count]
        return picked

    arrays = [len(columns) for _, columns, _ in plan]
    inputs, small_refs = pick(2 * sum(arrays)), pick(len(lines))
    outputs, (small_out,) = pick(sum(arrays)), pick(1)
    kinds, first = [], 0
    for rounds, columns, chunk in plan:
        whole, other, result = pick(3)
        sums = pick(len(rounds))
        send_sems, recv_sems = pick(2)
        rows, start, steps = whole.shape[0], 0, []
        for name, bit in rounds:
            step = dict(name=name, rows=rows, before=start)
            if name == "swap":
                step["upper"] = lax.rem(me // bit, 2)
                step["partner"] = me + bit * (1 - 2 * step["upper"])
                step["sends"] = step["takes"] = None
            else:
                place = lax.rem(me // bit, 4)
                inner = (place == 1) | (place == 2)
                if name == "give":
                    step["partner"] = me + bit * (1 - 2 * lax.rem(place, 2))
                    step["sends"], step["takes"] = jnp.logical_not(inner), inner
                else:
                    step["upper"] = place // 2
                    step["partner"] = me + bit * (1 - 2 * step["upper"])
                    step["sends"] = step["takes"] = inner
            if name != "give":
                rows //= 2
                start = start + step["upper"] * rows
            step["after"] = start
            steps.append(step)
        edges = [sum(columns[:k]) for k in range(len(columns) + 1)]
        kinds.append(
            dict(
                steps=steps,
                columns=columns,
                edges=edges,
                chunk=chunk,
                count=edges[-1] // chunk,
                whole=whole,
                other=other,
                result=result,
                sums=sums,
                send=send_sems,
                recv=recv_sems,
                first=first,
            )
        )
        first += len(columns)
    load_sems, store_sems, slots, small_send, small_recv = refs
    partners = pair_partners(axes)

    def loads(kind, place):
        index = kind["first"] + place
        columns = pl.ds(kind["edges"][place], kind["columns"][place])
        return [
            pltpu.make_async_copy(
                inputs[2 * index + term],
                kind[name].at[:, columns],
                load_sems.at[2 * index + term],
            )
            for term, name in enumerate(("whole", "other"))
        ]

    def store(kind, place):
        index = kind["first"] + place
        columns = pl.ds(kind["edges"][place], kind["columns"][place])
        return pltpu.make_async_copy(
            kind["result"].at[:, columns], outputs[index], store_sems.at[index]
        )

    for place in range(max(arrays)):
        for kind in kinds:
            if place < len(kind["columns"]):
                for copy in loads(kind, place):
                    copy.start()
    small_out[...] = jnp.zeros_like(small_out)
    line = 0
    for ref, rows in zip(small_refs, lines):
        for row in rows:
            small_out[line : line + 1, : ref.shape[1]] = ref[row : row + 1, :]
            line += 1
    barrier = pltpu.get_barrier_semaphore()
    lines = sorted({bit for rounds, _, _ in plan for name, bit in rounds if name == "mid"})
    for partner in partners:
        pl.semaphore_signal(barrier, inc=1, device_id=partner, device_id_type=pl.DeviceIdType.MESH)
    if lines:
        (bit,) = lines
        place = lax.rem(me // bit, 4)
        inner = (place == 1) | (place == 2)

        @pl.when(inner)
        def _():
            pl.semaphore_signal(
                barrier,
                inc=1,
                device_id={"dp": me + bit * (1 - 2 * (place // 2))},
                device_id_type=pl.DeviceIdType.MESH,
            )
            pl.semaphore_wait(barrier, len(partners) + 1)

        @pl.when(jnp.logical_not(inner))
        def _():
            pl.semaphore_wait(barrier, len(partners))

    else:
        pl.semaphore_wait(barrier, len(partners))

    def window(kind, index):
        return pl.ds(pl.multiple_of(index * kind["chunk"], kind["chunk"]), kind["chunk"])

    def aligned(start, rows):
        return pl.ds(start if isinstance(start, int) else pl.multiple_of(start, rows), rows)

    def source(kind, number):
        return kind["whole"] if number == 0 else kind["sums"][number - 1]

    def copy_in(kind, number, index):
        step, columns = kind["steps"][number], window(kind, index)
        rows = step["rows"]
        given = pl.ds(0, rows)
        if step["name"] != "give":
            given = aligned((1 - step["upper"]) * (rows // 2), rows // 2)
        return pltpu.make_async_remote_copy(
            src_ref=source(kind, number).at[given, columns],
            dst_ref=kind["sums"][number].at[:, columns],
            send_sem=kind["send"].at[number, index],
            recv_sem=kind["recv"].at[number, index],
            device_id={"dp": step["partner"]},
            device_id_type=pl.DeviceIdType.MESH,
        )

    def copy_out(kind, number, index):
        step = kind["steps"][number]
        rows = step["rows"] if step["name"] == "give" else step["rows"] // 2
        start = step["before"] if step["name"] == "give" else step["after"]
        block = kind["result"].at[aligned(start, rows), window(kind, index)]
        slot = 2 * len(kind["steps"]) - 1 - number
        return pltpu.make_async_remote_copy(
            src_ref=block,
            dst_ref=block,
            send_sem=kind["send"].at[slot, index],
            recv_sem=kind["recv"].at[slot, index],
            device_id={"dp": step["partner"]},
            device_id_type=pl.DeviceIdType.MESH,
        )

    def when(condition, action):
        if condition is None:
            action()
        else:
            pl.when(condition)(action)

    def end_in(kind, number, index):
        step, columns = kind["steps"][number], window(kind, index)
        copy = copy_in(kind, number, index)
        last = number == len(kind["steps"]) - 1

        def add():
            copy.wait_recv()
            rows = step["rows"]
            kept = pl.ds(0, rows)
            if step["name"] != "give":
                rows //= 2
                kept = aligned(step["upper"] * rows, rows)
            total = (
                source(kind, number)[kept, columns].astype(jnp.float32)
                + kind["sums"][number][:, columns].astype(jnp.float32)
            ).astype(kind["whole"].dtype)
            if last:
                kind["result"][aligned(step["after"], rows), columns] = total
            else:
                kind["sums"][number][:, columns] = total

        when(step["sends"], copy.wait_send)
        when(step["takes"], add)

    def advance(kind, stage, index):
        depth = len(kind["steps"])
        if stage == 0:
            for place, edge in enumerate(kind["edges"][:-1]):

                @pl.when(index == edge // kind["chunk"])
                def _(place=place):
                    for copy in loads(kind, place):
                        copy.wait()

            columns = window(kind, index)
            kind["whole"][:, columns] = (
                kind["whole"][:, columns].astype(jnp.float32)
                + kind["other"][:, columns].astype(jnp.float32)
            ).astype(kind["whole"].dtype)
        elif stage <= depth:
            end_in(kind, stage - 1, index)
        else:
            number = 2 * depth - stage
            step = kind["steps"][number]
            copy = copy_out(kind, number, index)
            when(step["takes"], copy.wait_send)
            when(step["sends"], copy.wait_recv)
        if stage < depth:
            when(kind["steps"][stage]["sends"], copy_in(kind, stage, index).start)
        elif stage < 2 * depth:
            number = 2 * depth - 1 - stage
            when(kind["steps"][number]["takes"], copy_out(kind, number, index).start)
        else:
            for place, edge in enumerate(kind["edges"][1:]):

                @pl.when(index == edge // kind["chunk"] - 1)
                def _(place=place):
                    store(kind, place).start()

    def exchange(stage):
        return pltpu.make_async_remote_copy(
            src_ref=small_out,
            dst_ref=slots.at[stage],
            send_sem=small_send.at[stage],
            recv_sem=small_recv.at[stage],
            device_id=partners[stage],
            device_id_type=pl.DeviceIdType.MESH,
        )

    last = max(kind["count"] + 2 * len(kind["steps"]) for kind in kinds)
    last = max(last, len(partners) + 1)

    @pl.loop(0, last)
    def _(tick):
        for stage in range(len(partners) + 1):

            @pl.when(tick == stage)
            def _(stage=stage):
                if stage > 0:
                    exchange(stage - 1).wait()
                    small_out[...] += slots[stage - 1]
                if stage < len(partners):
                    exchange(stage).start()

        for stage in range(2 * max(len(kind["steps"]) for kind in kinds) + 1):
            for kind in kinds:
                if stage <= 2 * len(kind["steps"]):

                    @pl.when((tick >= stage) & (tick < stage + kind["count"]))
                    def _(kind=kind, stage=stage):
                        advance(kind, stage, tick - stage)

    for kind in kinds:
        for place in range(len(kind["columns"])):
            store(kind, place).wait()


def sum_cube(axes, parts, plan, small, lines, width, collective_id):
    shape = (-(-sum(len(rows) for rows in lines) // 8) * 8, width)
    flat = [term for kind in parts for pair in kind for term in pair]
    scratch = []
    for kind, (rounds, columns, chunk) in zip(parts, plan):
        rows, total, dtype = kind[0][0].shape[0], sum(columns), kind[0][0].dtype
        scratch += [pltpu.VMEM((rows, total), dtype)] * 3
        for name, _ in rounds:
            rows = rows if name == "give" else rows // 2
            scratch.append(pltpu.VMEM((rows, total), dtype))
        scratch += [pltpu.SemaphoreType.DMA((2 * len(rounds), total // chunk))] * 2
    stages = sum(size.bit_length() - 1 for _, size in axes)
    scratch += [
        pltpu.SemaphoreType.DMA((len(flat),)),
        pltpu.SemaphoreType.DMA((len(flat) // 2,)),
        pltpu.VMEM((stages,) + shape, jnp.float32),
        pltpu.SemaphoreType.DMA((stages,)),
        pltpu.SemaphoreType.DMA((stages,)),
    ]
    *out, sums = pl.pallas_call(
        functools.partial(cube_kernel, axes, plan, lines),
        out_shape=[jax.ShapeDtypeStruct(own.shape, own.dtype) for kind in parts for own, _ in kind]
        + [jax.ShapeDtypeStruct(shape, jnp.float32)],
        in_specs=[pl.BlockSpec(memory_space=pl.ANY)] * len(flat)
        + [pl.BlockSpec(memory_space=pltpu.VMEM)] * len(small),
        out_specs=[pl.BlockSpec(memory_space=pl.ANY)] * (len(flat) // 2)
        + [pl.BlockSpec(memory_space=pltpu.VMEM)],
        scratch_shapes=scratch,
        compiler_params=pltpu.CompilerParams(
            collective_id=collective_id, has_side_effects=True, vmem_limit_bytes=60 * 2**20
        ),
    )(*flat, *small)
    result = []
    for kind in parts:
        result.append(out[: len(kind)])
        out = out[len(kind) :]
    return result, sums


class Groups:
    def __init__(self, axes):
        self.axes = axes
        self.size = dict(axes)["dp"]
        self.me = lax.axis_index("dp")
        bits = [1 << k for k in range(self.size.bit_length() - 1)]
        self.plain = any(size & (size - 1) for _, size in axes) or not bits
        first, rest = bits[:3], bits[3:]
        self.orders = [[1]] * 4
        if first:
            one, two, three = first[0], first[1 % len(first)], first[2 % len(first)]
            for kind, order in enumerate(
                ((one, two, three), (two, one, three), (three, one, two), (three, two, one))
            ):
                self.orders[kind] = list(dict.fromkeys(order)) + rest

    def swap(self, values, bit):
        return lax.ppermute(values, "dp", [(j, j ^ bit) for j in range(self.size)])

    def upper(self, bit):
        return lax.rem(self.me // bit, 2)

    def in_order(self, bit, mine, other):
        low = self.upper(bit) == 0
        return jnp.concatenate([jnp.where(low, mine, other), jnp.where(low, other, mine)], axis=0)

    def along(self, jobs, call, **arguments):
        bits = [order[0] for order in self.orders]
        lefts = jobs[0][0]
        if self.plain or lefts[0].shape[1] // len(lefts) % 256:
            results, received, _ = call(**arguments)
            pairs = {
                key: (keep, give if self.plain else self.swap(give, bits[key[1]]))
                for key, (give, keep) in halves_plainly(jobs, bits).items()
            }
        else:
            results, received, pairs = call(**arguments, jobs=jobs, bits=bits)
        bundles = {}
        for (bundle, kind), pair in pairs.items():
            bundles.setdefault(bundle, {})[kind] = pair
        return results, received, bundles

    def middle(self, parts, small, lines, width, collective_id):
        if self.plain:
            sums = self.stacked(small, lines, width)
            return parts, lax.psum(sums, tuple(name for name, _ in self.axes))
        plan, fits = [], True
        for order, arrays in zip(self.orders, parts):
            columns = tuple(own.shape[1] for own, _ in arrays)
            blocks = sum(columns) // 128
            chunk = 512 if blocks >= 48 else 256
            plan.append((cube_rounds(order[1:]), columns, chunk))
            fits &= all(count % chunk == 0 for count in columns)
            fits &= (arrays[0][0].shape[0] >> len(order[1:])) % 16 == 0 and len(order) > 1
        if fits:
            return sum_cube(self.axes, parts, plan, small, lines, width, collective_id)
        sums = [
            [self.rounds(order[1:], own, other) for own, other in arrays]
            for order, arrays in zip(self.orders, parts)
        ]
        small = self.stacked(small, lines, width)
        return sums, sum_and_share(None, self.axes, small, [], collective_id)[0]

    def stacked(self, small, lines, width):
        rows = [
            jnp.pad(array[row], (0, width - array.shape[1]))
            for array, picked in zip(small, lines)
            for row in picked
        ]
        return eight_lines(*rows)

    def rounds(self, bits, own, other):
        total = (own.astype(jnp.float32) + other.astype(jnp.float32)).astype(jnp.bfloat16)
        for bit in bits:
            count = total.shape[0] // 2
            given = lax.dynamic_slice_in_dim(total, (1 - self.upper(bit)) * count, count, axis=0)
            mine = lax.dynamic_slice_in_dim(total, self.upper(bit) * count, count, axis=0)
            other = self.swap(given, bit)
            total = (mine.astype(jnp.float32) + other.astype(jnp.float32)).astype(jnp.bfloat16)
        for bit in reversed(bits):
            total = self.in_order(bit, total, self.swap(total, bit))
        return total

    def finish(self, bundle):
        if self.plain:
            return {kind: (self.orders[kind][0], *pair) for kind, pair in bundle.items()}
        return {
            kind: (self.orders[kind][0], total, self.swap(total, self.orders[kind][0]))
            for kind, total in bundle.items()
        }

    def join(self, *parts):
        if self.plain:
            return jnp.concatenate(
                [
                    lax.psum(
                        self.in_order(*halves)[:, first : first + columns].astype(jnp.float32),
                        "dp",
                    )
                    for halves, first, columns in parts
                ],
                axis=1,
            )
        return join([(*halves, first, columns) for halves, first, columns in parts])


class Flow:
    def __init__(self, sources, held, in_sems, results, staged, out_sems, chunks):
        self.sources, self.held, self.in_sems = sources, held, in_sems
        self.results, self.staged, self.out_sems = results, staged, out_sems
        self.chunks = chunks
        self.sent, self.shared = [], []

    def copy_in(self, index, part):
        width = self.chunks[index]
        columns = pl.ds(part * width, width)
        first = sum(
            source.shape[1] // chunk for source, chunk in zip(self.sources[:index], self.chunks)
        )
        return pltpu.make_async_copy(
            self.sources[index].at[:, columns],
            self.held[index].at[:, columns],
            self.in_sems.at[first + part],
        )

    def start(self, order):
        for index, part in order:
            self.copy_in(index, part).start()

    def pulls(self, held, outs, sems, small):
        self.pull_held, self.pull_outs, self.pull_sems, self.pull_small = held, outs, sems, small
        self.pull_slots, self.pulled = {}, []

    def push(self, order):
        me = lax.axis_index("fsdp")
        for own, places in self.pull_small:
            for step, peer in enumerate(self.peers):
                self.push_one(("small", id(places)), 0, step, peer, own, places[step])
        for index, part in order:
            if index in self.pull_held:
                columns = pl.ds(part * self.chunks[index], self.chunks[index])
                for step, peer in enumerate(self.peers):
                    target = self.pull_held[index][step].at[:, columns]
                    source = self.sources[index].at[:, columns]
                    self.push_one(index, part, step, peer, source, target)

    def carry(self, sources, modes, outs, sems):
        for index, (source, mode) in enumerate(zip(sources, modes)):
            for step, peer in enumerate(self.peers):
                given = source
                if mode == "columns":
                    width = source.shape[1] // self.size
                    given = source.at[:, pl.ds(pl.multiple_of(peer * width, width), width)]
                copy = pltpu.make_async_remote_copy(
                    src_ref=given,
                    dst_ref=outs[index][step],
                    send_sem=sems[0].at[index, step],
                    recv_sem=sems[1].at[index, step],
                    device_id={"fsdp": peer},
                    device_id_type=pl.DeviceIdType.MESH,
                )
                copy.start()
                self.shared.append(copy)

    def push_one(self, index, part, step, peer, source, target):
        send_sems, recv_sems, _ = self.pull_sems
        slot = len(self.pull_slots)
        copy = pltpu.make_async_remote_copy(
            src_ref=source,
            dst_ref=target,
            send_sem=send_sems.at[slot],
            recv_sem=recv_sems.at[slot],
            device_id={"fsdp": peer},
            device_id_type=pl.DeviceIdType.MESH,
        )
        self.pull_slots[index, part, step] = (slot, copy)
        copy.start()

    def take_small(self, places):
        for step in range(len(self.peers)):
            self.pull_slots[("small", id(places)), 0, step][1].wait_recv()
        return places

    def take_all(self, index, part=0):
        blocks = [self.take(index, part)]
        width = self.chunks[index]
        columns = pl.ds(part * width, width)
        for step in range(len(self.peers)):
            slot, copy = self.pull_slots[index, part, step]
            copy.wait_recv()
            block = self.pull_held[index][step].at[:, columns]
            blocks.append(block)
            if not self.pull_outs:
                continue
            out = pltpu.make_async_copy(
                block, self.pull_outs[index][step].at[:, columns], self.pull_sems[2].at[slot]
            )
            out.start()
            self.pulled.append(out)
        return blocks

    def held_all(self, index, part):
        columns = pl.ds(part * self.chunks[index], self.chunks[index])
        return [block.at[:, columns] for block in [self.held[index], *self.pull_held[index]]]

    def take(self, index, part=0):
        self.copy_in(index, part).wait()
        width = self.chunks[index]
        return self.held[index].at[:, pl.ds(part * width, width)]

    def put(self, index, columns=None):
        columns = slice(None) if columns is None else columns
        copy = pltpu.make_async_copy(
            self.staged[index].at[:, columns],
            self.results[index].at[:, columns],
            self.out_sems.at[len(self.sent)],
        )
        copy.start()
        self.sent.append(copy)

    def greet(self, shares, outs, sems, size):
        me = lax.axis_index("fsdp")
        self.shares, self.share_outs, self.share_sems, self.size = shares, outs, sems, size
        self.peers = [lax.rem(me + size - step, size) for step in range(1, size)]

    def share(self, index):
        place = list(self.shares).index(index)
        send_sems, recv_sems = self.share_sems
        for step, peer in enumerate(self.peers):
            source = self.staged[index]
            if self.shares[index] == "columns":
                width = source.shape[1] // self.size
                source = source.at[:, pl.ds(pl.multiple_of(peer * width, width), width)]
            copy = pltpu.make_async_remote_copy(
                src_ref=source,
                dst_ref=self.share_outs[place][step],
                send_sem=send_sems.at[place, step],
                recv_sem=recv_sems.at[place, step],
                device_id={"fsdp": peer},
                device_id_type=pl.DeviceIdType.MESH,
            )
            copy.start()
            self.shared.append(copy)

    def finish(self):
        for copy in self.sent + self.shared + self.pulled:
            copy.wait()
        for _, copy in self.pull_slots.values():
            copy.wait_send()


class Grads:
    AHEAD = 6

    def __init__(self, plan, lefts, rights, outs, lefts_held, scratch):
        self.steps, self.bits, self.count, self.tile = plan
        self.lefts, self.rights, self.outs, self.lefts_held = lefts, rights, outs, lefts_held
        self.rights_held, self.staged, *sems = scratch
        self.left_sems, self.right_sems, self.out_sems, self.send_sems, self.recv_sems = sems
        self.frames, self.rows = rights[0][0].shape[0], self.staged.shape[0]
        self.half = self.rows // 2
        self.me = lax.axis_index("dp")

    def partners(self):
        bits = sorted({self.bits[step[3][1]] for step in self.steps})
        return [{"dp": self.me + bit * (1 - 2 * lax.rem(self.me // bit, 2))} for bit in bits]

    def left_in(self, group, place):
        source = self.lefts[group][place]
        return pltpu.make_async_copy(
            source.at[:, own_columns(self.count, 0, self.rows)] if place == 0 else source,
            self.lefts_held[group].at[pl.ds(place * self.frames, self.frames)],
            self.left_sems.at[group, place],
        )

    def right_in(self, index, place):
        _, right, first, _, _ = self.steps[index]
        return pltpu.make_async_copy(
            self.rights[right][place].at[:, pl.ds(first, self.tile)],
            self.rights_held.at[index % self.AHEAD, pl.ds(place * self.frames, self.frames)],
            self.right_sems.at[index, place],
        )

    def halves_out(self, index):
        _, _, _, key, start = self.steps[index]
        bit = self.bits[key[1]]
        upper = lax.rem(self.me // bit, 2)
        source, columns = [
            self.staged.at[
                pl.ds(pl.multiple_of(part * self.half, self.half), self.half),
                pl.ds(index * self.tile, self.tile),
            ]
            for part in (1 - upper, upper)
        ], pl.ds(start, self.tile)
        keep, recv = self.outs[key]
        return (
            pltpu.make_async_remote_copy(
                src_ref=source[0],
                dst_ref=recv.at[:, columns],
                send_sem=self.send_sems.at[index],
                recv_sem=self.recv_sems.at[index],
                device_id={"dp": self.me + bit * (1 - 2 * upper)},
                device_id_type=pl.DeviceIdType.MESH,
            ),
            pltpu.make_async_copy(source[1], keep.at[:, columns], self.out_sems.at[index]),
        )

    def begin(self):
        loaded = set()
        for index in range(min(self.AHEAD, len(self.steps))):
            self.load(index, loaded)
        self.loaded = loaded

    def load(self, index, loaded):
        group = self.steps[index][0]
        for place in range(self.count):
            if group not in loaded:
                self.left_in(group, place).start()
            self.right_in(index, place).start()
        loaded.add(group)

    def run(self, then):
        waited = set()
        for index, step in enumerate(self.steps):
            for place in range(self.count):
                if step[0] not in waited:
                    self.left_in(step[0], place).wait()
                self.right_in(index, place).wait()
            waited.add(step[0])
            right = self.rights_held[index % self.AHEAD]
            product = dot_down(self.lefts_held[step[0]][...], right)
            self.staged[:, pl.ds(index * self.tile, self.tile)] = product.astype(jnp.bfloat16)
            for copy in self.halves_out(index):
                copy.start()
            if index + self.AHEAD < len(self.steps):
                self.load(index + self.AHEAD, self.loaded)
            if index == max(len(self.steps) - self.AHEAD - 1, 0):
                then()

    def finish(self):
        for index in range(len(self.steps)):
            for copy in self.halves_out(index):
                copy.wait()


def gradient_plan(jobs, tile, spread):
    lefts, rights, steps, totals = [], [], [], {}
    for job_lefts, job_rights, first, columns, key in jobs:
        for known, group in ((lefts, job_lefts), (rights, job_rights)):
            if not any(group is other for other in known):
                known.append(group)
        left = [group is job_lefts for group in lefts].index(True)
        right = [group is job_rights for group in rights].index(True)
        for start in range(0, columns, tile):
            steps.append((left, right, first + start, key, totals.setdefault(key, 0)))
            totals[key] += tile
    turns = {key: 0 for key in totals}
    ranks = []
    for step in steps:
        turns[step[3]] += 1
        ranks.append((turns[step[3]] - 0.5) / (totals[step[3]] // tile))
    if spread:
        steps = [steps[k] for k in sorted(range(len(steps)), key=lambda k: ranks[k])]
    return lefts, rights, steps, totals


def fused(
    body,
    small,
    large,
    results,
    order=None,
    scratch=(),
    shares=None,
    size=1,
    collective_id=None,
    jobs=(),
    bits=(),
    pulls=(),
    small_pulls=(),
    carried=(),
    pulls_stay=False,
    spread=False,
):
    shares = {} if shares is None or size == 1 else shares
    chunks = [width for _, width in large]
    parts = [array.shape[1] // width for array, width in large]
    if order is None:
        order = [(index, part) for index, count in enumerate(parts) for part in range(count)]
    share_shapes = [
        (shape if mode == "all" else (shape[0], shape[1] // size), dtype)
        for (shape, dtype), mode in ((results[index], mode) for index, mode in shares.items())
        for _ in range(size - 1)
    ]
    pulls = list(pulls) if size > 1 else []
    pull_shapes = [
        (large[index][0].shape, large[index][0].dtype) for index in pulls for _ in range(size - 1)
    ]
    carried = list(carried) if size > 1 else []
    carry_shapes = [
        (array.shape if mode == "all" else (array.shape[0], array.shape[1] // size), array.dtype)
        for array, mode in carried
        for _ in range(size - 1)
    ]
    pull_count = (sum(parts[index] for index in pulls) + len(small_pulls)) * (size - 1)
    tile = 512
    lefts, rights, steps, totals = gradient_plan(jobs, tile, spread)
    flat = [array for group in lefts + rights for array in group]
    half_shapes, grad_scratch = [], []
    if jobs:
        count, frames = len(lefts[0]), lefts[0][0].shape[0]
        rows = lefts[0][0].shape[1] // count
        half_shapes = [
            ((rows // 2, columns), jnp.bfloat16) for columns in totals.values() for _ in range(2)
        ]
        grad_scratch = [pltpu.VMEM((count * frames, rows), jnp.bfloat16) for _ in lefts] + [
            pltpu.VMEM((Grads.AHEAD, count * frames, tile), jnp.bfloat16),
            pltpu.VMEM((rows, len(steps) * tile), jnp.bfloat16),
            pltpu.SemaphoreType.DMA((len(lefts), count)),
            pltpu.SemaphoreType.DMA((len(steps), count)),
        ] + [pltpu.SemaphoreType.DMA((len(steps),))] * 3

    def kernel(*refs):
        refs = list(refs)

        def pick(count):
            picked = refs[:count]
            del refs[:count]
            return picked

        small_refs, sources = pick(len(small)), pick(len(large))
        left_refs, right_refs = [pick(len(group)) for group in lefts], [
            pick(len(group)) for group in rights
        ]
        carry_refs = pick(len(carried))
        outs = pick(len(results))
        share_outs = [pick(size - 1) for _ in shares]
        half_outs = {key: pick(2) for key in totals}
        pull_outs = {} if pulls_stay else {index: pick(size - 1) for index in pulls}
        carry_outs = [pick(size - 1) for _ in carried]
        held, staged, rest = pick(len(large)), pick(len(results)), pick(len(scratch))
        in_sems, out_sems = pick(2)
        share_sems = pick(2) if shares else []
        pull_held = {index: pick(size - 1) for index in pulls}
        pull_small = [(small_refs[index], pick(size - 1)) for index in small_pulls]
        pull_sems = pick(3) if pull_count else []
        carry_sems = pick(2) if carried else []
        flow = Flow(sources, held, in_sems, outs, staged, out_sems, chunks)
        greeted = []
        if jobs:
            plan = (steps, bits, len(lefts[0]), tile)
            grads = Grads(plan, left_refs, right_refs, half_outs, pick(len(lefts)), refs)
            grads.begin()
            greeted = grads.partners()
        flow.greet(shares, share_outs, share_sems, size)
        flow.pulls(pull_held, pull_outs, pull_sems, pull_small)
        if pull_count:
            flow.start(order)
        if shares or pull_count or carried:
            greeted += [{"fsdp": peer} for peer in flow.peers]
        if greeted:
            barrier = pltpu.get_barrier_semaphore()
            for device in greeted:
                pl.semaphore_signal(
                    barrier, inc=1, device_id=device, device_id_type=pl.DeviceIdType.MESH
                )
            pl.semaphore_wait(barrier, len(greeted))
        if carried:
            modes = [mode for _, mode in carried]
            flow.carry(carry_refs, modes, carry_outs, carry_sems)
        if jobs:
            grads.run(functools.partial(flow.start, order))
        elif pull_count:
            flow.push(order)
        else:
            flow.start(order)
        if body is not None:
            body(flow, small_refs, rest)
        flow.finish()
        if jobs:
            grads.finish()

    semaphores = [
        pltpu.SemaphoreType.DMA((max(sum(parts), 1),)),
        pltpu.SemaphoreType.DMA((64,)),
    ]
    params = dict(vmem_limit_bytes=60 * 2**20)
    if shares:
        semaphores += [pltpu.SemaphoreType.DMA((len(shares), size - 1))] * 2
    pull_scratch = []
    if pull_count:
        pull_scratch = [pltpu.VMEM(shape, dtype) for shape, dtype in pull_shapes] + [
            pltpu.VMEM(small[index].shape, small[index].dtype)
            for index in small_pulls
            for _ in range(size - 1)
        ]
        pull_scratch += [pltpu.SemaphoreType.DMA((pull_count,))] * 3
    if carried:
        pull_scratch += [pltpu.SemaphoreType.DMA((len(carried), size - 1))] * 2
    if shares or jobs or pull_count or carried:
        params.update(collective_id=collective_id, has_side_effects=True)
    pull_results = [] if pulls_stay else pull_shapes
    shapes = results + share_shapes + half_shapes + pull_results + carry_shapes
    out = pl.pallas_call(
        kernel,
        out_shape=[jax.ShapeDtypeStruct(shape, dtype) for shape, dtype in shapes],
        in_specs=[
            pl.BlockSpec(memory_space=pltpu.SMEM if array.dtype == jnp.int32 else pltpu.VMEM)
            for array in small
        ]
        + [pl.BlockSpec(memory_space=pl.ANY)] * (len(large) + len(flat) + len(carried)),
        out_specs=[pl.BlockSpec(memory_space=pl.ANY)] * len(shapes),
        scratch_shapes=[pltpu.VMEM(array.shape, array.dtype) for array, _ in large]
        + [pltpu.VMEM(shape, dtype) for shape, dtype in results]
        + list(scratch)
        + semaphores
        + pull_scratch
        + grad_scratch,
        compiler_params=pltpu.CompilerParams(**params),
    )(*small, *[array for array, _ in large], *flat, *[array for array, _ in carried])
    others = out[len(results) : len(results) + len(share_shapes)]
    received = [others[k * (size - 1) : (k + 1) * (size - 1)] for k in range(len(shares))]
    halves = out[len(results) + len(share_shapes) :]
    others = out[len(shapes) - len(pull_results) - len(carry_shapes) :]
    received += [
        others[k : k + size - 1] for k in range(0, len(others), max(size - 1, 1)) if size > 1
    ]
    return (
        out[: len(results)],
        received or [[] for _ in range(16)],
        {key: (halves[2 * k], halves[2 * k + 1]) for k, key in enumerate(totals)},
    )


def dot(left, right):
    return jnp.dot(left, right, preferred_element_type=jnp.float32)


def dot_across(left, right):
    return lax.dot_general(left, right, ACROSS_DIMS, preferred_element_type=jnp.float32)


def dot_down(left, right):
    return lax.dot_general(left, right, DOWN_DIMS, preferred_element_type=jnp.float32)


def own_columns(size, place, width):
    owner = lax.rem(lax.axis_index("fsdp") + place, size)
    return pl.ds(pl.multiple_of(owner * width, width), width)


def times_blocks(values_ref, blocks):
    total = None
    for place, block in enumerate(blocks):
        columns = own_columns(len(blocks), place, block.shape[0])
        part = dot(values_ref[:, columns], block[...])
        total = part if total is None else total + part
    return total


def add_back(total_ref, values, blocks, scale=None):
    for place, block in enumerate(blocks):
        columns = own_columns(len(blocks), place, block.shape[0])
        part = dot_across(values, block[...])
        total_ref[:, columns] += part if scale is None else scale * part


def centred(values):
    centre = values - jnp.mean(values, axis=-1, keepdims=True)
    spread = jnp.mean(centre * centre, axis=-1, keepdims=True)
    scale = lax.rsqrt(spread + EPSILON)
    return centre * scale, scale


BIAS_LINES = (6, 7, 9, 10, 8, 11)
TAP_LINE = 12


def gain_line(lines_ref, norm):
    return lines_ref[norm : norm + 1, :]


def bias_line(lines_ref, norm):
    return lines_ref[BIAS_LINES[norm] : BIAS_LINES[norm] + 1, :]


def tap_line(lines_ref, tap):
    return lines_ref[TAP_LINE + tap : TAP_LINE + tap + 1, :]


def norm_low(values, lines_ref, norm):
    hat, _ = centred(values)
    return (hat * gain_line(lines_ref, norm) + bias_line(lines_ref, norm)).astype(jnp.bfloat16)


def norm_grad(grad, values, gain_row):
    hat, scale = centred(values)
    inner = grad * gain_row
    first = jnp.mean(inner, axis=-1, keepdims=True)
    second = jnp.mean(inner * hat, axis=-1, keepdims=True)
    return (
        (inner - first - hat * second) * scale,
        jnp.sum(grad * hat, axis=0, keepdims=True),
        jnp.sum(grad, axis=0, keepdims=True),
    )


def put_rows(ref, *lines):
    for place, line in enumerate(lines):
        ref[pl.ds(place, 1), :] = line
    ref[pl.ds(len(lines), ref.shape[0] - len(lines)), :] = jnp.zeros(
        (ref.shape[0] - len(lines), ref.shape[1]), ref.dtype
    )


def segment_of(lengths_ref, places):
    ends = lengths_ref[0, 0]
    segment = (places >= ends).astype(jnp.int32)
    for index in range(1, lengths_ref.shape[1]):
        ends = ends + lengths_ref[0, index]
        segment += (places >= ends).astype(jnp.int32)
    return segment


def frame_marks(lengths_ref, frames, taps=0):
    places = lax.broadcasted_iota(jnp.int32, (frames, 1), 0)
    segment = segment_of(lengths_ref, places)
    valid = (segment < lengths_ref.shape[1]).astype(jnp.float32)
    marks = []
    for tap in range(taps):
        moved = places + (tap - taps // 2)
        same = (segment_of(lengths_ref, moved) == segment) & (moved >= 0) & (moved < frames)
        marks.append(same.astype(jnp.float32))
    return valid, marks


def same_segment(lengths_ref, frames):
    down = segment_of(lengths_ref, lax.broadcasted_iota(jnp.int32, (frames, 1), 0))
    across = segment_of(lengths_ref, lax.broadcasted_iota(jnp.int32, (1, frames), 1))
    return down == across


TILE = 1024


def feed_forward(w_in, w_out, flow, normed_ref, hidden, slope_ref, y_ref):
    inner = slope_ref.shape[1]
    for part in range(inner // TILE):
        columns = pl.ds(part * TILE, TILE)
        before = times_blocks(normed_ref, w_in(part))
        gate = jax.nn.sigmoid(before)
        value = (before * gate).astype(jnp.bfloat16)
        flow.staged[hidden][:, columns] = value
        flow.put(hidden, columns)
        slope_ref[:, columns] = (gate * (1.0 + before * (1.0 - gate))).astype(jnp.bfloat16)
        add_back(y_ref, value, w_out(part), 0.5)


def feed_forward_back(blocks_in, blocks_out, low_ref, slope_ref, flow, result, normed_ref):
    inner = slope_ref.shape[1]
    normed_ref[...] = jnp.zeros_like(normed_ref)
    for part in range(inner // TILE):
        columns = pl.ds(part * TILE, TILE)
        grad = times_blocks(low_ref, blocks_out(part)) * slope_ref[:, columns].astype(jnp.float32)
        grad = grad.astype(jnp.bfloat16)
        flow.staged[result][:, columns] = grad
        flow.put(result, columns)
        add_back(normed_ref, grad, blocks_in(part))


def head_scores(query, key, bias_row, same, scale):
    frames = query.shape[0]
    spread = jnp.broadcast_to(bias_row, (frames, bias_row.shape[1]))
    relative = pltpu.roll(spread, 0, 1, stride=1, stride_axis=0)[:, :frames]
    return jnp.where(same, dot_across(query, key) * scale + relative, MASKED)


def softmax_rows(scores):
    powers = jnp.exp(scores - jnp.max(scores, axis=-1, keepdims=True))
    return powers / jnp.sum(powers, axis=-1, keepdims=True)


def split(items, count):
    items = list(items)
    return [items[k : k + count] for k in range(0, len(items), count)]


def front(
    x, own_lines, own_bias, lengths, heads, taps, weights, size, collective_id
):
    frames, width = x.shape
    inner = weights[0].shape[1]
    head = width // heads
    small = [own_lines, own_bias, lengths]
    large = [(x, width)]
    large += [(block, TILE) for block in weights[:2]] + [(block, width) for block in weights[2:]]
    order = [(0, 0)]
    order += [(index, part) for part in range(inner // TILE) for index in (1, 2)]
    order += [(3, part) for part in range(3)] + [(4, 0), (5, 1), (5, 0)]
    low, full = jnp.bfloat16, jnp.float32
    results = [
        ((frames, width), low),
        ((frames, inner), low),
        ((frames, inner), low),
        ((frames, width), full),
        ((frames, width), low),
        ((frames, width), low),
        ((frames, width), low),
        ((frames, width), low),
        ((frames, width), low),
        ((frames, width), full),
        ((frames, width), low),
        ((frames, width), full),
        ((frames, width), full),
        ((frames, width), full),
        ((8, width), full),
        ((own_lines.shape[0], width), full),
        ((-(-heads // 8) * 8, own_bias.shape[1]), full),
    ]

    def body(flow, small_refs, _):
        own_lines_ref, own_bias_ref, lengths_ref = small_refs
        valid, marks = frame_marks(lengths_ref, frames, taps)
        (
            normed_one,
            hidden,
            slope,
            x1,
            normed_attn,
            query_ref,
            key_ref,
            value_ref,
            context,
            x2,
            normed_conv,
            gated_ref,
            gate_ref,
            mixed_ref,
            sums_ref,
            lines_ref,
            bias_ref,
        ) = flow.staged
        small_places = [places for _, places in flow.pull_small]
        blocks = [own_lines_ref] + (flow.take_small(small_places[0]) if size > 1 else [])
        for place, block in enumerate(blocks):
            lines_ref[:, own_columns(size, place, block.shape[1])] = block[...]
        flow.put(15)
        blocks = [own_bias_ref] + (flow.take_small(small_places[1]) if size > 1 else [])
        for place, block in enumerate(blocks):
            owner = lax.rem(lax.axis_index("fsdp") + place, size)
            for row in range(heads // size):
                bias_ref[pl.ds(owner * (heads // size) + row, 1), :] = block[row : row + 1, :]
        flow.put(16)
        values = flow.take(0)[...].astype(jnp.float32)
        normed_one[...] = norm_low(values, lines_ref, 0)
        flow.put(0)
        x1[...] = values
        feed_forward(
            lambda part: flow.take_all(1, part),
            lambda part: flow.take_all(2, part),
            flow,
            normed_one,
            1,
            slope,
            x1,
        )
        flow.put(2)
        flow.put(3)

        normed_attn[...] = norm_low(x1[...], lines_ref, 1)
        flow.put(4)
        for part, ref in enumerate((query_ref, key_ref, value_ref)):
            ref[...] = times_blocks(normed_attn, flow.take_all(3, part)).astype(jnp.bfloat16)
            flow.put(5 + part)
        same = same_segment(lengths_ref, frames)
        for place in range(heads):
            columns = slice(place * head, (place + 1) * head)
            scores = head_scores(
                query_ref[:, columns],
                key_ref[:, columns],
                bias_ref[place : place + 1, :],
                same,
                head**-0.5,
            )
            attend = softmax_rows(scores).astype(jnp.bfloat16)
            context[:, columns] = dot(attend, value_ref[:, columns]).astype(jnp.bfloat16)
        flow.put(8)
        x2[...] = x1[...] + times_blocks(context, flow.take_all(4))
        flow.put(9)

        normed_conv[...] = norm_low(x2[...], lines_ref, 2)
        flow.put(10)
        gate = jax.nn.sigmoid(times_blocks(normed_conv, flow.take_all(5, 1)))
        gate_ref[...] = gate
        flow.put(12)
        gated_ref[...] = times_blocks(normed_conv, flow.take_all(5, 0)) * gate
        flow.put(11)
        mixed = jnp.zeros((frames, width), jnp.float32)
        for tap in range(taps):
            offset = tap - taps // 2
            gated = gated_ref[...]
            moved = gated if offset == 0 else pltpu.roll(gated, -offset % frames, 0)
            mixed += tap_line(lines_ref, tap) * (moved * marks[tap])
        mixed_ref[...] = mixed
        flow.put(13)
        weighted = valid * mixed
        put_rows(
            sums_ref,
            jnp.sum(weighted, axis=0, keepdims=True),
            jnp.sum(weighted * mixed, axis=0, keepdims=True),
            jnp.broadcast_to(jnp.sum(valid, axis=0, keepdims=True), (1, width)),
        )
        flow.put(14)

    results, pulled, _ = fused(
        body,
        small,
        large,
        results,
        order,
        size=size,
        collective_id=collective_id,
        pulls=range(1, 6),
        small_pulls=(0, 1),
    )
    return results, [[own, *others] for own, others in zip(weights, pulled)]


def batch_stats(totals_ref):
    count = totals_ref[2:3, :]
    mean = totals_ref[0:1, :] / count
    rstd = lax.rsqrt(totals_ref[1:2, :] / count - mean * mean + EPSILON)
    return count, mean, rstd


def turn(x, mixed, totals, cotangent, lengths, lines, w_conv, w_in, w_out, size, collective_id):
    frames, width = x.shape
    inner = w_in.shape[1]
    small = [totals, lengths, lines]
    large = [(mixed, width), (x, width), (w_conv, width), (w_in, TILE), (w_out, TILE)]
    large += [(cotangent, width)]
    order = [(0, 0), (1, 0), (2, 0)]
    order += [(index, part) for part in range(inner // TILE) for index in (3, 4)]
    order += [(5, 0)]
    low, full = jnp.bfloat16, jnp.float32
    results = [
        ((frames, width), low),
        ((frames, width), low),
        ((frames, inner), low),
        ((frames, width), low),
        ((frames, width), low),
        ((frames, inner), low),
        ((frames, width), low),
        ((frames, width), full),
        ((frames, width), full),
        ((8, width), full),
        ((8, width), full),
        ((8, width), full),
    ]
    scratch = [
        pltpu.VMEM((frames, inner), low),
        pltpu.VMEM((frames, width), full),
        pltpu.VMEM((frames, width), full),
        pltpu.VMEM((frames, width), full),
    ]

    def body(flow, small_refs, rest):
        totals_ref, lengths_ref, lines_ref = small_refs
        valid, _ = frame_marks(lengths_ref, frames)
        slope, x3, x4, normed_grad = rest
        (
            swish,
            normed,
            hidden,
            out_ref,
            low_two,
            before,
            low_conv,
            grad_ref,
            hat_grad,
            sums_final,
            sums_two,
            sums_batch,
        ) = flow.staged
        _, mean, rstd = batch_stats(totals_ref)
        mixed_ref = flow.take(0)
        z = (mixed_ref[...] - mean) * rstd * gain_line(lines_ref, 5) + bias_line(lines_ref, 5)
        swish[...] = (z * jax.nn.sigmoid(z)).astype(jnp.bfloat16)
        flow.put(0)
        x2_ref = flow.take(1)
        conv_blocks = flow.take_all(2)
        x3[...] = x2_ref[...] + times_blocks(swish, conv_blocks)
        normed[...] = norm_low(x3[...], lines_ref, 3)
        flow.put(1)
        x4[...] = x3[...]
        feed_forward(
            functools.partial(flow.take_all, 3),
            functools.partial(flow.take_all, 4),
            flow,
            normed,
            2,
            slope,
            x4,
        )

        gain_row = gain_line(lines_ref, 4)
        hat, _ = centred(x4[...])
        out_ref[...] = (valid * (hat * gain_row + bias_line(lines_ref, 4))).astype(jnp.bfloat16)
        flow.put(3)
        grad = valid * flow.take(len(large) - 1)[...].astype(jnp.float32)
        grad_values, grad_gain, grad_bias = norm_grad(grad, x4[...], gain_row)
        grad_ref[...] = grad_values
        low_two[...] = (0.5 * grad_values).astype(jnp.bfloat16)
        flow.put(4)
        put_rows(sums_final, grad_gain, grad_bias)
        flow.put(9)

        feed_forward_back(
            functools.partial(flow.held_all, 3),
            functools.partial(flow.held_all, 4),
            low_two,
            slope,
            flow,
            5,
            normed_grad,
        )
        branch, grad_gain, grad_bias = norm_grad(
            normed_grad[...], x3[...], gain_line(lines_ref, 3)
        )
        total = grad_ref[...] + branch
        grad_ref[...] = total
        flow.put(7)
        low_conv[...] = total.astype(jnp.bfloat16)
        flow.put(6)
        put_rows(sums_two, grad_gain, grad_bias)
        flow.put(10)

        for place, block in enumerate(conv_blocks):
            columns = own_columns(size, place, block.shape[0])
            hat_grad[:, columns] = dot_across(low_conv[...], block[...])
        hat = (mixed_ref[...] - mean) * rstd
        gain_row = gain_line(lines_ref, 5)
        z = hat * gain_row + bias_line(lines_ref, 5)
        gate = jax.nn.sigmoid(z)
        grad_z = hat_grad[...] * gate * (1.0 + z * (1.0 - gate))
        grad_hat = grad_z * gain_row
        hat_grad[...] = grad_hat
        flow.put(8)
        put_rows(
            sums_batch,
            jnp.sum(grad_hat, axis=0, keepdims=True),
            jnp.sum(grad_hat * hat, axis=0, keepdims=True),
            jnp.sum(grad_z * hat, axis=0, keepdims=True),
            jnp.sum(grad_z, axis=0, keepdims=True),
        )
        flow.put(11)

    return fused(
        body,
        small,
        large,
        results,
        order,
        scratch,
        size=size,
        collective_id=collective_id,
        pulls=(2, 3, 4),
        pulls_stay=True,
    )[0]


def back_front(
    hat_grad,
    gated,
    gate,
    mixed,
    totals,
    back,
    grad,
    x2,
    x1,
    lines,
    bias_table,
    lengths,
    taps,
    packed,
    w_conv,
    w_out,
    w_qkv,
    collective_id,
    **jobs,
):
    frames, width = x1.shape
    count = len(w_conv)
    heads = bias_table.shape[0]
    head = width // heads
    flip = (
        jnp.arange(frames)[:, None] + jnp.arange(frames)[None, :] == frames - 1
    ).astype(jnp.bfloat16)
    small = [totals, back, lengths, lines, bias_table, flip]
    large = [(array, width) for array in (hat_grad, mixed, gated, gate)]
    large += [(block, width) for block in w_conv]
    large += [(array, width) for array in (x2, grad)]
    large += [(block, width) for block in w_out]
    large += [(array, width) for array in packed]
    large += [(block, width) for block in w_qkv]
    large += [(x1, width)]
    conv = list(range(4, 4 + count))
    place_x2 = 4 + count
    out = list(range(place_x2 + 2, place_x2 + 2 + count))
    place_packed = out[-1] + 1
    qkv = list(range(place_packed + 3, place_packed + 3 + count))
    order = None
    low, full = jnp.bfloat16, jnp.float32
    results = [((frames, width), low)] * 7 + [((frames, width), full)]
    results += [((8, width), full)] * 3 + [(bias_table.shape, full)]
    scratch = [
        pltpu.VMEM((frames, width), full),
        pltpu.VMEM((frames, width), full),
        pltpu.VMEM((frames, width), low),
    ]

    def body(flow, small_refs, rest):
        (
            totals_ref,
            back_ref,
            lengths_ref,
            lines_ref,
            bias_ref,
            flip_ref,
        ) = small_refs
        valid, marks = frame_marks(lengths_ref, frames, taps)
        normed_grad, grad_mixed_ref, grad_context = rest
        one, two, low_attn, *grad_refs = flow.staged[:6]
        low_one, grad_ref, sums_kernel, sums_conv, sums_attn, sums_rel = flow.staged[6:]
        valid_count, mean, rstd = batch_stats(totals_ref)
        grad_var = -0.5 * rstd * rstd * back_ref[1:2, :]
        grad_mean = -rstd * back_ref[0:1, :] - 2.0 * mean * grad_var
        hat_ref, mixed_ref = flow.take(0), flow.take(1)
        grad_mixed_ref[...] = (
            hat_ref[...] * rstd
            + valid * (grad_mean + 2.0 * mixed_ref[...] * grad_var) / valid_count
        )
        gated_ref = flow.take(2)
        normed_grad[...] = jnp.zeros_like(normed_grad)
        kernel_grads = []
        for tap in range(taps):
            offset = tap - taps // 2
            masked = grad_mixed_ref[...] * marks[tap]
            gated = gated_ref[...]
            moved = gated if offset == 0 else pltpu.roll(gated, -offset % frames, 0)
            kernel_grads.append(jnp.sum(masked * moved, axis=0, keepdims=True))
            moved = masked if offset == 0 else pltpu.roll(masked, offset % frames, 0)
            normed_grad[...] += tap_line(lines_ref, tap) * moved
        put_rows(sums_kernel, *kernel_grads)
        flow.put(8)
        gate_now = flow.take(3)[...]
        grad_gated = normed_grad[...]
        one[...] = (grad_gated * gate_now).astype(jnp.bfloat16)
        flow.put(0)
        if count > 1:
            flow.share(0)
        two[...] = (grad_gated * gated_ref[...] * (1.0 - gate_now)).astype(jnp.bfloat16)
        flow.put(1)
        if count > 1:
            flow.share(1)
        normed_grad[...] = jnp.zeros_like(normed_grad)
        for part, ref in enumerate((one, two)):
            add_back(normed_grad, ref[...], [flow.take(index, part) for index in conv])
        branch, grad_gain, grad_bias = norm_grad(
            normed_grad[...], flow.take(place_x2)[...], gain_line(lines_ref, 2)
        )
        total = flow.take(place_x2 + 1)[...] + branch
        grad_ref[...] = total
        low_attn[...] = total.astype(jnp.bfloat16)
        flow.put(2)
        if count > 1:
            flow.share(2)
        put_rows(sums_conv, grad_gain, grad_bias)
        flow.put(9)

        for place, index in enumerate(out):
            block = flow.take(index)
            columns = own_columns(count, place, block.shape[0])
            grad_context[:, columns] = dot_across(low_attn[...], block[...]).astype(jnp.bfloat16)
        packed_refs = [flow.take(place_packed + part) for part in range(3)]
        same = same_segment(lengths_ref, frames)
        scale = head**-0.5
        reach = bias_ref.shape[1]
        for place in range(heads):
            columns = slice(place * head, (place + 1) * head)
            query, key, value = (ref[:, columns] for ref in packed_refs)
            bias_row = bias_ref[place : place + 1, :]
            attend = softmax_rows(head_scores(query, key, bias_row, same, scale))
            context = grad_context[:, columns]
            grad_attend = dot_across(context, value)
            grad_value = dot_down(attend.astype(jnp.bfloat16), context)
            grad_scores = attend * (
                grad_attend - jnp.sum(grad_attend * attend, axis=-1, keepdims=True)
            )
            grad_low = grad_scores.astype(jnp.bfloat16)
            padded = jnp.concatenate(
                [dot(grad_low, flip_ref[...]), jnp.zeros((frames, reach - frames), jnp.float32)],
                axis=1,
            )
            skewed = pltpu.roll(padded, 0, 1, stride=1, stride_axis=0)
            sums_rel[place : place + 1, :] = jnp.sum(skewed, axis=0, keepdims=True)
            grad_query = dot(grad_low, key) * scale
            grad_key = dot_down(grad_low, query) * scale
            for ref, part in zip(grad_refs, (grad_query, grad_key, grad_value)):
                ref[:, columns] = part.astype(jnp.bfloat16)
        flow.put(11)
        normed_grad[...] = jnp.zeros_like(normed_grad)
        for part, ref in enumerate(grad_refs):
            flow.put(3 + part)
            if count > 1:
                flow.share(3 + part)
            add_back(normed_grad, ref[...], [flow.take(index, part) for index in qkv])
        branch, grad_gain, grad_bias = norm_grad(
            normed_grad[...], flow.take(len(large) - 1)[...], gain_line(lines_ref, 1)
        )
        total = grad_ref[...] + branch
        grad_ref[...] = total
        flow.put(7)
        low_one[...] = (0.5 * total).astype(jnp.bfloat16)
        flow.put(6)
        if count > 1:
            flow.share(6)
        put_rows(sums_attn, grad_gain, grad_bias)
        flow.put(10)

    shares = {0: "all", 1: "all", 2: "all", 3: "all", 4: "all", 5: "all", 6: "columns"}
    return fused(
        body, small, large, results, order, scratch, shares, count, collective_id, **jobs
    )


def back_end(low, grad, x, lines, slope, w_in, w_out, collective_id, **jobs):
    frames, width = x.shape
    inner, count = w_in[0].shape[1], len(w_in)
    large = [(low, width)] + [(block, TILE) for block in w_out + w_in]
    large += [(slope, TILE), (x, width), (grad, width)]
    groups = split(range(1, 1 + 2 * count), count)
    place_slope = 1 + 2 * count
    order = [(0, 0)]
    for part in range(inner // TILE):
        order += [(index, part) for index in groups[0]] + [(place_slope, part)]
        order += [(index, part) for index in groups[1]]
    order += [(place_slope + 1, 0), (place_slope + 2, 0)]
    results = [
        ((frames, inner), jnp.bfloat16),
        ((frames, width), jnp.bfloat16),
        ((8, width), jnp.float32),
    ]

    def body(flow, small_refs, rest):
        (lines_ref,), (normed_grad,) = small_refs, rest
        before, out_ref, sums_ref = flow.staged

        def w_out_part(part):
            blocks = [flow.take(index, part) for index in groups[0]]
            flow.take(place_slope, part)
            return blocks

        def w_in_part(part):
            return [flow.take(index, part) for index in groups[1]]

        feed_forward_back(
            w_in_part, w_out_part, flow.take(0), flow.held[place_slope], flow, 0, normed_grad
        )
        if count > 1:
            flow.share(0)
        values = flow.take(place_slope + 1)[...].astype(jnp.float32)
        branch, grad_gain, grad_bias = norm_grad(normed_grad[...], values, gain_line(lines_ref, 0))
        out_ref[...] = (flow.take(place_slope + 2)[...] + branch).astype(jnp.bfloat16)
        flow.put(1)
        put_rows(sums_ref, grad_gain, grad_bias)
        flow.put(2)

    scratch = [pltpu.VMEM((frames, width), jnp.float32)]
    shares = {0: "all"}
    return fused(
        body, [lines], large, results, order, scratch, shares, count, collective_id, **jobs
    )


def halves_plainly(jobs, bits):
    products = {}
    for lefts, rights, first, columns, key in jobs:
        rows = lefts[0].shape[1] // len(lefts)
        own = lax.dynamic_slice_in_dim(lefts[0], lax.axis_index("fsdp") * rows, rows, axis=1)
        left = jnp.concatenate([own, *lefts[1:]])
        right = jnp.concatenate(rights)[:, first : first + columns]
        products.setdefault(key, []).append(dot_down(left, right).astype(jnp.bfloat16))
    halves = {}
    for key, parts in products.items():
        product = jnp.concatenate(parts, axis=1)
        half = product.shape[0] // 2
        upper = lax.rem(lax.axis_index("dp") // bits[key[1]], 2)
        halves[key] = tuple(
            lax.dynamic_slice_in_dim(product, part * half, half, axis=0)
            for part in (1 - upper, upper)
        )
    return halves


def join_body(bits, counts, *refs):
    step = pl.program_id(0)
    out_ref = refs[-1]
    half = refs[0].shape[0]
    first = 0
    for index, (bit, count) in enumerate(zip(bits, counts)):
        upper = lax.rem(lax.axis_index("dp") // bit, 2)

        @pl.when((step >= first) & (step < first + count))
        def _(index=index, upper=upper):
            for ref, part in zip(refs[2 * index : 2 * index + 2], (upper, 1 - upper)):
                rows = pl.ds(pl.multiple_of(part * half, half), half)
                out_ref[rows, :] = ref[...].astype(jnp.float32)

        first += count


def join(parts, tile=512):
    counts = [columns // tile for _, _, _, _, columns in parts]
    rows = 2 * parts[0][1].shape[0]
    specs, flat, first = [], [], 0
    for (_, mine, other, start, _), count in zip(parts, counts):

        def index(step, first=first, count=count, start=start // tile):
            return (0, start + jnp.clip(step - first, 0, count - 1))

        specs += [pl.BlockSpec((rows // 2, tile), index)] * 2
        flat += [mine, other]
        first += count
    return pl.pallas_call(
        functools.partial(join_body, [part[0] for part in parts], counts),
        grid=(first,),
        out_shape=jax.ShapeDtypeStruct((rows, first * tile), jnp.float32),
        in_specs=specs,
        out_specs=pl.BlockSpec((rows, tile), lambda step: (0, step)),
        compiler_params=pltpu.CompilerParams(vmem_limit_bytes=60 * 2**20),
    )(*flat)


def bias_lines(table, frames):
    heads, middle = table.shape[0], (table.shape[1] - 1) // 2
    half = -(-frames // 64) * 64
    above = jnp.broadcast_to(table[:, -1:], (heads, half - middle - 1))
    below = jnp.broadcast_to(table[:, :1], (heads, half - middle))
    return jnp.concatenate([table[:, middle:], above, below, table[:, :middle]], axis=1)


def bias_lines_back(sums, frames, reach):
    return jnp.concatenate(
        [
            jnp.sum(sums[:, frames - 1 + reach :], axis=1, keepdims=True),
            sums[:, frames - reach : frames - 1 + reach][:, ::-1],
            jnp.sum(sums[:, : frames - reach], axis=1, keepdims=True),
        ],
        axis=1,
    )


def eight_lines(*lines):
    lines = list(lines)
    return jnp.stack(lines + [jnp.zeros_like(lines[0])] * (-len(lines) % 8))


def per_device(
    sizes,
    inputs,
    cotangent,
    lengths,
    ffn1_in,
    ffn1_out,
    attn_qkv,
    attn_out,
    rel_table,
    conv_in,
    depth_kernel,
    conv_out,
    ffn2_in,
    ffn2_out,
    gains,
    biases,
    inner_biases,
):
    dp_size, fsdp_size = sizes
    axes = (("fsdp", fsdp_size), ("dp", dp_size))
    rows = Rows(fsdp_size)
    groups = Groups(axes)
    frames, width = inputs.shape
    taps = depth_kernel.shape[1]

    own_lines = jnp.concatenate([gains, biases, inner_biases, depth_kernel], axis=1)
    own_lines = jnp.pad(own_lines, ((0, 0), (0, -own_lines.shape[1] % 8))).astype(jnp.float32).T
    own_bias = bias_lines(rel_table.astype(jnp.float32), frames)
    own_bias = jnp.pad(own_bias, ((0, -own_bias.shape[0] % 8), (0, 0)))
    heads = rel_table.shape[0] * fsdp_size

    (
        (
            normed_one,
            hidden_one,
            slope_one,
            x1,
            normed_attn,
            *packed,
            context,
            x2,
            normed_conv,
            gated,
            gate,
            mixed,
            sums,
            lines,
            bias_table,
        ),
        (w_ffn1_in, w_ffn1_out, w_qkv, w_attn_out, w_conv_in),
    ) = front(
        inputs,
        own_lines,
        own_bias,
        lengths,
        heads,
        taps,
        (ffn1_in, ffn1_out, attn_qkv, attn_out, conv_in),
        fsdp_size,
        6,
    )
    totals, _ = sum_and_share(rows, axes, sums, [], 0)
    (
        swish,
        normed_two,
        hidden_two,
        layer_out,
        low_two,
        before_two,
        low_conv,
        grad,
        hat_grad,
        sums_final,
        sums_two,
        sums_batch,
    ) = turn(
        x2,
        mixed,
        totals,
        cotangent,
        lengths,
        lines,
        conv_out,
        ffn2_in,
        ffn2_out,
        fsdp_size,
        7,
    )
    arrays = (low_two, normed_two, swish, hidden_two, before_two, low_conv)
    modes = ("columns",) * 3 + ("all",) * 3
    back, shared = sum_and_share(rows, axes, sums_batch, list(zip(arrays, modes)), 1)
    left_low_two, left_normed_two, left_swish, right_hidden_two, right_before_two, right_low_conv = [
        [own, *others] for own, others in zip(arrays, shared)
    ]

    inner = hidden_two.shape[1]
    main, half, rest = inner * 3 // 4, inner * 3 // 8, inner // 4
    jobs = [
        (left_low_two, right_hidden_two, 0, main, (0, 0)),
        (left_normed_two, right_before_two, 0, main, (0, 1)),
        (left_low_two, right_hidden_two, main, rest, (0, 2)),
        (left_swish, right_low_conv, 0, width, (0, 2)),
        (left_normed_two, right_before_two, main, rest, (0, 3)),
    ]
    arrays = (normed_conv, context, normed_attn, normed_one)
    results, shared, bundles = groups.along(
        jobs,
        functools.partial(
            back_front,
            hat_grad,
            gated,
            gate,
            mixed,
            totals,
            back,
            grad,
            x2,
            x1,
            lines,
            bias_table,
            lengths,
            taps,
            packed,
            w_conv_in,
            w_attn_out,
            w_qkv,
            3,
            spread=True,
            carried=[(array, "columns") for array in arrays] + [(hidden_one, "all")],
        ),
    )
    two = bundles[0]
    *back_lefts, low_one, grad, sums_kernel, sums_conv, sums_attn, sums_rel = results
    right_one, right_two, right_low_attn, right_q, right_k, right_v, left_low_one = [
        [own, *others] for own, others in zip((*back_lefts, low_one), shared)
    ]
    left_normed_conv, left_context, left_normed_attn, left_normed_one, right_hidden_one = [
        [own, *others] for own, others in zip((*arrays, hidden_one), shared[7:])
    ]

    jobs = [
        (left_normed_conv, right_one, 0, width, (0, 0)),
        (left_normed_conv, right_two, 0, width, (0, 1)),
        (left_context, right_low_attn, 0, width, (0, 3)),
        (left_normed_attn, right_q, 0, width, (0, 0)),
        (left_normed_attn, right_k, 0, width, (0, 1)),
        (left_normed_attn, right_v, 0, width, (0, 3)),
        (left_low_one, right_hidden_one, 0, half, (1, 0)),
        (left_low_one, right_hidden_one, half, half, (1, 1)),
        (left_low_one, right_hidden_one, main, rest, (1, 2)),
    ]
    (before_one, input_grad, sums_one), shared, bundles = groups.along(
        jobs,
        functools.partial(
            back_end, low_one, grad, inputs, lines, slope_one, w_ffn1_in, w_ffn1_out, 4
        ),
    )
    mid, out = bundles[0], bundles[1]
    right_before_one = [before_one, *shared[0]]

    jobs = [
        (left_normed_one, right_before_one, 0, half, (0, 0)),
        (left_normed_one, right_before_one, half, half, (0, 1)),
        (left_normed_one, right_before_one, main, rest, (0, 3)),
    ]
    _, _, bundles = groups.along(
        jobs, functools.partial(fused, None, [], [], [], collective_id=5, spread=True)
    )
    end = bundles[0]

    bundles = (two, mid, out, end)
    middle, sums = groups.middle(
        [[bundle[kind] for bundle in bundles if kind in bundle] for kind in range(4)],
        (
            sums_one,
            sums_attn,
            sums_conv,
            sums_two,
            sums_final,
            sums_batch,
            sums_kernel,
            sums_rel,
        ),
        [(0, 1)] * 5 + [(2, 3), tuple(range(taps)), tuple(range(heads))],
        width,
        2,
    )
    middle = [iter(arrays) for arrays in middle]
    two, mid, out, end = [
        {kind: next(middle[kind]) for kind in range(4) if kind in bundle} for bundle in bundles
    ]
    two, mid = groups.finish(two), groups.finish(mid)
    sum_ffn2_out = groups.join((two[0], 0, main), (two[2], 0, rest))
    sum_ffn2_in = groups.join((two[1], 0, main), (two[3], 0, rest))
    sum_conv_out = groups.join((two[2], rest, width))
    out, end, sum_ffn2_out, sum_ffn2_in, sum_conv_out = lax.optimization_barrier(
        (out, end, sum_ffn2_out, sum_ffn2_in, sum_conv_out)
    )
    out, end = groups.finish(out), groups.finish(end)
    sum_qkv = groups.join(*[(mid[kind], width, width) for kind in (0, 1, 3)])
    sum_conv_in = groups.join((mid[0], 0, width), (mid[1], 0, width))
    sum_attn_out = groups.join((mid[3], 0, width))
    sum_ffn1_out = groups.join((out[0], 0, half), (out[1], 0, half), (out[2], 0, rest))
    sum_ffn1_in = groups.join((end[0], 0, half), (end[1], 0, half), (end[3], 0, rest))
    own = lax.dynamic_slice_in_dim(sums, rows.me * gains.shape[0], gains.shape[0], axis=1)
    first = 12 + taps
    rel_sum = lax.dynamic_slice_in_dim(
        sums, first + rows.me * rel_table.shape[0], rel_table.shape[0], axis=0
    )
    rel_sum = bias_lines_back(
        rel_sum[:, : sums_rel.shape[1]], frames, (rel_table.shape[1] - 1) // 2
    )
    return (
        layer_out,
        input_grad,
        sum_ffn1_in,
        sum_ffn1_out,
        sum_qkv,
        sum_attn_out,
        rel_sum,
        sum_conv_in,
        own[12:first].T,
        sum_conv_out,
        sum_ffn2_in,
        sum_ffn2_out,
        own[0:12:2].T,
        jnp.stack([own[1], own[3], own[9]], axis=1),
        jnp.stack([own[5], own[7], own[11]], axis=1),
    )


def solution(mesh):
    frame_spec = P(("dp", "fsdp"), None)
    row_spec = P("fsdp", None)
    sizes = (mesh.shape["dp"], mesh.shape["fsdp"])
    return jax.shard_map(
        functools.partial(per_device, sizes),
        mesh=mesh,
        in_specs=(frame_spec,) * 3 + (row_spec,) * 13,
        out_specs=(frame_spec,) * 2 + (row_spec,) * 13,
        check_vma=False,
    )
```

time: 1150 us -> 513 us (0.45)
  waiting for transfers between devices: 670 us -> 48.8 us
  Pallas kernels: 0 us -> 438 us
  matrix products: 176 us -> 0 us
  blocking collectives: 175 us -> 0 us
  other arithmetic: 67.5 us -> 5.05 us
  local copies, waits for them, and re-layouts: 34.6 us -> 6.94 us
  between operations: 18.9 us -> 1.01 us
    psum x1 -> x0, waiting for transfers between devices: 576 us -> none  [reduce_rest(): lax.psum(parts[0].astype(jnp.bfloat16), 'dp').astype(jnp.float32)]
    pallas_call x0 -> x16, Pallas kernels: none -> 438 us  [the longest x1 182 us: sum_cube(): pl.pallas_call(functools.partial(cube_kernel, axes, plan, lines), out_sha...]
    dot_general x32 -> x0, matrix products: 176 us -> none  [the longest x8 56.6 us: weight_grad(): lax.dot_general(left, right, DOWN_DIMS, preferred_element_type=jnp.float32)]
    psum x3 -> x0, blocking collectives: 163 us -> none  [the longest x1 80.6 us: reduce_rest(): lax.psum(parts[2].astype(jnp.bfloat16), 'dp').astype(jnp.float32)]
    reduce_scatter x10 -> x0, waiting for transfers between devices: 60.4 us -> none  [the longest x3 21 us: reduce_pair(): lax.psum_scatter(second_grad.astype(jnp.bfloat16), 'fsdp', scatter_dimens...]
    ppermute x0 -> x13, waiting for transfers between devices: none -> 48.8 us  [swap(): return lax.ppermute(values, 'dp', [(j, j ^ bit) for j in range(self.size)])]
    convert_element_type x19 -> x2, other arithmetic: 40.1 us -> 1.4 us  [the longest x1 0.71 us: back_front(): flip = (jnp.arange(frames)[:, None] + jnp.arange(frames)[None, :] == fram...]
    all_gather x8 -> x0, waiting for transfers between devices: 29.1 us -> none  [the longest x1 11.7 us: per_device(): lax.all_gather(attn_qkv, 'fsdp', axis=0, tiled=True)]
  transfers between devices with their start and end apart: 21 -> 13, of which waited for: 10 -> 4; matrix products, arithmetic and copies ran while one was open for 16% -> 1% of each run, Pallas kernels for 0% -> 8%
where the time goes in v2:
time: 513 us; the launch traced here: 508 us
  Pallas kernels  438 us (85%)
  waiting for transfers between devices  48.8 us (10%)
  starting transfers between devices  8.55 us (2%)
  local copies, waits for them, and re-layouts  6.94 us (1%)
    pallas_call x1, Pallas kernels, sum_cube(): pl.pallas_call(functools.partial(cube_kernel, axes, plan, lines), out_sha...  182 us
    pallas_call x5, Pallas kernels, fused(): pl.pallas_call(kernel, out_shape=[jax.ShapeDtypeStruct(shape, dtype) for...  179 us
    ppermute x13, waiting for transfers between devices, swap(): return lax.ppermute(values, 'dp', [(j, j ^ bit) for j in range(self.size)])  48.8 us
    pallas_call x8, Pallas kernels, join(): pl.pallas_call(functools.partial(join_body, [part[0] for part in parts],...  46.4 us
    pallas_call x2, Pallas kernels, sum_and_share(): pl.pallas_call(functools.partial(pair_kernel, axes, [mode for _, mode in...  30.3 us
  transfers between devices with their start and end apart: 13, of which 4 were waited for; matrix products, arithmetic and copies ran while one was open for 1% of the time, Pallas kernels for 8%

profile of v2, /device:TPU:0, one launch (start us, length us, event | category | flops | bytes accessed | tf_op | source)
XLA Modules:
  0.0 508.1 jit_solution(6983731285673122877)
XLA Ops:
  1.3 0.7 slice.49
  4.5 1.4 convert_bitcast_fusion.refs_0_
  5.9 29.7 %shard_map.271 = (bf16[288,1024]{1,0:T(8,128)(2,1)}, bf16[288,4096]{1,0:T(8,128)(2,1)}, bf16[288,4096]{1,0:T(8,128)(2,1)}, f32[288,1024]{1,0:T(8,128)}, bf16[288...) custom-call(f32[24,512]{1,0:T(8,128)} %convert_bitcast_fusion.refs_0, ...), custom_call_target="tpu_custom_call" | custom-call | tf_op jit(solution)/shard_map/pallas_call | solution.py:1023
  35.5 15.6 %shard_map.272.refs_0_ = f32[8,1024]{1,0:T(8,128)} custom-call(f32[8,1024]{1,0:T(8,128)} %get-tuple-element.133.refs_0_), custom_call_target="tpu_custom_call" | custom-call | tf_op jit(solution)/shard_map/pallas_call | solution.py:149
  51.2 37.7 %shard_map.273 = (bf16[288,1024]{1,0:T(8,128)(2,1)}, bf16[288,1024]{1,0:T(8,128)(2,1)}, bf16[288,4096]{1,0:T(8,128)(2,1)}, bf16[288,1024]{1,0:T(8,128)(2,1)}, bf...) custom-call(f32[8,1024]{1,0:T(8,128)} %shard_map.272.refs_0_, ...), custom_call_target="tpu_custom_call" | custom-call | tf_op jit(solution)/shard_map/pallas_call | solution.py:1023
  88.8 14.7 %shard_map.274 = (f32[8,1024]{1,0:T(8,128)}, bf16[288,512]{1,0:T(8,128)(2,1)}, bf16[288,512]{1,0:T(8,128)(2,1)}, bf16[288,512]{1,0:T(8,128)(2,1)}, bf16[288,4096...) custom-call(f32[8,1024]{1,0:T(8,128)} %get-tuple-element.138.refs_0_.refs_31_, ...), custom_call_target="tpu_custom_call" | custom-call | tf_op jit(solution)/shard_map/pallas_call | solution.py:149
  103.5 42.4 %shard_map.275 = (bf16[288,1024]{1,0:T(8,128)(2,1)}, bf16[288,1024]{1,0:T(8,128)(2,1)}, bf16[288,1024]{1,0:T(8,128)(2,1)}, bf16[288,1024]{1,0:T(8,128)(2,1)}, bf...) custom-call(f32[8,1024]{1,0:T(8,128)} %shard_map.272.refs_0_, ...), custom_call_target="tpu_custom_call" | custom-call | tf_op jit(solution)/shard_map/pallas_call | solution.py:1023
  145.9 47.7 %shard_map.276 = (bf16[288,4096]{1,0:T(8,128)(2,1)}, bf16[288,1024]{1,0:T(8,128)(2,1)}, f32[8,1024]{1,0:T(8,128)}, bf16[288,4096]{1,0:T(8,128)(2,1)}, bf16[256,2...) custom-call(f32[24,1024]{1,0:T(8,128)} %get-tuple-element.134.refs_2, ...), custom_call_target="tpu_custom_call" | custom-call | tf_op jit(solution)/shard_map/pallas_call | solution.py:1023
  193.6 22.1 %shard_map.277 = (bf16[256,1536]{1,0:T(8,128)(2,1)}, bf16[256,1536]{1,0:T(8,128)(2,1)}, bf16[256,1536]{1,0:T(8,128)(2,1)}, bf16[256,1536]{1,0:T(8,128)(2,1)}, bf...) custom-call(bf16[288,1024]{1,0:T(8,128)(2,1)} %get-tuple-element.167.refs_37_.refs_0_, ...), custom_call_target="tpu_custom_call" | custom-call | tf_op jit(solution)/shard_map/pallas_call | solution.py:1023
  215.7 181.6 %shard_map.278 = (bf16[256,3072]{1,0:T(8,128)(2,1)}, bf16[256,2048]{1,0:T(8,128)(2,1)}, bf16[256,1536]{1,0:T(8,128)(2,1)}, bf16[256,1536]{1,0:T(8,128)(2,1)}, bf...) custom-call(bf16[256,3072]{1,0:T(8,128)(2,1)} %get-tuple-element.192, ...), custom_call_target="tpu_custom_call" | custom-call | tf_op jit(solution)/shard_map/pallas_call | solution.py:500
  397.8 1.4 collective-permute-start.2
  399.2 0.9 collective-permute-start.10
  400.1 1.4 collective-permute-start.11
  401.5 18.6 %collective-permute-done.1.refs_3_.refs_1_ = bf16[256,2048]{1,0:T(8,128)(2,1)S(1)} collective-permute-done((bf16[256,2048]{1,0:T(8,128)(2,1)}, bf16[256,2048]{1,0:T(8,128)(2,1)S(1)}, u32[]{:S(2)}, u32[]{:S(2)}) %collective-permute-start.1) | collective-permute-done | bytes 1048608 | tf_op jit(solution)/shard_map/ppermute | solution.py:537
  420.1 1.0 copy-done.3
  421.1 14.0 %collective-permute-done.refs_1_ = bf16[256,3072]{1,0:T(8,128)(2,1)} collective-permute-done((bf16[256,3072]{1,0:T(8,128)(2,1)}, bf16[256,3072]{1,0:T(8,128)(2,1)}, u32[]{:S(2)}, u32[]{:S(2)}) %collective-permute-start) | collective-permute-done | bytes 1572896 | tf_op jit(solution)/shard_map/ppermute | solution.py:537
  435.1 2.4 shard_map.281
  437.5 7.6 %shard_map.279 = f32[512,4096]{1,0:T(8,128)} custom-call(bf16[256,3072]{1,0:T(8,128)(2,1)} %get-tuple-element.234.refs_0_, bf16[256,3072]{1,0:T(8,128)(2,1)} %collective-permute-done.refs_1_, bf16[256,2048]{1,0:T(8,128)(2,1)} %get-tuple-element.235.refs_2_.refs_0_, bf16[256,2048]{1,0:T(8,128)(2,1)} %copy-done.3), custom_call_target="tpu_custom_call" | custom-call | tf_op jit(solution)/shard_map/pallas_call | solution.py:1755
  445.1 6.2 %collective-permute-done.3.refs_3_ = bf16[256,1024]{1,0:T(8,128)(2,1)S(1)} collective-permute-done((bf16[256,1024]{1,0:T(8,128)(2,1)}, bf16[256,1024]{1,0:T(8,128)(2,1)S(1)}, u32[]{:S(2)}, u32[]{:S(2)}) %collective-permute-start.3) | collective-permute-done | bytes 524320 | tf_op jit(solution)/shard_map/ppermute | solution.py:537
  451.3 0.8 copy-done.6
  452.0 7.6 %shard_map.280 = f32[512,4096]{1,0:T(8,128)} custom-call(bf16[256,3072]{1,0:T(8,128)(2,1)} %get-tuple-element.236.refs_0_, bf16[256,3072]{1,0:T(8,128)(2,1)} %collective-permute-done.2.refs_1_, bf16[256,1024]{1,0:T(8,128)(2,1)} %get-tuple-element.237.refs_2_, bf16[256,1024]{1,0:T(8,128)(2,1)} %copy-done.6), custom_call_target="tpu_custom_call" | custom-call | tf_op jit(solution)/shard_map/pallas_call | solution.py:1755
  459.9 1.7 collective-permute-start.7
  461.6 1.0 collective-permute-start.8
  462.5 1.0 collective-permute-start.4
  464.7 9.9 %collective-permute-done.9.refs_5_ = bf16[256,1024]{1,0:T(8,128)(2,1)} collective-permute-done((bf16[256,1024]{1,0:T(8,128)(2,1)}, bf16[256,1024]{1,0:T(8,128)(2,1)}, u32[]{:S(2)}, u32[]{:S(2)}) %collective-permute-start.9) | collective-permute-done | bytes 524320 | tf_op jit(solution)/shard_map/ppermute | solution.py:537
  477.4 2.4 shard_map.285
  479.8 4.5 shard_map.286
  484.3 6.2 %shard_map.284 = f32[512,3072]{1,0:T(8,128)} custom-call(bf16[256,2048]{1,0:T(8,128)(2,1)} %get-tuple-element.244.refs_0_, bf16[256,2048]{1,0:T(8,128)(2,1)} %copy-done.1, bf16[256,2048]{1,0:T(8,128)(2,1)} %get-tuple-element.245.refs_2_, bf16[256,2048]{1,0:T(8,128)(2,1)} %copy-done.2, bf16[256,2048]{1,0:T(8,128)(2,1)} %get-tuple-element.246.refs_4_.refs_0_, ...), custom_call_target="tpu_custom_call" | custom-call | tf_op jit(solution)/shard_map/pallas_call | solution.py:1755
  490.5 7.8 %shard_map.283 = f32[512,4096]{1,0:T(8,128)} custom-call(bf16[256,1536]{1,0:T(8,128)(2,1)} %get-tuple-element.241.refs_0_, bf16[256,1536]{1,0:T(8,128)(2,1)} %collective-permute-done.7.refs_1_, bf16[256,1536]{1,0:T(8,128)(2,1)} %get-tuple-element.242.refs_2_, bf16[256,1536]{1,0:T(8,128)(2,1)} %collective-permute-done.8.refs_3_, ...), custom_call_target="tpu_custom_call" | custom-call | tf_op jit(solution)/shard_map/pallas_call | solution.py:1755
  498.4 7.8 %shard_map.282 = f32[512,4096]{1,0:T(8,128)} custom-call(bf16[256,1536]{1,0:T(8,128)(2,1)} %get-tuple-element.238.refs_0_, bf16[256,1536]{1,0:T(8,128)(2,1)} %collective-permute-done.4.refs_1_, bf16[256,1536]{1,0:T(8,128)(2,1)} %get-tuple-element.239.refs_2_, bf16[256,1536]{1,0:T(8,128)(2,1)} %collective-permute-done.5.refs_3_, ...), custom_call_target="tpu_custom_call" | custom-call | tf_op jit(solution)/shard_map/pallas_call | solution.py:1755
  506.2 0.8 copy.37
  507.0 0.8 copy.38
  (49 shorter events, 7.8 us)
Async XLA Ops:
  397.3 37.7 %collective-permute-start = (bf16[256,3072]{1,0:T(8,128)(2,1)}, bf16[256,3072]{1,0:T(8,128)(2,1)}, u32[]{:S(2)}, u32[]{:S(2)}) collective-permute-start(bf16[256,3072]{1,0:T(8,128)(2,1)} %get-tuple-element.234.refs_0_), channel_id=1, source_target_pairs={{0,2},{2,0},{4,6},{6,4},{8,10},{10,8},{12,14},{14,12},{16,18},{18,... | collective-permute-start | bytes 4718600 | tf_op jit(solution)/shard_map/ppermute | solution.py:537
  397.8 22.2 %collective-permute-start.1 = (bf16[256,2048]{1,0:T(8,128)(2,1)}, bf16[256,2048]{1,0:T(8,128)(2,1)S(1)}, u32[]{:S(2)}, u32[]{:S(2)}) collective-permute-start(bf16[256,2048]{1,0:T(8,128)(2,1)} %get-tuple-element.235.refs_2_.refs_0_), channel_id=1, source_target_pairs={{0,8},{2,10},{4,12},{6,14},{8,0},{10,2},{12,4},{14,6},{16,24},{18,... | collective-permute-start | bytes 3145736 | tf_op jit(solution)/shard_map/ppermute | solution.py:537
  397.8 53.4 %collective-permute-start.2 = (bf16[256,3072]{1,0:T(8,128)(2,1)}, bf16[256,3072]{1,0:T(8,128)(2,1)}, u32[]{:S(2)}, u32[]{:S(2)}) collective-permute-start(bf16[256,3072]{1,0:T(8,128)(2,1)} %get-tuple-element.236.refs_0_), channel_id=1, source_target_pairs={{0,4},{2,6},{4,0},{6,2},{8,12},{10,14},{12,8},{14,10},{16,20},{18,... | collective-permute-start | bytes 4718600 | tf_op jit(solution)/shard_map/ppermute | solution.py:537
  399.2 62.4 %collective-permute-start.10 = (bf16[256,2048]{1,0:T(8,128)(2,1)}, bf16[256,2048]{1,0:T(8,128)(2,1)S(1)}, u32[]{:S(2)}, u32[]{:S(2)}) collective-permute-start(bf16[256,2048]{1,0:T(8,128)(2,1)} %get-tuple-element.244.refs_0_), channel_id=1, source_target_pairs={{0,2},{2,0},{4,6},{6,4},{8,10},{10,8},{12,14},{14,12},{16,18},{18,... | collective-permute-start | bytes 3145736 | tf_op jit(solution)/shard_map/ppermute | solution.py:537
  400.1 62.5 %collective-permute-start.11 = (bf16[256,2048]{1,0:T(8,128)(2,1)}, bf16[256,2048]{1,0:T(8,128)(2,1)S(1)}, u32[]{:S(2)}, u32[]{:S(2)}) collective-permute-start(bf16[256,2048]{1,0:T(8,128)(2,1)} %get-tuple-element.245.refs_2_), channel_id=1, source_target_pairs={{0,4},{2,6},{4,0},{6,2},{8,12},{10,14},{12,8},{14,10},{16,20},{18,... | collective-permute-start | bytes 3145736 | tf_op jit(solution)/shard_map/ppermute | solution.py:537
  420.1 1.0 copy-start.3
  421.1 42.5 %collective-permute-start.12 = (bf16[256,2048]{1,0:T(8,128)(2,1)}, bf16[256,2048]{1,0:T(8,128)(2,1)S(1)}, u32[]{:S(2)}, u32[]{:S(2)}) collective-permute-start(bf16[256,2048]{1,0:T(8,128)(2,1)} %get-tuple-element.246.refs_4_.refs_0_), channel_id=1, source_target_pairs={{0,8},{2,10},{4,12},{6,14},{8,0},{10,2},{12,4},{14,6},{16,24},{18,... | collective-permute-start | bytes 3145736 | tf_op jit(solution)/shard_map/ppermute | solution.py:537
  435.1 16.2 %collective-permute-start.3 = (bf16[256,1024]{1,0:T(8,128)(2,1)}, bf16[256,1024]{1,0:T(8,128)(2,1)S(1)}, u32[]{:S(2)}, u32[]{:S(2)}) collective-permute-start(bf16[256,1024]{1,0:T(8,128)(2,1)} %get-tuple-element.237.refs_2_), channel_id=1, source_target_pairs={{0,8},{2,10},{4,12},{6,14},{8,0},{10,2},{12,4},{14,6},{16,24},{18,... | collective-permute-start | bytes 1572872 | tf_op jit(solution)/shard_map/ppermute | solution.py:537
  445.1 18.9 %copy-start.7 = (f32[32,1024]{1,0:T(8,128)S(1)}, f32[32,1024]{1,0:T(8,128)}, u32[]{:S(2)}) copy-start(f32[32,1024]{1,0:T(8,128)} %get-tuple-element.247) | copy-start | bytes 393220
  451.3 0.8 copy-start.6
  459.6 15.0 %collective-permute-start.9 = (bf16[256,1024]{1,0:T(8,128)(2,1)}, bf16[256,1024]{1,0:T(8,128)(2,1)}, u32[]{:S(2)}, u32[]{:S(2)}) collective-permute-start(bf16[256,1024]{1,0:T(8,128)(2,1)} %get-tuple-element.243.refs_4_), channel_id=1, source_target_pairs={{0,8},{2,10},{4,12},{6,14},{8,0},{10,2},{12,4},{14,6},{16,24},{18,... | collective-permute-start | bytes 1572872 | tf_op jit(solution)/shard_map/ppermute | solution.py:537
  459.9 30.6 %collective-permute-start.7 = (bf16[256,1536]{1,0:T(8,128)(2,1)}, bf16[256,1536]{1,0:T(8,128)(2,1)}, u32[]{:S(2)}, u32[]{:S(2)}) collective-permute-start(bf16[256,1536]{1,0:T(8,128)(2,1)} %get-tuple-element.241.refs_0_), channel_id=1, source_target_pairs={{0,2},{2,0},{4,6},{6,4},{8,10},{10,8},{12,14},{14,12},{16,18},{18,... | collective-permute-start | bytes 2359304 | tf_op jit(solution)/shard_map/ppermute | solution.py:537
  461.6 18.2 %copy-start.1 = (bf16[256,2048]{1,0:T(8,128)(2,1)}, bf16[256,2048]{1,0:T(8,128)(2,1)S(1)}, u32[]{:S(2)}) copy-start(bf16[256,2048]{1,0:T(8,128)(2,1)S(1)} %collective-permute-done.10.refs_1_) | copy-start | bytes 3145732
  461.6 29.0 %collective-permute-start.8 = (bf16[256,1536]{1,0:T(8,128)(2,1)}, bf16[256,1536]{1,0:T(8,128)(2,1)}, u32[]{:S(2)}, u32[]{:S(2)}) collective-permute-start(bf16[256,1536]{1,0:T(8,128)(2,1)} %get-tuple-element.242.refs_2_), channel_id=1, source_target_pairs={{0,4},{2,6},{4,0},{6,2},{8,12},{10,14},{12,8},{14,10},{16,20},{18,... | collective-permute-start | bytes 2359304 | tf_op jit(solution)/shard_map/ppermute | solution.py:537
  462.5 17.3 %copy-start.2 = (bf16[256,2048]{1,0:T(8,128)(2,1)}, bf16[256,2048]{1,0:T(8,128)(2,1)S(1)}, u32[]{:S(2)}) copy-start(bf16[256,2048]{1,0:T(8,128)(2,1)S(1)} %collective-permute-done.11.refs_3_) | copy-start | bytes 3145732
  462.5 35.8 %collective-permute-start.4 = (bf16[256,1536]{1,0:T(8,128)(2,1)}, bf16[256,1536]{1,0:T(8,128)(2,1)}, u32[]{:S(2)}, u32[]{:S(2)}) collective-permute-start(bf16[256,1536]{1,0:T(8,128)(2,1)} %get-tuple-element.238.refs_0_), channel_id=1, source_target_pairs={{0,2},{2,0},{4,6},{6,4},{8,10},{10,8},{12,14},{14,12},{16,18},{18,... | collective-permute-start | bytes 2359304 | tf_op jit(solution)/shard_map/ppermute | solution.py:537
  463.5 13.8 %copy-start = (bf16[256,2048]{1,0:T(8,128)(2,1)}, bf16[256,2048]{1,0:T(8,128)(2,1)S(1)}, u32[]{:S(2)}) copy-start(bf16[256,2048]{1,0:T(8,128)(2,1)S(1)} %collective-permute-done.12.refs_5_.refs_1_) | copy-start | bytes 3145732
  463.5 34.8 %collective-permute-start.5 = (bf16[256,1536]{1,0:T(8,128)(2,1)}, bf16[256,1536]{1,0:T(8,128)(2,1)}, u32[]{:S(2)}, u32[]{:S(2)}) collective-permute-start(bf16[256,1536]{1,0:T(8,128)(2,1)} %get-tuple-element.239.refs_2_), channel_id=1, source_target_pairs={{0,4},{2,6},{4,0},{6,2},{8,12},{10,14},{12,8},{14,10},{16,20},{18,... | collective-permute-start | bytes 2359304 | tf_op jit(solution)/shard_map/ppermute | solution.py:537
  474.6 23.7 %collective-permute-start.6 = (bf16[256,1024]{1,0:T(8,128)(2,1)}, bf16[256,1024]{1,0:T(8,128)(2,1)}, u32[]{:S(2)}, u32[]{:S(2)}) collective-permute-start(bf16[256,1024]{1,0:T(8,128)(2,1)} %get-tuple-element.240.refs_4_), channel_id=1, source_target_pairs={{0,8},{2,10},{4,12},{6,14},{8,0},{10,2},{12,4},{14,6},{16,24},{18,... | collective-permute-start | bytes 1572872 | tf_op jit(solution)/shard_map/ppermute | solution.py:537
  498.3 7.9 %copy-start.4 = (bf16[288,1024]{1,0:T(8,128)(2,1)S(1)}, bf16[288,1024]{1,0:T(8,128)(2,1)}, u32[]{:S(2)}) copy-start(bf16[288,1024]{1,0:T(8,128)(2,1)} %get-tuple-element.276) | copy-start | bytes 1769476
  498.3 8.7 %copy-start.5 = (bf16[288,1024]{1,0:T(8,128)(2,1)S(1)}, bf16[288,1024]{1,0:T(8,128)(2,1)}, u32[]{:S(2)}) copy-start(bf16[288,1024]{1,0:T(8,128)(2,1)} %get-tuple-element.277) | copy-start | bytes 1769476

commit v3 on v2

--- a/solution.py
+++ b/solution.py
@@ -26,21 +26,29 @@
 
 
 def sum_stages(axes):
+    near = [(name, 1 << k) for name, size in axes for k in range(size.bit_length() - 1)]
     stages = []
-    for name, size in axes:
-        bits = [1 << k for k in range(size.bit_length() - 1)]
-        stages += [(name, bits[k : k + 2]) for k in range(0, len(bits), 2)]
+    while near:
+        count = 3 if len(near) in (3, 5) or len(near) > 6 else 2
+        stages.append(near[:count])
+        near = near[count:]
     return stages
 
 
-def stage_partners(name, bits):
-    me = lax.axis_index(name)
-    low, count = bits[0], 2 ** len(bits)
-    place = lax.rem(me // low, count)
-    return place, [{name: me + low * (other - place)} for other in range(count)]
-
-
-def pair_kernel(axes, modes, *refs):
+def stage_partners(bits):
+    uppers = [lax.rem(lax.axis_index(name) // bit, 2) for name, bit in bits]
+    place = sum(upper << k for k, upper in enumerate(uppers))
+    devices = []
+    for other in range(1 << len(bits)):
+        device = {}
+        for k, (name, bit) in enumerate(bits):
+            start = device.get(name, lax.axis_index(name))
+            device[name] = start + bit * (((other >> k) & 1) - uppers[k])
+        devices.append(device)
+    return place, devices
+
+
+def pair_kernel(axes, modes, lines, *refs):
     refs = list(refs)
 
     def pick(count):
@@ -51,9 +59,13 @@
     size = dict(axes)["fsdp"]
     (x_ref,), shared, (o_ref,) = pick(1), pick(len(modes)), pick(1)
     outs = [pick(size - 1) for _ in modes]
-    slots, send_sems, recv_sems, share_send, share_recv = refs
-    stages = [stage_partners(name, bits) for name, bits in sum_stages(axes)]
-    near = len([name for name, _ in sum_stages(axes) if name == "fsdp"])
+    slots, packed, send_sems, recv_sems, share_send, share_recv = refs
+    tiles = x_ref.shape[1] // 128
+
+    def lanes(index):
+        return pl.ds(index // tiles, 1), pl.ds(index % tiles * 128, 128)
+
+    stages = [stage_partners(bits) for bits in sum_stages(axes)]
     me = lax.axis_index("fsdp")
     peers = [{"fsdp": lax.rem(me + size - step, size)} for step in range(1, size)]
     barrier = pltpu.get_barrier_semaphore()
@@ -68,7 +80,7 @@
                 )
 
         greeted += len(devices) - 1
-    if modes and size > 4:
+    if modes and size > 2:
         for peer in peers:
             pl.semaphore_signal(barrier, inc=1, device_id=peer, device_id_type=pl.DeviceIdType.MESH)
         greeted += size - 1
@@ -92,13 +104,14 @@
                     device_id_type=pl.DeviceIdType.MESH,
                 )
             )
-    o_ref[...] = x_ref[...]
-    started = False
+    for index in range(packed.shape[0]):
+        row, columns = lanes(index)
+        packed[pl.ds(index, 1), :] = x_ref[row, columns]
     for stage, (place, devices) in enumerate(stages):
 
         def exchange(other, device, stage=stage, place=place):
             return pltpu.make_async_remote_copy(
-                src_ref=o_ref,
+                src_ref=packed,
                 dst_ref=slots.at[stage, place],
                 send_sem=send_sems.at[stage, other],
                 recv_sem=recv_sems.at[stage, place],
@@ -108,7 +121,7 @@
 
         def arrival(other, device, stage=stage):
             return pltpu.make_async_remote_copy(
-                src_ref=o_ref,
+                src_ref=packed,
                 dst_ref=slots.at[stage, other],
                 send_sem=send_sems.at[stage, other],
                 recv_sem=recv_sems.at[stage, other],
@@ -118,36 +131,41 @@
 
         for other, device in enumerate(devices):
             pl.when(other != place)(exchange(other, device).start)
-        if not started and stage + 1 >= near:
-            started = True
+        if stage == 0:
             for copy in copies:
                 copy.start()
         for other, device in enumerate(devices):
             pl.when(other != place)(arrival(other, device).wait)
-        slots[stage, pl.ds(place, 1)] = o_ref[...][None]
+        slots[stage, pl.ds(place, 1)] = packed[...][None]
         total = slots[stage, 0]
         for other in range(1, len(devices)):
             total += slots[stage, other]
-        o_ref[...] = total
+        packed[...] = total
+    o_ref[...] = jnp.zeros_like(o_ref)
+    for index in range(packed.shape[0]):
+        row, columns = lanes(index)
+        o_ref[row, columns] = packed[pl.ds(index, 1), :]
     for copy in copies:
         copy.wait()
 
 
-def sum_and_share(rows, axes, values, shared, collective_id):
+def sum_and_share(rows, axes, values, lines, shared, collective_id):
     size = dict(axes)["fsdp"]
     stages = len(sum_stages(axes))
     if any(count & (count - 1) for _, count in axes) or stages == 0:
         total = lax.psum(values, tuple(name for name, _ in axes))
+        total = jnp.concatenate([total[:lines], jnp.zeros_like(total[lines:])])
         return total, [
             (rows.all_frames if mode == "all" else rows.all_frames_own_columns)(array)[1:]
             for array, mode in shared
         ]
+    packed = (lines * values.shape[1] // 128, 128)
     shapes = [
         array.shape if mode == "all" else (array.shape[0], array.shape[1] // size)
         for array, mode in shared
     ]
     out = pl.pallas_call(
-        functools.partial(pair_kernel, axes, [mode for _, mode in shared]),
+        functools.partial(pair_kernel, axes, [mode for _, mode in shared], lines),
         out_shape=[jax.ShapeDtypeStruct(values.shape, values.dtype)]
         + [
             jax.ShapeDtypeStruct(shape, array.dtype)
@@ -159,9 +177,10 @@
         out_specs=[pl.BlockSpec(memory_space=pltpu.VMEM)]
         + [pl.BlockSpec(memory_space=pl.ANY)] * (len(shared) * (size - 1)),
         scratch_shapes=[
-            pltpu.VMEM((stages, 4) + values.shape, values.dtype),
-            pltpu.SemaphoreType.DMA((stages, 4)),
-            pltpu.SemaphoreType.DMA((stages, 4)),
+            pltpu.VMEM((stages, 8) + packed, values.dtype),
+            pltpu.VMEM(packed, values.dtype),
+            pltpu.SemaphoreType.DMA((stages, 8)),
+            pltpu.SemaphoreType.DMA((stages, 8)),
             pltpu.SemaphoreType.DMA((max(len(shared), 1), max(size - 1, 1))),
             pltpu.SemaphoreType.DMA((max(len(shared), 1), max(size - 1, 1))),
         ],
@@ -214,10 +233,10 @@
         ]
 
 
-def cube_rounds(bits):
-    if len(bits) > 2 and bits[-1] == 2 * bits[-2]:
-        return tuple(("swap", bit) for bit in bits[:-2]) + (("give", bits[-2]), ("mid", bits[-2]))
-    return tuple(("swap", bit) for bit in bits)
+def cube_rounds(bits, line):
+    swaps = bits[:-2] if line and tuple(bits[-2:]) == line else bits
+    rounds = tuple(("swap", bit) for bit in swaps)
+    return rounds if swaps == bits else rounds + (("give", line[0]), ("mid", line[0]))
 
 
 def cube_kernel(axes, plan, lines, *refs):
@@ -528,10 +547,15 @@
         self.orders = [[1]] * 4
         if first:
             one, two, three = first[0], first[1 % len(first)], first[2 % len(first)]
-            for kind, order in enumerate(
-                ((one, two, three), (two, one, three), (three, one, two), (three, two, one))
-            ):
-                self.orders[kind] = list(dict.fromkeys(order)) + rest
+            orders = (
+                (one, two, three, *rest),
+                (two, one, three, *rest),
+                (three, one, two, *rest),
+                (three, two, one, *rest),
+            )
+            self.orders = [list(dict.fromkeys(order)) for order in orders]
+        self.kinds = range(len(self.orders))
+        self.line = tuple(bits[-2:]) if len(bits) > 3 else ()
 
     def swap(self, values, bit):
         return lax.ppermute(values, "dp", [(j, j ^ bit) for j in range(self.size)])
@@ -548,6 +572,10 @@
         lefts = jobs[0][0]
         if self.plain or lefts[0].shape[1] // len(lefts) % 256:
             results, received, _ = call(**arguments)
+            jobs = [
+                (lefts, [results[rights], *received[0]] if isinstance(rights, int) else rights, *rest)
+                for lefts, rights, *rest in jobs
+            ]
             pairs = {
                 key: (keep, give if self.plain else self.swap(give, bits[key[1]]))
                 for key, (give, keep) in halves_plainly(jobs, bits).items()
@@ -568,7 +596,7 @@
             columns = tuple(own.shape[1] for own, _ in arrays)
             blocks = sum(columns) // 128
             chunk = 512 if blocks >= 48 else 256
-            plan.append((cube_rounds(order[1:]), columns, chunk))
+            plan.append((cube_rounds(order[1:], self.line), columns, chunk))
             fits &= all(count % chunk == 0 for count in columns)
             fits &= (arrays[0][0].shape[0] >> len(order[1:])) % 16 == 0 and len(order) > 1
         if fits:
@@ -578,7 +606,7 @@
             for order, arrays in zip(self.orders, parts)
         ]
         small = self.stacked(small, lines, width)
-        return sums, sum_and_share(None, self.axes, small, [], collective_id)[0]
+        return sums, sum_and_share(None, self.axes, small, small.shape[0], [], collective_id)[0]
 
     def stacked(self, small, lines, width):
         rows = [
@@ -761,6 +789,11 @@
             copy.start()
             self.shared.append(copy)
 
+    def wait_shared(self):
+        for copy in self.shared:
+            copy.wait()
+        self.shared = []
+
     def finish(self):
         for copy in self.sent + self.shared + self.pulled:
             copy.wait()
@@ -776,7 +809,7 @@
         self.lefts, self.rights, self.outs, self.lefts_held = lefts, rights, outs, lefts_held
         self.rights_held, self.staged, *sems = scratch
         self.left_sems, self.right_sems, self.out_sems, self.send_sems, self.recv_sems = sems
-        self.frames, self.rows = rights[0][0].shape[0], self.staged.shape[0]
+        self.frames, self.rows = lefts[0][0].shape[0], self.staged.shape[0]
         self.half = self.rows // 2
         self.me = lax.axis_index("dp")
 
@@ -824,23 +857,23 @@
             pltpu.make_async_copy(source[1], keep.at[:, columns], self.out_sems.at[index]),
         )
 
-    def begin(self):
-        loaded = set()
-        for index in range(min(self.AHEAD, len(self.steps))):
-            self.load(index, loaded)
-        self.loaded = loaded
-
-    def load(self, index, loaded):
+    def begin(self, first, last):
+        self.first, self.last, self.loaded = first, last, set()
+        for index in range(first, min(first + self.AHEAD, last)):
+            self.load(index)
+
+    def load(self, index):
         group = self.steps[index][0]
         for place in range(self.count):
-            if group not in loaded:
+            if group not in self.loaded:
                 self.left_in(group, place).start()
             self.right_in(index, place).start()
-        loaded.add(group)
+        self.loaded.add(group)
 
     def run(self, then):
         waited = set()
-        for index, step in enumerate(self.steps):
+        for index in range(self.first, self.last):
+            step = self.steps[index]
             for place in range(self.count):
                 if step[0] not in waited:
                     self.left_in(step[0], place).wait()
@@ -851,9 +884,9 @@
             self.staged[:, pl.ds(index * self.tile, self.tile)] = product.astype(jnp.bfloat16)
             for copy in self.halves_out(index):
                 copy.start()
-            if index + self.AHEAD < len(self.steps):
-                self.load(index + self.AHEAD, self.loaded)
-            if index == max(len(self.steps) - self.AHEAD - 1, 0):
+            if index + self.AHEAD < self.last:
+                self.load(index + self.AHEAD)
+            if index == max(self.last - self.AHEAD - 1, self.first):
                 then()
 
     def finish(self):
@@ -878,8 +911,9 @@
     for step in steps:
         turns[step[3]] += 1
         ranks.append((turns[step[3]] - 0.5) / (totals[step[3]] // tile))
-    if spread:
-        steps = [steps[k] for k in sorted(range(len(steps)), key=lambda k: ranks[k])]
+    late = [isinstance(rights[step[1]], int) for step in steps]
+    keys = [(late[k], ranks[k] if spread else k) for k in range(len(steps))]
+    steps = [steps[k] for k in sorted(range(len(steps)), key=lambda k: keys[k])]
     return lefts, rights, steps, totals
 
 
@@ -924,7 +958,8 @@
     pull_count = (sum(parts[index] for index in pulls) + len(small_pulls)) * (size - 1)
     tile = 512
     lefts, rights, steps, totals = gradient_plan(jobs, tile, spread)
-    flat = [array for group in lefts + rights for array in group]
+    early = len([step for step in steps if not isinstance(rights[step[1]], int)])
+    flat = [array for group in lefts + rights if not isinstance(group, int) for array in group]
     half_shapes, grad_scratch = [], []
     if jobs:
         count, frames = len(lefts[0]), lefts[0][0].shape[0]
@@ -948,9 +983,8 @@
             return picked
 
         small_refs, sources = pick(len(small)), pick(len(large))
-        left_refs, right_refs = [pick(len(group)) for group in lefts], [
-            pick(len(group)) for group in rights
-        ]
+        left_refs = [pick(len(group)) for group in lefts]
+        right_refs = [group if isinstance(group, int) else pick(len(group)) for group in rights]
         carry_refs = pick(len(carried))
         outs = pick(len(results))
         share_outs = [pick(size - 1) for _ in shares]
@@ -968,8 +1002,12 @@
         greeted = []
         if jobs:
             plan = (steps, bits, len(lefts[0]), tile)
+            for place, group in enumerate(right_refs):
+                if isinstance(group, int):
+                    others = share_outs[list(shares).index(group)] if shares else []
+                    right_refs[place] = [staged[group], *others]
             grads = Grads(plan, left_refs, right_refs, half_outs, pick(len(lefts)), refs)
-            grads.begin()
+            grads.begin(0, early)
             greeted = grads.partners()
         flow.greet(shares, share_outs, share_sems, size)
         flow.pulls(pull_held, pull_outs, pull_sems, pull_small)
@@ -995,6 +1033,10 @@
             flow.start(order)
         if body is not None:
             body(flow, small_refs, rest)
+        if early < len(steps):
+            flow.wait_shared()
+            grads.begin(early, len(steps))
+            grads.run(lambda: None)
         flow.finish()
         if jobs:
             grads.finish()
@@ -1421,6 +1463,9 @@
             slope,
             x4,
         )
+        if size > 1:
+            for index in (2, 1, 0):
+                flow.share(index)
 
         gain_row = gain_line(lines_ref, 4)
         hat, _ = centred(x4[...])
@@ -1431,6 +1476,8 @@
         grad_ref[...] = grad_values
         low_two[...] = (0.5 * grad_values).astype(jnp.bfloat16)
         flow.put(4)
+        if size > 1:
+            flow.share(4)
         put_rows(sums_final, grad_gain, grad_bias)
         flow.put(9)
 
@@ -1443,6 +1490,8 @@
             5,
             normed_grad,
         )
+        if size > 1:
+            flow.share(5)
         branch, grad_gain, grad_bias = norm_grad(
             normed_grad[...], x3[...], gain_line(lines_ref, 3)
         )
@@ -1451,6 +1500,8 @@
         flow.put(7)
         low_conv[...] = total.astype(jnp.bfloat16)
         flow.put(6)
+        if size > 1:
+            flow.share(6)
         put_rows(sums_two, grad_gain, grad_bias)
         flow.put(10)
 
@@ -1481,11 +1532,12 @@
         results,
         order,
         scratch,
+        shares={0: "columns", 1: "columns", 2: "all", 4: "columns", 5: "all", 6: "all"},
         size=size,
         collective_id=collective_id,
         pulls=(2, 3, 4),
         pulls_stay=True,
-    )[0]
+    )[:2]
 
 
 def back_front(
@@ -1848,21 +1900,8 @@
         fsdp_size,
         6,
     )
-    totals, _ = sum_and_share(rows, axes, sums, [], 0)
-    (
-        swish,
-        normed_two,
-        hidden_two,
-        layer_out,
-        low_two,
-        before_two,
-        low_conv,
-        grad,
-        hat_grad,
-        sums_final,
-        sums_two,
-        sums_batch,
-    ) = turn(
+    totals, _ = sum_and_share(rows, axes, sums, 3, [], 0)
+    results, shared = turn(
         x2,
         mixed,
         totals,
@@ -1875,12 +1914,13 @@
         fsdp_size,
         7,
     )
-    arrays = (low_two, normed_two, swish, hidden_two, before_two, low_conv)
-    modes = ("columns",) * 3 + ("all",) * 3
-    back, shared = sum_and_share(rows, axes, sums_batch, list(zip(arrays, modes)), 1)
-    left_low_two, left_normed_two, left_swish, right_hidden_two, right_before_two, right_low_conv = [
+    swish, normed_two, hidden_two, layer_out, low_two, before_two, low_conv = results[:7]
+    grad, hat_grad, sums_final, sums_two, sums_batch = results[7:]
+    arrays = (swish, normed_two, hidden_two, low_two, before_two, low_conv)
+    left_swish, left_normed_two, right_hidden_two, left_low_two, right_before_two, right_low_conv = [
         [own, *others] for own, others in zip(arrays, shared)
     ]
+    back, _ = sum_and_share(rows, axes, sums_batch, 2, [], 1)
 
     inner = hidden_two.shape[1]
     main, half, rest = inner * 3 // 4, inner * 3 // 8, inner // 4
@@ -1937,29 +1977,21 @@
         (left_low_one, right_hidden_one, 0, half, (1, 0)),
         (left_low_one, right_hidden_one, half, half, (1, 1)),
         (left_low_one, right_hidden_one, main, rest, (1, 2)),
+        (left_normed_one, 0, 0, half, (2, 0)),
+        (left_normed_one, 0, half, half, (2, 1)),
+        (left_normed_one, 0, main, rest, (2, 3)),
     ]
-    (before_one, input_grad, sums_one), shared, bundles = groups.along(
+    (_, input_grad, sums_one), _, bundles = groups.along(
         jobs,
         functools.partial(
             back_end, low_one, grad, inputs, lines, slope_one, w_ffn1_in, w_ffn1_out, 4
         ),
     )
-    mid, out = bundles[0], bundles[1]
-    right_before_one = [before_one, *shared[0]]
-
-    jobs = [
-        (left_normed_one, right_before_one, 0, half, (0, 0)),
-        (left_normed_one, right_before_one, half, half, (0, 1)),
-        (left_normed_one, right_before_one, main, rest, (0, 3)),
-    ]
-    _, _, bundles = groups.along(
-        jobs, functools.partial(fused, None, [], [], [], collective_id=5, spread=True)
-    )
-    end = bundles[0]
+    mid, out, end = bundles[0], bundles[1], bundles[2]
 
     bundles = (two, mid, out, end)
     middle, sums = groups.middle(
-        [[bundle[kind] for bundle in bundles if kind in bundle] for kind in range(4)],
+        [[bundle[kind] for bundle in bundles if kind in bundle] for kind in groups.kinds],
         (
             sums_one,
             sums_attn,
@@ -1976,19 +2008,19 @@
     )
     middle = [iter(arrays) for arrays in middle]
     two, mid, out, end = [
-        {kind: next(middle[kind]) for kind in range(4) if kind in bundle} for bundle in bundles
+        {kind: next(middle[kind]) for kind in groups.kinds if kind in bundle} for bundle in bundles
     ]
     two, mid = groups.finish(two), groups.finish(mid)
     sum_ffn2_out = groups.join((two[0], 0, main), (two[2], 0, rest))
     sum_ffn2_in = groups.join((two[1], 0, main), (two[3], 0, rest))
     sum_conv_out = groups.join((two[2], rest, width))
-    out, end, sum_ffn2_out, sum_ffn2_in, sum_conv_out = lax.optimization_barrier(
-        (out, end, sum_ffn2_out, sum_ffn2_in, sum_conv_out)
-    )
-    out, end = groups.finish(out), groups.finish(end)
+    out, sum_ffn2_out, sum_conv_out = lax.optimization_barrier((out, sum_ffn2_out, sum_conv_out))
+    out = groups.finish(out)
     sum_qkv = groups.join(*[(mid[kind], width, width) for kind in (0, 1, 3)])
     sum_conv_in = groups.join((mid[0], 0, width), (mid[1], 0, width))
     sum_attn_out = groups.join((mid[3], 0, width))
+    end, sum_qkv = lax.optimization_barrier((end, sum_qkv))
+    end = groups.finish(end)
     sum_ffn1_out = groups.join((out[0], 0, half), (out[1], 0, half), (out[2], 0, rest))
     sum_ffn1_in = groups.join((end[0], 0, half), (end[1], 0, half), (end[3], 0, rest))
     own = lax.dynamic_slice_in_dim(sums, rows.me * gains.shape[0], gains.shape[0], axis=1)

time: 513 us -> 498 us (0.971)
  Pallas kernels: 438 us -> 427 us
    pallas_call x2, Pallas kernels: 30.3 us -> 24.6 us  [sum_and_share(): pl.pallas_call(functools.partial(pair_kernel, axes, [mode for _, mode in...]
    pallas_call x5 -> x4, Pallas kernels: 179 us -> 177 us  [fused(): pl.pallas_call(kernel, out_shape=[jax.ShapeDtypeStruct(shape, dtype) for...]
  transfers between devices with their start and end apart: 13 -> 13, of which waited for: 4 -> 5; matrix products, arithmetic and copies ran while one was open for 1% -> 1% of each run, Pallas kernels for 8% -> 8%
where the time goes in v3:
time: 498 us; the launch traced here: 494 us
  Pallas kernels  427 us (86%)
  waiting for transfers between devices  44.7 us (9%)
  starting transfers between devices  9.53 us (2%)
  local copies, waits for them, and re-layouts  6.18 us (1%)
  other arithmetic  5.05 us (1%)
    pallas_call x1, Pallas kernels, sum_cube(): pl.pallas_call(functools.partial(cube_kernel, axes, plan, lines), out_sha...  180 us
    pallas_call x4, Pallas kernels, fused(): pl.pallas_call(kernel, out_shape=[jax.ShapeDtypeStruct(shape, dtype) for...  177 us
    pallas_call x8, Pallas kernels, join(): pl.pallas_call(functools.partial(join_body, [part[0] for part in parts],...  46.3 us
    ppermute x13, waiting for transfers between devices, swap(): return lax.ppermute(values, 'dp', [(j, j ^ bit) for j in range(self.size)])  44.7 us
    pallas_call x2, Pallas kernels, sum_and_share(): pl.pallas_call(functools.partial(pair_kernel, axes, [mode for _, mode in...  24.6 us
  transfers between devices with their start and end apart: 13, of which 5 were waited for; matrix products, arithmetic and copies ran while one was open for 1% of the time, Pallas kernels for 8%

profile of v3, /device:TPU:0, one launch (start us, length us, event | category | flops | bytes accessed | tf_op | source)
XLA Modules:
  0.0 493.6 jit_solution(9397193493340703321)
XLA Ops:
  1.3 0.7 slice.49
  2.8 0.7 fusion.refs_5_
  4.5 1.4 convert_bitcast_fusion.refs_0_
  5.9 29.7 %shard_map.271 = (bf16[288,1024]{1,0:T(8,128)(2,1)}, bf16[288,4096]{1,0:T(8,128)(2,1)}, bf16[288,4096]{1,0:T(8,128)(2,1)}, f32[288,1024]{1,0:T(8,128)}, bf16[288...) custom-call(f32[24,512]{1,0:T(8,128)} %convert_bitcast_fusion.refs_0, ...), custom_call_target="tpu_custom_call" | custom-call | tf_op jit(solution)/shard_map/pallas_call | solution.py:1065
  35.6 13.4 %shard_map.272.refs_0_ = f32[8,1024]{1,0:T(8,128)} custom-call(f32[8,1024]{1,0:T(8,128)} %get-tuple-element.130.refs_0_), custom_call_target="tpu_custom_call" | custom-call | tf_op jit(solution)/shard_map/pallas_call | solution.py:167
  49.0 39.9 %shard_map.273 = (bf16[288,1024]{1,0:T(8,128)(2,1)}, bf16[288,1024]{1,0:T(8,128)(2,1)}, bf16[288,4096]{1,0:T(8,128)(2,1)}, bf16[288,1024]{1,0:T(8,128)(2,1)}, bf...) custom-call(f32[8,1024]{1,0:T(8,128)} %shard_map.272.refs_0_, ...), custom_call_target="tpu_custom_call" | custom-call | tf_op jit(solution)/shard_map/pallas_call | solution.py:1065
  88.9 11.2 %shard_map.274.refs_1_ = f32[8,1024]{1,0:T(8,128)} custom-call(f32[8,1024]{1,0:T(8,128)} %get-tuple-element.135.refs_0_.refs_31_), custom_call_target="tpu_custom_call" | custom-call | tf_op jit(solution)/shard_map/pallas_call | solution.py:167
  100.1 41.7 %shard_map.275 = (bf16[288,1024]{1,0:T(8,128)(2,1)}, bf16[288,1024]{1,0:T(8,128)(2,1)}, bf16[288,1024]{1,0:T(8,128)(2,1)}, bf16[288,1024]{1,0:T(8,128)(2,1)}, bf...) custom-call(f32[8,1024]{1,0:T(8,128)} %shard_map.272.refs_0_, ...), custom_call_target="tpu_custom_call" | custom-call | tf_op jit(solution)/shard_map/pallas_call | solution.py:1065
  141.8 65.3 %shard_map.276 = (bf16[288,4096]{1,0:T(8,128)(2,1)}, bf16[288,1024]{1,0:T(8,128)(2,1)}, f32[8,1024]{1,0:T(8,128)}, bf16[288,4096]{1,0:T(8,128)(2,1)}, bf16[256,2...) custom-call(f32[24,1024]{1,0:T(8,128)} %get-tuple-element.131.refs_2, ...), custom_call_target="tpu_custom_call" | custom-call | tf_op jit(solution)/shard_map/pallas_call | solution.py:1065
  207.1 179.6 %shard_map.277 = (bf16[256,3072]{1,0:T(8,128)(2,1)}, bf16[256,2048]{1,0:T(8,128)(2,1)}, bf16[256,1536]{1,0:T(8,128)(2,1)}, bf16[256,1536]{1,0:T(8,128)(2,1)}, bf...) custom-call(bf16[256,3072]{1,0:T(8,128)(2,1)} %get-tuple-element.189, ...), custom_call_target="tpu_custom_call" | custom-call | tf_op jit(solution)/shard_map/pallas_call | solution.py:519
  386.7 1.6 collective-permute-start
  388.8 1.8 collective-permute-start.1
  390.8 22.3 %collective-permute-done.refs_1_ = bf16[256,2048]{1,0:T(8,128)(2,1)S(1)} collective-permute-done((bf16[256,2048]{1,0:T(8,128)(2,1)}, bf16[256,2048]{1,0:T(8,128)(2,1)S(1)}, u32[]{:S(2)}, u32[]{:S(2)}) %collective-permute-start) | collective-permute-done | bytes 1048608 | tf_op jit(solution)/shard_map/ppermute | solution.py:561
  413.1 2.0 collective-permute-done.1.refs_3_
  415.1 1.8 collective-permute-done.2.refs_5_.refs_1_
  416.9 1.0 copy-done
  417.9 6.2 %shard_map.278 = f32[512,3072]{1,0:T(8,128)} custom-call(bf16[256,2048]{1,0:T(8,128)(2,1)} %get-tuple-element.225.refs_0_, bf16[256,2048]{1,0:T(8,128)(2,1)} %copy-done.1, bf16[256,2048]{1,0:T(8,128)(2,1)} %get-tuple-element.226.refs_2_, bf16[256,2048]{1,0:T(8,128)(2,1)} %copy-done.2, bf16[256,2048]{1,0:T(8,128)(2,1)} %get-tuple-element.227.refs_4_.refs_0_, ...), custom_call_target="tpu_custom_call" | custom-call | tf_op jit(solution)/shard_map/pallas_call | solution.py:1807
  424.3 15.2 %collective-permute-done.7.refs_3_.refs_1_ = bf16[256,2048]{1,0:T(8,128)(2,1)} collective-permute-done((bf16[256,2048]{1,0:T(8,128)(2,1)}, bf16[256,2048]{1,0:T(8,128)(2,1)}, u32[]{:S(2)}, u32[]{:S(2)}) %collective-permute-start.7) | collective-permute-done | bytes 1048608 | tf_op jit(solution)/shard_map/ppermute | solution.py:561
  439.5 1.5 collective-permute-start.3
  441.0 2.4 shard_map.281
  443.4 3.4 collective-permute-done.6.refs_1_
  446.9 1.8 collective-permute-start.4
  448.7 7.6 %shard_map.280 = f32[512,4096]{1,0:T(8,128)} custom-call(bf16[256,3072]{1,0:T(8,128)(2,1)} %get-tuple-element.234.refs_0_, bf16[256,3072]{1,0:T(8,128)(2,1)} %collective-permute-done.6.refs_1_, bf16[256,2048]{1,0:T(8,128)(2,1)} %get-tuple-element.235.refs_2_.refs_0_, bf16[256,2048]{1,0:T(8,128)(2,1)} %collective-permute-done.7.refs_3_.refs_1_), custom_call_target="tpu_custom_call" | custom-call | tf_op jit(solution)/shard_map/pallas_call | solution.py:1807
  456.3 1.0 collective-permute-start.8
  457.3 0.8 collective-permute-start.9
  461.5 4.5 shard_map.284
  466.0 2.4 shard_map.283
  468.4 7.6 %shard_map.285 = f32[512,4096]{1,0:T(8,128)} custom-call(bf16[256,3072]{1,0:T(8,128)(2,1)} %get-tuple-element.242.refs_0_, bf16[256,3072]{1,0:T(8,128)(2,1)} %collective-permute-done.11.refs_1_, bf16[256,1024]{1,0:T(8,128)(2,1)} %get-tuple-element.243.refs_2_, bf16[256,1024]{1,0:T(8,128)(2,1)} %collective-permute-done.12.refs_3_), custom_call_target="tpu_custom_call" | custom-call | tf_op jit(solution)/shard_map/pallas_call | solution.py:1807
  476.0 7.8 %shard_map.279 = f32[512,4096]{1,0:T(8,128)} custom-call(bf16[256,1536]{1,0:T(8,128)(2,1)} %get-tuple-element.228.refs_0_, bf16[256,1536]{1,0:T(8,128)(2,1)} %collective-permute-done.3.refs_1_, bf16[256,1536]{1,0:T(8,128)(2,1)} %get-tuple-element.229.refs_2_, bf16[256,1536]{1,0:T(8,128)(2,1)} %collective-permute-done.4.refs_3_, ...), custom_call_target="tpu_custom_call" | custom-call | tf_op jit(solution)/shard_map/pallas_call | solution.py:1807
  483.8 7.8 %shard_map.282 = f32[512,4096]{1,0:T(8,128)} custom-call(bf16[256,1536]{1,0:T(8,128)(2,1)} %get-tuple-element.236.refs_0_, bf16[256,1536]{1,0:T(8,128)(2,1)} %collective-permute-done.8.refs_1_, bf16[256,1536]{1,0:T(8,128)(2,1)} %get-tuple-element.237.refs_2_, bf16[256,1536]{1,0:T(8,128)(2,1)} %collective-permute-done.9.refs_3_, ...), custom_call_target="tpu_custom_call" | custom-call | tf_op jit(solution)/shard_map/pallas_call | solution.py:1807
  491.7 0.8 copy.37
  492.5 0.8 copy.38
  (54 shorter events, 6.7 us)
Async XLA Ops:
  386.7 26.4 %collective-permute-start = (bf16[256,2048]{1,0:T(8,128)(2,1)}, bf16[256,2048]{1,0:T(8,128)(2,1)S(1)}, u32[]{:S(2)}, u32[]{:S(2)}) collective-permute-start(bf16[256,2048]{1,0:T(8,128)(2,1)} %get-tuple-element.225.refs_0_), channel_id=1, source_target_pairs={{0,2},{2,0},{4,6},{6,4},{8,10},{10,8},{12,14},{14,12},{16,18},{18,... | collective-permute-start | bytes 3145736 | tf_op jit(solution)/shard_map/ppermute | solution.py:561
  388.3 58.6 %collective-permute-start.6 = (bf16[256,3072]{1,0:T(8,128)(2,1)}, bf16[256,3072]{1,0:T(8,128)(2,1)}, u32[]{:S(2)}, u32[]{:S(2)}) collective-permute-start(bf16[256,3072]{1,0:T(8,128)(2,1)} %get-tuple-element.234.refs_0_), channel_id=1, source_target_pairs={{0,2},{2,0},{4,6},{6,4},{8,10},{10,8},{12,14},{14,12},{16,18},{18,... | collective-permute-start | bytes 4718600 | tf_op jit(solution)/shard_map/ppermute | solution.py:561
  388.8 26.3 %collective-permute-start.1 = (bf16[256,2048]{1,0:T(8,128)(2,1)}, bf16[256,2048]{1,0:T(8,128)(2,1)S(1)}, u32[]{:S(2)}, u32[]{:S(2)}) collective-permute-start(bf16[256,2048]{1,0:T(8,128)(2,1)} %get-tuple-element.226.refs_2_), channel_id=1, source_target_pairs={{0,4},{2,6},{4,0},{6,2},{8,12},{10,14},{12,8},{14,10},{16,20},{18,... | collective-permute-start | bytes 3145736 | tf_op jit(solution)/shard_map/ppermute | solution.py:561
  390.6 26.3 %collective-permute-start.2 = (bf16[256,2048]{1,0:T(8,128)(2,1)}, bf16[256,2048]{1,0:T(8,128)(2,1)S(1)}, u32[]{:S(2)}, u32[]{:S(2)}) collective-permute-start(bf16[256,2048]{1,0:T(8,128)(2,1)} %get-tuple-element.227.refs_4_.refs_0_), channel_id=1, source_target_pairs={{0,8},{2,10},{4,12},{6,14},{8,0},{10,2},{12,4},{14,6},{16,24},{18,... | collective-permute-start | bytes 3145736 | tf_op jit(solution)/shard_map/ppermute | solution.py:561
  390.6 68.2 %collective-permute-start.11 = (bf16[256,3072]{1,0:T(8,128)(2,1)}, bf16[256,3072]{1,0:T(8,128)(2,1)}, u32[]{:S(2)}, u32[]{:S(2)}) collective-permute-start(bf16[256,3072]{1,0:T(8,128)(2,1)} %get-tuple-element.242.refs_0_), channel_id=1, source_target_pairs={{0,4},{2,6},{4,0},{6,2},{8,12},{10,14},{12,8},{14,10},{16,20},{18,... | collective-permute-start | bytes 4718600 | tf_op jit(solution)/shard_map/ppermute | solution.py:561
  413.1 3.9 copy-start.1
  413.1 26.4 %collective-permute-start.7 = (bf16[256,2048]{1,0:T(8,128)(2,1)}, bf16[256,2048]{1,0:T(8,128)(2,1)}, u32[]{:S(2)}, u32[]{:S(2)}) collective-permute-start(bf16[256,2048]{1,0:T(8,128)(2,1)} %get-tuple-element.235.refs_2_.refs_0_), channel_id=1, source_target_pairs={{0,8},{2,10},{4,12},{6,14},{8,0},{10,2},{12,4},{14,6},{16,24},{18,... | collective-permute-start | bytes 3145736 | tf_op jit(solution)/shard_map/ppermute | solution.py:561
  415.1 1.8 copy-start.2
  415.1 24.4 %copy-start.5 = (bf16[256,1536]{1,0:T(8,128)(2,1)S(1)}, bf16[256,1536]{1,0:T(8,128)(2,1)}, u32[]{:S(2)}) copy-start(bf16[256,1536]{1,0:T(8,128)(2,1)} %get-tuple-element.228.refs_0_) | copy-start | bytes 2359300
  415.1 41.2 %collective-permute-start.12 = (bf16[256,1024]{1,0:T(8,128)(2,1)}, bf16[256,1024]{1,0:T(8,128)(2,1)}, u32[]{:S(2)}, u32[]{:S(2)}) collective-permute-start(bf16[256,1024]{1,0:T(8,128)(2,1)} %get-tuple-element.243.refs_2_), channel_id=1, source_target_pairs={{0,8},{2,10},{4,12},{6,14},{8,0},{10,2},{12,4},{14,6},{16,24},{18,... | collective-permute-start | bytes 1572872 | tf_op jit(solution)/shard_map/ppermute | solution.py:561
  416.9 1.0 copy-start
  424.1 22.8 %copy-start.6 = (bf16[256,1536]{1,0:T(8,128)(2,1)S(1)}, bf16[256,1536]{1,0:T(8,128)(2,1)}, u32[]{:S(2)}) copy-start(bf16[256,1536]{1,0:T(8,128)(2,1)} %get-tuple-element.229.refs_2_) | copy-start | bytes 2359300
  424.1 33.2 %collective-permute-start.5 = (bf16[256,1024]{1,0:T(8,128)(2,1)}, bf16[256,1024]{1,0:T(8,128)(2,1)S(1)}, u32[]{:S(2)}, u32[]{:S(2)}) collective-permute-start(bf16[256,1024]{1,0:T(8,128)(2,1)} %get-tuple-element.230.refs_4_), channel_id=1, source_target_pairs={{0,8},{2,10},{4,12},{6,14},{8,0},{10,2},{12,4},{14,6},{16,24},{18,... | collective-permute-start | bytes 1572872 | tf_op jit(solution)/shard_map/ppermute | solution.py:561
  439.5 36.5 %collective-permute-start.3 = (bf16[256,1536]{1,0:T(8,128)(2,1)S(1)}, bf16[256,1536]{1,0:T(8,128)(2,1)}, u32[]{:S(2)}, u32[]{:S(2)}) collective-permute-start(bf16[256,1536]{1,0:T(8,128)(2,1)S(1)} %copy-done.5), channel_id=1, source_target_pairs={{0,2},{2,0},{4,6},{6,4},{8,10},{10,8},{12,14},{14,12},{16,18},{18,... | collective-permute-start | bytes 2359304 | tf_op jit(solution)/shard_map/ppermute | solution.py:561
  443.4 12.9 %copy-start.3 = (bf16[256,1536]{1,0:T(8,128)(2,1)S(1)}, bf16[256,1536]{1,0:T(8,128)(2,1)}, u32[]{:S(2)}) copy-start(bf16[256,1536]{1,0:T(8,128)(2,1)} %get-tuple-element.236.refs_0_) | copy-start | bytes 2359300
  443.4 13.9 %copy-start.4 = (bf16[256,1536]{1,0:T(8,128)(2,1)S(1)}, bf16[256,1536]{1,0:T(8,128)(2,1)}, u32[]{:S(2)}) copy-start(bf16[256,1536]{1,0:T(8,128)(2,1)} %get-tuple-element.237.refs_2_) | copy-start | bytes 2359300
  443.4 14.7 %copy-start.10 = (f32[32,1024]{1,0:T(8,128)S(1)}, f32[32,1024]{1,0:T(8,128)}, u32[]{:S(2)}) copy-start(f32[32,1024]{1,0:T(8,128)} %get-tuple-element.240) | copy-start | bytes 393220
  446.9 29.2 %collective-permute-start.4 = (bf16[256,1536]{1,0:T(8,128)(2,1)S(1)}, bf16[256,1536]{1,0:T(8,128)(2,1)}, u32[]{:S(2)}, u32[]{:S(2)}) collective-permute-start(bf16[256,1536]{1,0:T(8,128)(2,1)S(1)} %copy-done.6), channel_id=1, source_target_pairs={{0,4},{2,6},{4,0},{6,2},{8,12},{10,14},{12,8},{14,10},{16,20},{18,... | collective-permute-start | bytes 2359304 | tf_op jit(solution)/shard_map/ppermute | solution.py:561
  456.3 27.5 %collective-permute-start.8 = (bf16[256,1536]{1,0:T(8,128)(2,1)S(1)}, bf16[256,1536]{1,0:T(8,128)(2,1)}, u32[]{:S(2)}, u32[]{:S(2)}) collective-permute-start(bf16[256,1536]{1,0:T(8,128)(2,1)S(1)} %copy-done.3), channel_id=1, source_target_pairs={{0,2},{2,0},{4,6},{6,4},{8,10},{10,8},{12,14},{14,12},{16,18},{18,... | collective-permute-start | bytes 2359304 | tf_op jit(solution)/shard_map/ppermute | solution.py:561
  457.3 0.8 copy-start.9
  457.3 26.5 %collective-permute-start.9 = (bf16[256,1536]{1,0:T(8,128)(2,1)S(1)}, bf16[256,1536]{1,0:T(8,128)(2,1)}, u32[]{:S(2)}, u32[]{:S(2)}) collective-permute-start(bf16[256,1536]{1,0:T(8,128)(2,1)S(1)} %copy-done.4), channel_id=1, source_target_pairs={{0,4},{2,6},{4,0},{6,2},{8,12},{10,14},{12,8},{14,10},{16,20},{18,... | collective-permute-start | bytes 2359304 | tf_op jit(solution)/shard_map/ppermute | solution.py:561
  458.8 25.0 %collective-permute-start.10 = (bf16[256,1024]{1,0:T(8,128)(2,1)}, bf16[256,1024]{1,0:T(8,128)(2,1)}, u32[]{:S(2)}, u32[]{:S(2)}) collective-permute-start(bf16[256,1024]{1,0:T(8,128)(2,1)} %get-tuple-element.238.refs_4_), channel_id=1, source_target_pairs={{0,8},{2,10},{4,12},{6,14},{8,0},{10,2},{12,4},{14,6},{16,24},{18,... | collective-permute-start | bytes 1572872 | tf_op jit(solution)/shard_map/ppermute | solution.py:561
  483.8 7.9 %copy-start.7 = (bf16[288,1024]{1,0:T(8,128)(2,1)S(1)}, bf16[288,1024]{1,0:T(8,128)(2,1)}, u32[]{:S(2)}) copy-start(bf16[288,1024]{1,0:T(8,128)(2,1)} %get-tuple-element.270) | copy-start | bytes 1769476
  483.8 8.7 %copy-start.8 = (bf16[288,1024]{1,0:T(8,128)(2,1)S(1)}, bf16[288,1024]{1,0:T(8,128)(2,1)}, u32[]{:S(2)}) copy-start(bf16[288,1024]{1,0:T(8,128)(2,1)} %get-tuple-element.271) | copy-start | bytes 1769476

commit v4 on v3

--- a/solution.py
+++ b/solution.py
@@ -1792,7 +1792,8 @@
         first += count
 
 
-def join(parts, tile=512):
+def join(parts):
+    tile = 512 if any(part[3] % 1024 or part[4] % 1024 for part in parts) else 1024
     counts = [columns // tile for _, _, _, _, columns in parts]
     rows = 2 * parts[0][1].shape[0]
     specs, flat, first = [], [], 0
@@ -2010,16 +2011,16 @@
     two, mid, out, end = [
         {kind: next(middle[kind]) for kind in groups.kinds if kind in bundle} for bundle in bundles
     ]
-    two, mid = groups.finish(two), groups.finish(mid)
+    mid, two = groups.finish(mid), groups.finish(two)
+    sum_qkv = groups.join(*[(mid[kind], width, width) for kind in (0, 1, 3)])
+    sum_conv_in = groups.join((mid[0], 0, width), (mid[1], 0, width))
+    sum_attn_out = groups.join((mid[3], 0, width))
+    out, sum_qkv, sum_conv_in = lax.optimization_barrier((out, sum_qkv, sum_conv_in))
+    out = groups.finish(out)
     sum_ffn2_out = groups.join((two[0], 0, main), (two[2], 0, rest))
     sum_ffn2_in = groups.join((two[1], 0, main), (two[3], 0, rest))
     sum_conv_out = groups.join((two[2], rest, width))
-    out, sum_ffn2_out, sum_conv_out = lax.optimization_barrier((out, sum_ffn2_out, sum_conv_out))
-    out = groups.finish(out)
-    sum_qkv = groups.join(*[(mid[kind], width, width) for kind in (0, 1, 3)])
-    sum_conv_in = groups.join((mid[0], 0, width), (mid[1], 0, width))
-    sum_attn_out = groups.join((mid[3], 0, width))
-    end, sum_qkv = lax.optimization_barrier((end, sum_qkv))
+    end, sum_ffn2_out = lax.optimization_barrier((end, sum_ffn2_out))
     end = groups.finish(end)
     sum_ffn1_out = groups.join((out[0], 0, half), (out[1], 0, half), (out[2], 0, rest))
     sum_ffn1_in = groups.join((end[0], 0, half), (end[1], 0, half), (end[3], 0, rest))

time: 498 us -> 495 us (level)
  Pallas kernels: 427 us -> 422 us
    pallas_call x8, Pallas kernels: 46.3 us -> 41.3 us  [join(): pl.pallas_call(functools.partial(join_body, [part[0] for part in parts],...]
  transfers between devices with their start and end apart: 13 -> 13, of which waited for: 5 -> 5; matrix products, arithmetic and copies ran while one was open for 1% -> 1% of each run, Pallas kernels for 8% -> 7%
where the time goes in v4:
time: 495 us; the launch traced here: 490 us
  Pallas kernels  422 us (85%)
  waiting for transfers between devices  45.5 us (9%)
  starting transfers between devices  9.62 us (2%)
  local copies, waits for them, and re-layouts  7.13 us (1%)
  other arithmetic  5.05 us (1%)
    pallas_call x1, Pallas kernels, sum_cube(): pl.pallas_call(functools.partial(cube_kernel, axes, plan, lines), out_sha...  180 us
    pallas_call x4, Pallas kernels, fused(): pl.pallas_call(kernel, out_shape=[jax.ShapeDtypeStruct(shape, dtype) for...  177 us
    ppermute x13, waiting for transfers between devices, swap(): return lax.ppermute(values, 'dp', [(j, j ^ bit) for j in range(self.size)])  45.5 us
    pallas_call x8, Pallas kernels, join(): pl.pallas_call(functools.partial(join_body, [part[0] for part in parts],...  41.3 us
    pallas_call x2, Pallas kernels, sum_and_share(): pl.pallas_call(functools.partial(pair_kernel, axes, [mode for _, mode in...  24.6 us
  transfers between devices with their start and end apart: 13, of which 5 were waited for; matrix products, arithmetic and copies ran while one was open for 1% of the time, Pallas kernels for 7%

profile of v4, /device:TPU:0, one launch (start us, length us, event | category | flops | bytes accessed | tf_op | source)
XLA Modules:
  0.0 490.3 jit_solution(9636797061122127389)
XLA Ops:
  1.3 0.7 slice.49
  4.5 1.4 convert_bitcast_fusion.refs_0_
  5.9 29.7 %shard_map.271 = (bf16[288,1024]{1,0:T(8,128)(2,1)}, bf16[288,4096]{1,0:T(8,128)(2,1)}, bf16[288,4096]{1,0:T(8,128)(2,1)}, f32[288,1024]{1,0:T(8,128)}, bf16[288...) custom-call(f32[24,512]{1,0:T(8,128)} %convert_bitcast_fusion.refs_0, ...), custom_call_target="tpu_custom_call" | custom-call | tf_op jit(solution)/shard_map/pallas_call | solution.py:1065
  35.6 13.4 %shard_map.272.refs_0_ = f32[8,1024]{1,0:T(8,128)} custom-call(f32[8,1024]{1,0:T(8,128)} %get-tuple-element.130.refs_0_), custom_call_target="tpu_custom_call" | custom-call | tf_op jit(solution)/shard_map/pallas_call | solution.py:167
  49.0 39.9 %shard_map.273 = (bf16[288,1024]{1,0:T(8,128)(2,1)}, bf16[288,1024]{1,0:T(8,128)(2,1)}, bf16[288,4096]{1,0:T(8,128)(2,1)}, bf16[288,1024]{1,0:T(8,128)(2,1)}, bf...) custom-call(f32[8,1024]{1,0:T(8,128)} %shard_map.272.refs_0_, ...), custom_call_target="tpu_custom_call" | custom-call | tf_op jit(solution)/shard_map/pallas_call | solution.py:1065
  88.9 11.2 %shard_map.274.refs_1_ = f32[8,1024]{1,0:T(8,128)} custom-call(f32[8,1024]{1,0:T(8,128)} %get-tuple-element.135.refs_0_.refs_31_), custom_call_target="tpu_custom_call" | custom-call | tf_op jit(solution)/shard_map/pallas_call | solution.py:167
  100.1 41.7 %shard_map.275 = (bf16[288,1024]{1,0:T(8,128)(2,1)}, bf16[288,1024]{1,0:T(8,128)(2,1)}, bf16[288,1024]{1,0:T(8,128)(2,1)}, bf16[288,1024]{1,0:T(8,128)(2,1)}, bf...) custom-call(f32[8,1024]{1,0:T(8,128)} %shard_map.272.refs_0_, ...), custom_call_target="tpu_custom_call" | custom-call | tf_op jit(solution)/shard_map/pallas_call | solution.py:1065
  141.8 65.3 %shard_map.276 = (bf16[288,4096]{1,0:T(8,128)(2,1)}, bf16[288,1024]{1,0:T(8,128)(2,1)}, f32[8,1024]{1,0:T(8,128)}, bf16[288,4096]{1,0:T(8,128)(2,1)}, bf16[256,2...) custom-call(f32[24,1024]{1,0:T(8,128)} %get-tuple-element.131.refs_2, ...), custom_call_target="tpu_custom_call" | custom-call | tf_op jit(solution)/shard_map/pallas_call | solution.py:1065
  207.1 179.6 %shard_map.277 = (bf16[256,3072]{1,0:T(8,128)(2,1)}, bf16[256,2048]{1,0:T(8,128)(2,1)}, bf16[256,1536]{1,0:T(8,128)(2,1)}, bf16[256,1536]{1,0:T(8,128)(2,1)}, bf...) custom-call(bf16[256,3072]{1,0:T(8,128)(2,1)} %get-tuple-element.189, ...), custom_call_target="tpu_custom_call" | custom-call | tf_op jit(solution)/shard_map/pallas_call | solution.py:519
  386.6 1.6 collective-permute-start.5
  388.7 1.8 collective-permute-start.6
  390.8 22.3 %collective-permute-done.5.refs_1_ = bf16[256,2048]{1,0:T(8,128)(2,1)S(1)} collective-permute-done((bf16[256,2048]{1,0:T(8,128)(2,1)}, bf16[256,2048]{1,0:T(8,128)(2,1)S(1)}, u32[]{:S(2)}, u32[]{:S(2)}) %collective-permute-start.5) | collective-permute-done | bytes 1048608 | tf_op jit(solution)/shard_map/ppermute | solution.py:561
  413.0 2.0 collective-permute-done.6.refs_3_
  415.1 1.0 copy-done.2
  416.0 3.7 shard_map.281
  419.7 1.0 copy-done
  420.7 4.8 shard_map.280
  425.5 1.1 collective-permute-start.10
  426.6 12.8 %collective-permute-done.1.refs_3_.refs_1_ = bf16[256,2048]{1,0:T(8,128)(2,1)} collective-permute-done((bf16[256,2048]{1,0:T(8,128)(2,1)}, bf16[256,2048]{1,0:T(8,128)(2,1)}, u32[]{:S(2)}, u32[]{:S(2)}) %collective-permute-start.1) | collective-permute-done | bytes 1048608 | tf_op jit(solution)/shard_map/ppermute | solution.py:561
  439.5 1.5 collective-permute-start.8
  441.0 5.9 %collective-permute-done.refs_1_ = bf16[256,3072]{1,0:T(8,128)(2,1)} collective-permute-done((bf16[256,3072]{1,0:T(8,128)(2,1)}, bf16[256,3072]{1,0:T(8,128)(2,1)}, u32[]{:S(2)}, u32[]{:S(2)}) %collective-permute-start) | collective-permute-done | bytes 1572896 | tf_op jit(solution)/shard_map/ppermute | solution.py:561
  446.8 1.8 collective-permute-start.9
  448.7 5.9 %shard_map.278 = f32[512,4096]{1,0:T(8,128)} custom-call(bf16[256,3072]{1,0:T(8,128)(2,1)} %get-tuple-element.225.refs_0_, bf16[256,3072]{1,0:T(8,128)(2,1)} %collective-permute-done.refs_1_, bf16[256,2048]{1,0:T(8,128)(2,1)} %get-tuple-element.226.refs_2_.refs_0_, bf16[256,2048]{1,0:T(8,128)(2,1)} %collective-permute-done.1.refs_3_.refs_1_), custom_call_target="tpu_custom_call" | custom-call | tf_op jit(solution)/shard_map/pallas_call | solution.py:1808
  454.6 1.0 collective-permute-start.2
  455.6 2.6 collective-permute-done.10.refs_5_
  461.5 2.7 shard_map.284
  464.3 2.7 shard_map.283
  466.9 5.9 %shard_map.285 = f32[512,4096]{1,0:T(8,128)} custom-call(bf16[256,3072]{1,0:T(8,128)(2,1)} %get-tuple-element.242.refs_0_, bf16[256,3072]{1,0:T(8,128)(2,1)} %collective-permute-done.11.refs_1_, bf16[256,1024]{1,0:T(8,128)(2,1)} %get-tuple-element.243.refs_2_, bf16[256,1024]{1,0:T(8,128)(2,1)} %collective-permute-done.12.refs_3_), custom_call_target="tpu_custom_call" | custom-call | tf_op jit(solution)/shard_map/pallas_call | solution.py:1808
  472.8 7.8 %shard_map.282 = f32[512,4096]{1,0:T(8,128)} custom-call(bf16[256,1536]{1,0:T(8,128)(2,1)} %get-tuple-element.236.refs_0_, bf16[256,1536]{1,0:T(8,128)(2,1)} %collective-permute-done.8.refs_1_, bf16[256,1536]{1,0:T(8,128)(2,1)} %get-tuple-element.237.refs_2_, bf16[256,1536]{1,0:T(8,128)(2,1)} %collective-permute-done.9.refs_3_, ...), custom_call_target="tpu_custom_call" | custom-call | tf_op jit(solution)/shard_map/pallas_call | solution.py:1808
  480.6 7.8 %shard_map.279 = f32[512,4096]{1,0:T(8,128)} custom-call(bf16[256,1536]{1,0:T(8,128)(2,1)} %get-tuple-element.227.refs_0_, bf16[256,1536]{1,0:T(8,128)(2,1)} %collective-permute-done.2.refs_1_, bf16[256,1536]{1,0:T(8,128)(2,1)} %get-tuple-element.228.refs_2_, bf16[256,1536]{1,0:T(8,128)(2,1)} %collective-permute-done.3.refs_3_, ...), custom_call_target="tpu_custom_call" | custom-call | tf_op jit(solution)/shard_map/pallas_call | solution.py:1808
  488.5 0.8 copy.37
  489.3 0.8 copy.38
  (54 shorter events, 7.2 us)
Async XLA Ops:
  386.6 26.4 %collective-permute-start.5 = (bf16[256,2048]{1,0:T(8,128)(2,1)}, bf16[256,2048]{1,0:T(8,128)(2,1)S(1)}, u32[]{:S(2)}, u32[]{:S(2)}) collective-permute-start(bf16[256,2048]{1,0:T(8,128)(2,1)} %get-tuple-element.233.refs_0_), channel_id=1, source_target_pairs={{0,2},{2,0},{4,6},{6,4},{8,10},{10,8},{12,14},{14,12},{16,18},{18,... | collective-permute-start | bytes 3145736 | tf_op jit(solution)/shard_map/ppermute | solution.py:561
  388.2 58.6 %collective-permute-start = (bf16[256,3072]{1,0:T(8,128)(2,1)}, bf16[256,3072]{1,0:T(8,128)(2,1)}, u32[]{:S(2)}, u32[]{:S(2)}) collective-permute-start(bf16[256,3072]{1,0:T(8,128)(2,1)} %get-tuple-element.225.refs_0_), channel_id=1, source_target_pairs={{0,2},{2,0},{4,6},{6,4},{8,10},{10,8},{12,14},{14,12},{16,18},{18,... | collective-permute-start | bytes 4718600 | tf_op jit(solution)/shard_map/ppermute | solution.py:561
  388.7 26.3 %collective-permute-start.6 = (bf16[256,2048]{1,0:T(8,128)(2,1)}, bf16[256,2048]{1,0:T(8,128)(2,1)S(1)}, u32[]{:S(2)}, u32[]{:S(2)}) collective-permute-start(bf16[256,2048]{1,0:T(8,128)(2,1)} %get-tuple-element.234.refs_2_), channel_id=1, source_target_pairs={{0,4},{2,6},{4,0},{6,2},{8,12},{10,14},{12,8},{14,10},{16,20},{18,... | collective-permute-start | bytes 3145736 | tf_op jit(solution)/shard_map/ppermute | solution.py:561
  390.6 29.1 %collective-permute-start.7 = (bf16[256,2048]{1,0:T(8,128)(2,1)}, bf16[256,2048]{1,0:T(8,128)(2,1)S(1)}, u32[]{:S(2)}, u32[]{:S(2)}) collective-permute-start(bf16[256,2048]{1,0:T(8,128)(2,1)} %get-tuple-element.235.refs_4_.refs_0_), channel_id=1, source_target_pairs={{0,8},{2,10},{4,12},{6,14},{8,0},{10,2},{12,4},{14,6},{16,24},{18,... | collective-permute-start | bytes 3145736 | tf_op jit(solution)/shard_map/ppermute | solution.py:561
  390.6 68.3 %collective-permute-start.11 = (bf16[256,3072]{1,0:T(8,128)(2,1)}, bf16[256,3072]{1,0:T(8,128)(2,1)}, u32[]{:S(2)}, u32[]{:S(2)}) collective-permute-start(bf16[256,3072]{1,0:T(8,128)(2,1)} %get-tuple-element.242.refs_0_), channel_id=1, source_target_pairs={{0,4},{2,6},{4,0},{6,2},{8,12},{10,14},{12,8},{14,10},{16,20},{18,... | collective-permute-start | bytes 4718600 | tf_op jit(solution)/shard_map/ppermute | solution.py:561
  413.0 2.0 copy-start.1
  413.0 26.4 %collective-permute-start.1 = (bf16[256,2048]{1,0:T(8,128)(2,1)}, bf16[256,2048]{1,0:T(8,128)(2,1)}, u32[]{:S(2)}, u32[]{:S(2)}) collective-permute-start(bf16[256,2048]{1,0:T(8,128)(2,1)} %get-tuple-element.226.refs_2_.refs_0_), channel_id=1, source_target_pairs={{0,8},{2,10},{4,12},{6,14},{8,0},{10,2},{12,4},{14,6},{16,24},{18,... | collective-permute-start | bytes 3145736 | tf_op jit(solution)/shard_map/ppermute | solution.py:561
  415.0 1.0 copy-start.2
  415.0 39.5 %collective-permute-start.12 = (bf16[256,1024]{1,0:T(8,128)(2,1)}, bf16[256,1024]{1,0:T(8,128)(2,1)}, u32[]{:S(2)}, u32[]{:S(2)}) collective-permute-start(bf16[256,1024]{1,0:T(8,128)(2,1)} %get-tuple-element.243.refs_2_), channel_id=1, source_target_pairs={{0,8},{2,10},{4,12},{6,14},{8,0},{10,2},{12,4},{14,6},{16,24},{18,... | collective-permute-start | bytes 1572872 | tf_op jit(solution)/shard_map/ppermute | solution.py:561
  419.7 5.8 %copy-start.9 = (bf16[256,1024]{1,0:T(8,128)(2,1)S(1)}, bf16[256,1024]{1,0:T(8,128)(2,1)}, u32[]{:S(2)}) copy-start(bf16[256,1024]{1,0:T(8,128)(2,1)} %get-tuple-element.238.refs_4_) | copy-start | bytes 1572868
  419.7 19.8 %copy-start.5 = (bf16[256,1536]{1,0:T(8,128)(2,1)S(1)}, bf16[256,1536]{1,0:T(8,128)(2,1)}, u32[]{:S(2)}) copy-start(bf16[256,1536]{1,0:T(8,128)(2,1)} %get-tuple-element.236.refs_0_) | copy-start | bytes 2359300
  419.7 27.1 %copy-start.6 = (bf16[256,1536]{1,0:T(8,128)(2,1)S(1)}, bf16[256,1536]{1,0:T(8,128)(2,1)}, u32[]{:S(2)}) copy-start(bf16[256,1536]{1,0:T(8,128)(2,1)} %get-tuple-element.237.refs_2_) | copy-start | bytes 2359300
  419.7 1.0 copy-start
  425.5 29.1 %copy-start.3 = (bf16[256,1536]{1,0:T(8,128)(2,1)S(1)}, bf16[256,1536]{1,0:T(8,128)(2,1)}, u32[]{:S(2)}) copy-start(bf16[256,1536]{1,0:T(8,128)(2,1)} %get-tuple-element.227.refs_0_) | copy-start | bytes 2359300
  425.5 32.6 %copy-start.4 = (bf16[256,1536]{1,0:T(8,128)(2,1)S(1)}, bf16[256,1536]{1,0:T(8,128)(2,1)}, u32[]{:S(2)}) copy-start(bf16[256,1536]{1,0:T(8,128)(2,1)} %get-tuple-element.228.refs_2_) | copy-start | bytes 2359300
  425.5 32.6 %copy-start.10 = (f32[32,1024]{1,0:T(8,128)S(1)}, f32[32,1024]{1,0:T(8,128)}, u32[]{:S(2)}) copy-start(f32[32,1024]{1,0:T(8,128)} %get-tuple-element.240) | copy-start | bytes 393220
  425.5 32.6 %collective-permute-start.10 = (bf16[256,1024]{1,0:T(8,128)(2,1)S(1)}, bf16[256,1024]{1,0:T(8,128)(2,1)}, u32[]{:S(2)}, u32[]{:S(2)}) collective-permute-start(bf16[256,1024]{1,0:T(8,128)(2,1)S(1)} %copy-done.9), channel_id=1, source_target_pairs={{0,8},{2,10},{4,12},{6,14},{8,0},{10,2},{12,4},{14,6},{16,24},{18,... | collective-permute-start | bytes 1572872 | tf_op jit(solution)/shard_map/ppermute | solution.py:561
  439.5 33.4 %collective-permute-start.8 = (bf16[256,1536]{1,0:T(8,128)(2,1)S(1)}, bf16[256,1536]{1,0:T(8,128)(2,1)}, u32[]{:S(2)}, u32[]{:S(2)}) collective-permute-start(bf16[256,1536]{1,0:T(8,128)(2,1)S(1)} %copy-done.5), channel_id=1, source_target_pairs={{0,2},{2,0},{4,6},{6,4},{8,10},{10,8},{12,14},{14,12},{16,18},{18,... | collective-permute-start | bytes 2359304 | tf_op jit(solution)/shard_map/ppermute | solution.py:561
  446.8 26.0 %collective-permute-start.9 = (bf16[256,1536]{1,0:T(8,128)(2,1)S(1)}, bf16[256,1536]{1,0:T(8,128)(2,1)}, u32[]{:S(2)}, u32[]{:S(2)}) collective-permute-start(bf16[256,1536]{1,0:T(8,128)(2,1)S(1)} %copy-done.6), channel_id=1, source_target_pairs={{0,4},{2,6},{4,0},{6,2},{8,12},{10,14},{12,8},{14,10},{16,20},{18,... | collective-permute-start | bytes 2359304 | tf_op jit(solution)/shard_map/ppermute | solution.py:561
  454.6 26.0 %collective-permute-start.2 = (bf16[256,1536]{1,0:T(8,128)(2,1)S(1)}, bf16[256,1536]{1,0:T(8,128)(2,1)}, u32[]{:S(2)}, u32[]{:S(2)}) collective-permute-start(bf16[256,1536]{1,0:T(8,128)(2,1)S(1)} %copy-done.3), channel_id=1, source_target_pairs={{0,2},{2,0},{4,6},{6,4},{8,10},{10,8},{12,14},{14,12},{16,18},{18,... | collective-permute-start | bytes 2359304 | tf_op jit(solution)/shard_map/ppermute | solution.py:561
  458.1 22.5 %collective-permute-start.3 = (bf16[256,1536]{1,0:T(8,128)(2,1)S(1)}, bf16[256,1536]{1,0:T(8,128)(2,1)}, u32[]{:S(2)}, u32[]{:S(2)}) collective-permute-start(bf16[256,1536]{1,0:T(8,128)(2,1)S(1)} %copy-done.4), channel_id=1, source_target_pairs={{0,4},{2,6},{4,0},{6,2},{8,12},{10,14},{12,8},{14,10},{16,20},{18,... | collective-permute-start | bytes 2359304 | tf_op jit(solution)/shard_map/ppermute | solution.py:561
  458.8 21.8 %collective-permute-start.4 = (bf16[256,1024]{1,0:T(8,128)(2,1)}, bf16[256,1024]{1,0:T(8,128)(2,1)}, u32[]{:S(2)}, u32[]{:S(2)}) collective-permute-start(bf16[256,1024]{1,0:T(8,128)(2,1)} %get-tuple-element.229.refs_4_), channel_id=1, source_target_pairs={{0,8},{2,10},{4,12},{6,14},{8,0},{10,2},{12,4},{14,6},{16,24},{18,... | collective-permute-start | bytes 1572872 | tf_op jit(solution)/shard_map/ppermute | solution.py:561
  480.6 7.9 %copy-start.7 = (bf16[288,1024]{1,0:T(8,128)(2,1)S(1)}, bf16[288,1024]{1,0:T(8,128)(2,1)}, u32[]{:S(2)}) copy-start(bf16[288,1024]{1,0:T(8,128)(2,1)} %get-tuple-element.270) | copy-start | bytes 1769476
  480.6 8.7 %copy-start.8 = (bf16[288,1024]{1,0:T(8,128)(2,1)S(1)}, bf16[288,1024]{1,0:T(8,128)(2,1)}, u32[]{:S(2)}) copy-start(bf16[288,1024]{1,0:T(8,128)(2,1)} %get-tuple-element.271) | copy-start | bytes 1769476

commit v5 on v4

--- a/solution.py
+++ b/solution.py
@@ -1985,12 +1985,21 @@
     (_, input_grad, sums_one), _, bundles = groups.along(
         jobs,
         functools.partial(
-            back_end, low_one, grad, inputs, lines, slope_one, w_ffn1_in, w_ffn1_out, 4
+            back_end,
+            low_one,
+            grad,
+            inputs,
+            lines,
+            slope_one,
+            w_ffn1_in,
+            w_ffn1_out,
+            4,
+            spread=True,
         ),
     )
     mid, out, end = bundles[0], bundles[1], bundles[2]
 
-    bundles = (two, mid, out, end)
+    bundles = (out, mid, two, end)
     middle, sums = groups.middle(
         [[bundle[kind] for bundle in bundles if kind in bundle] for kind in groups.kinds],
         (
@@ -2008,7 +2017,7 @@
         2,
     )
     middle = [iter(arrays) for arrays in middle]
-    two, mid, out, end = [
+    out, mid, two, end = [
         {kind: next(middle[kind]) for kind in groups.kinds if kind in bundle} for bundle in bundles
     ]
     mid, two = groups.finish(mid), groups.finish(two)

time: 495 us -> 494 us (level)
  no operation moved by 1% of the time
where the time goes in v5:
time: 494 us; the launch traced here: 489 us
  Pallas kernels  421 us (85%)
  waiting for transfers between devices  45 us (9%)
  starting transfers between devices  10.2 us (2%)
  local copies, waits for them, and re-layouts  7.12 us (1%)
  other arithmetic  5.05 us (1%)
    pallas_call x1, Pallas kernels, sum_cube(): pl.pallas_call(functools.partial(cube_kernel, axes, plan, lines), out_sha...  179 us
    pallas_call x4, Pallas kernels, fused(): pl.pallas_call(kernel, out_shape=[jax.ShapeDtypeStruct(shape, dtype) for...  176 us
    ppermute x13, waiting for transfers between devices, swap(): return lax.ppermute(values, 'dp', [(j, j ^ bit) for j in range(self.size)])  45 us
    pallas_call x8, Pallas kernels, join(): pl.pallas_call(functools.partial(join_body, [part[0] for part in parts],...  41.3 us
    pallas_call x2, Pallas kernels, sum_and_share(): pl.pallas_call(functools.partial(pair_kernel, axes, [mode for _, mode in...  24.6 us
    ppermute x13, starting transfers between devices, swap(): return lax.ppermute(values, 'dp', [(j, j ^ bit) for j in range(self.size)])  10.2 us
  transfers between devices with their start and end apart: 13, of which 5 were waited for; matrix products, arithmetic and copies ran while one was open for 1% of the time, Pallas kernels for 7%

profile of v5, /device:TPU:0, one launch (start us, length us, event | category | flops | bytes accessed | tf_op | source)
XLA Modules:
  0.0 489.1 jit_solution(15537447308792359955)
XLA Ops:
  1.3 0.7 slice.49
  4.5 1.4 convert_bitcast_fusion.refs_0_
  5.9 29.7 %shard_map.271 = (bf16[288,1024]{1,0:T(8,128)(2,1)}, bf16[288,4096]{1,0:T(8,128)(2,1)}, bf16[288,4096]{1,0:T(8,128)(2,1)}, f32[288,1024]{1,0:T(8,128)}, bf16[288...) custom-call(f32[24,512]{1,0:T(8,128)} %convert_bitcast_fusion.refs_0, ...), custom_call_target="tpu_custom_call" | custom-call | tf_op jit(solution)/shard_map/pallas_call | solution.py:1065
  35.6 13.4 %shard_map.272.refs_0_ = f32[8,1024]{1,0:T(8,128)} custom-call(f32[8,1024]{1,0:T(8,128)} %get-tuple-element.130.refs_0_), custom_call_target="tpu_custom_call" | custom-call | tf_op jit(solution)/shard_map/pallas_call | solution.py:167
  49.0 39.9 %shard_map.273 = (bf16[288,1024]{1,0:T(8,128)(2,1)}, bf16[288,1024]{1,0:T(8,128)(2,1)}, bf16[288,4096]{1,0:T(8,128)(2,1)}, bf16[288,1024]{1,0:T(8,128)(2,1)}, bf...) custom-call(f32[8,1024]{1,0:T(8,128)} %shard_map.272.refs_0_, ...), custom_call_target="tpu_custom_call" | custom-call | tf_op jit(solution)/shard_map/pallas_call | solution.py:1065
  88.9 11.2 %shard_map.274.refs_1_ = f32[8,1024]{1,0:T(8,128)} custom-call(f32[8,1024]{1,0:T(8,128)} %get-tuple-element.135.refs_0_.refs_31_), custom_call_target="tpu_custom_call" | custom-call | tf_op jit(solution)/shard_map/pallas_call | solution.py:167
  100.1 41.7 %shard_map.275 = (bf16[288,1024]{1,0:T(8,128)(2,1)}, bf16[288,1024]{1,0:T(8,128)(2,1)}, bf16[288,1024]{1,0:T(8,128)(2,1)}, bf16[288,1024]{1,0:T(8,128)(2,1)}, bf...) custom-call(f32[8,1024]{1,0:T(8,128)} %shard_map.272.refs_0_, ...), custom_call_target="tpu_custom_call" | custom-call | tf_op jit(solution)/shard_map/pallas_call | solution.py:1065
  141.8 64.5 %shard_map.276 = (bf16[288,4096]{1,0:T(8,128)(2,1)}, bf16[288,1024]{1,0:T(8,128)(2,1)}, f32[8,1024]{1,0:T(8,128)}, bf16[288,4096]{1,0:T(8,128)(2,1)}, bf16[256,2...) custom-call(f32[24,1024]{1,0:T(8,128)} %get-tuple-element.131.refs_2, ...), custom_call_target="tpu_custom_call" | custom-call | tf_op jit(solution)/shard_map/pallas_call | solution.py:1065
  206.3 179.1 %shard_map.277 = (bf16[256,1536]{1,0:T(8,128)(2,1)}, bf16[256,2048]{1,0:T(8,128)(2,1)}, bf16[256,3072]{1,0:T(8,128)(2,1)}, bf16[256,1536]{1,0:T(8,128)(2,1)}, bf...) custom-call(bf16[256,1536]{1,0:T(8,128)(2,1)} %get-tuple-element.189, ...), custom_call_target="tpu_custom_call" | custom-call | tf_op jit(solution)/shard_map/pallas_call | solution.py:519
  385.4 1.9 collective-permute-start.5
  387.5 1.6 collective-permute-start.6
  389.6 22.3 %collective-permute-done.5.refs_1_ = bf16[256,2048]{1,0:T(8,128)(2,1)S(1)} collective-permute-done((bf16[256,2048]{1,0:T(8,128)(2,1)}, bf16[256,2048]{1,0:T(8,128)(2,1)S(1)}, u32[]{:S(2)}, u32[]{:S(2)}) %collective-permute-start.5) | collective-permute-done | bytes 1048608 | tf_op jit(solution)/shard_map/ppermute | solution.py:561
  411.8 2.0 collective-permute-done.6.refs_3_
  413.8 1.0 copy-done.2
  414.8 3.7 shard_map.281
  418.5 1.0 copy-done
  419.5 4.8 shard_map.280
  424.3 1.1 collective-permute-start.10
  425.4 12.8 %collective-permute-done.1.refs_3_.refs_1_ = bf16[256,2048]{1,0:T(8,128)(2,1)} collective-permute-done((bf16[256,2048]{1,0:T(8,128)(2,1)}, bf16[256,2048]{1,0:T(8,128)(2,1)}, u32[]{:S(2)}, u32[]{:S(2)}) %collective-permute-start.1) | collective-permute-done | bytes 1048608 | tf_op jit(solution)/shard_map/ppermute | solution.py:561
  438.2 1.8 collective-permute-start.8
  440.0 5.6 %collective-permute-done.refs_1_ = bf16[256,3072]{1,0:T(8,128)(2,1)} collective-permute-done((bf16[256,3072]{1,0:T(8,128)(2,1)}, bf16[256,3072]{1,0:T(8,128)(2,1)}, u32[]{:S(2)}, u32[]{:S(2)}) %collective-permute-start) | collective-permute-done | bytes 1572896 | tf_op jit(solution)/shard_map/ppermute | solution.py:561
  445.6 1.6 collective-permute-start.9
  447.2 5.9 %shard_map.278 = f32[512,4096]{1,0:T(8,128)} custom-call(bf16[256,3072]{1,0:T(8,128)(2,1)} %get-tuple-element.225.refs_0_, bf16[256,3072]{1,0:T(8,128)(2,1)} %collective-permute-done.refs_1_, bf16[256,2048]{1,0:T(8,128)(2,1)} %get-tuple-element.226.refs_2_.refs_0_, bf16[256,2048]{1,0:T(8,128)(2,1)} %collective-permute-done.1.refs_3_.refs_1_), custom_call_target="tpu_custom_call" | custom-call | tf_op jit(solution)/shard_map/pallas_call | solution.py:1808
  453.2 1.4 collective-permute-start.2
  454.6 2.3 collective-permute-done.10.refs_5_
  460.3 2.7 shard_map.284
  463.0 2.7 shard_map.283
  465.7 5.9 %shard_map.285 = f32[512,4096]{1,0:T(8,128)} custom-call(bf16[256,3072]{1,0:T(8,128)(2,1)} %get-tuple-element.242.refs_0_, bf16[256,3072]{1,0:T(8,128)(2,1)} %collective-permute-done.11.refs_1_, bf16[256,1024]{1,0:T(8,128)(2,1)} %get-tuple-element.243.refs_2_, bf16[256,1024]{1,0:T(8,128)(2,1)} %collective-permute-done.12.refs_3_), custom_call_target="tpu_custom_call" | custom-call | tf_op jit(solution)/shard_map/pallas_call | solution.py:1808
  471.6 7.8 %shard_map.282 = f32[512,4096]{1,0:T(8,128)} custom-call(bf16[256,1536]{1,0:T(8,128)(2,1)} %get-tuple-element.236.refs_0_, bf16[256,1536]{1,0:T(8,128)(2,1)} %collective-permute-done.8.refs_1_, bf16[256,1536]{1,0:T(8,128)(2,1)} %get-tuple-element.237.refs_2_, bf16[256,1536]{1,0:T(8,128)(2,1)} %collective-permute-done.9.refs_3_, ...), custom_call_target="tpu_custom_call" | custom-call | tf_op jit(solution)/shard_map/pallas_call | solution.py:1808
  479.4 7.8 %shard_map.279 = f32[512,4096]{1,0:T(8,128)} custom-call(bf16[256,1536]{1,0:T(8,128)(2,1)} %get-tuple-element.227.refs_0_, bf16[256,1536]{1,0:T(8,128)(2,1)} %collective-permute-done.2.refs_1_, bf16[256,1536]{1,0:T(8,128)(2,1)} %get-tuple-element.228.refs_2_, bf16[256,1536]{1,0:T(8,128)(2,1)} %collective-permute-done.3.refs_3_, ...), custom_call_target="tpu_custom_call" | custom-call | tf_op jit(solution)/shard_map/pallas_call | solution.py:1808
  487.2 0.8 copy.37
  488.1 0.8 copy.38
  (54 shorter events, 7.1 us)
Async XLA Ops:
  385.4 26.4 %collective-permute-start.5 = (bf16[256,2048]{1,0:T(8,128)(2,1)}, bf16[256,2048]{1,0:T(8,128)(2,1)S(1)}, u32[]{:S(2)}, u32[]{:S(2)}) collective-permute-start(bf16[256,2048]{1,0:T(8,128)(2,1)} %get-tuple-element.233.refs_0_), channel_id=1, source_target_pairs={{0,2},{2,0},{4,6},{6,4},{8,10},{10,8},{12,14},{14,12},{16,18},{18,... | collective-permute-start | bytes 3145736 | tf_op jit(solution)/shard_map/ppermute | solution.py:561
  387.3 58.3 %collective-permute-start = (bf16[256,3072]{1,0:T(8,128)(2,1)}, bf16[256,3072]{1,0:T(8,128)(2,1)}, u32[]{:S(2)}, u32[]{:S(2)}) collective-permute-start(bf16[256,3072]{1,0:T(8,128)(2,1)} %get-tuple-element.225.refs_0_), channel_id=1, source_target_pairs={{0,2},{2,0},{4,6},{6,4},{8,10},{10,8},{12,14},{14,12},{16,18},{18,... | collective-permute-start | bytes 4718600 | tf_op jit(solution)/shard_map/ppermute | solution.py:561
  387.5 26.3 %collective-permute-start.6 = (bf16[256,2048]{1,0:T(8,128)(2,1)}, bf16[256,2048]{1,0:T(8,128)(2,1)S(1)}, u32[]{:S(2)}, u32[]{:S(2)}) collective-permute-start(bf16[256,2048]{1,0:T(8,128)(2,1)} %get-tuple-element.234.refs_2_), channel_id=1, source_target_pairs={{0,4},{2,6},{4,0},{6,2},{8,12},{10,14},{12,8},{14,10},{16,20},{18,... | collective-permute-start | bytes 3145736 | tf_op jit(solution)/shard_map/ppermute | solution.py:561
  389.1 29.3 %collective-permute-start.7 = (bf16[256,2048]{1,0:T(8,128)(2,1)}, bf16[256,2048]{1,0:T(8,128)(2,1)S(1)}, u32[]{:S(2)}, u32[]{:S(2)}) collective-permute-start(bf16[256,2048]{1,0:T(8,128)(2,1)} %get-tuple-element.235.refs_4_.refs_0_), channel_id=1, source_target_pairs={{0,8},{2,10},{4,12},{6,14},{8,0},{10,2},{12,4},{14,6},{16,24},{18,... | collective-permute-start | bytes 3145736 | tf_op jit(solution)/shard_map/ppermute | solution.py:561
  389.1 68.4 %collective-permute-start.11 = (bf16[256,3072]{1,0:T(8,128)(2,1)}, bf16[256,3072]{1,0:T(8,128)(2,1)}, u32[]{:S(2)}, u32[]{:S(2)}) collective-permute-start(bf16[256,3072]{1,0:T(8,128)(2,1)} %get-tuple-element.242.refs_0_), channel_id=1, source_target_pairs={{0,4},{2,6},{4,0},{6,2},{8,12},{10,14},{12,8},{14,10},{16,20},{18,... | collective-permute-start | bytes 4718600 | tf_op jit(solution)/shard_map/ppermute | solution.py:561
  411.8 2.0 copy-start.1
  411.8 26.4 %collective-permute-start.1 = (bf16[256,2048]{1,0:T(8,128)(2,1)}, bf16[256,2048]{1,0:T(8,128)(2,1)}, u32[]{:S(2)}, u32[]{:S(2)}) collective-permute-start(bf16[256,2048]{1,0:T(8,128)(2,1)} %get-tuple-element.226.refs_2_.refs_0_), channel_id=1, source_target_pairs={{0,8},{2,10},{4,12},{6,14},{8,0},{10,2},{12,4},{14,6},{16,24},{18,... | collective-permute-start | bytes 3145736 | tf_op jit(solution)/shard_map/ppermute | solution.py:561
  413.8 1.0 copy-start.2
  413.8 39.3 %collective-permute-start.12 = (bf16[256,1024]{1,0:T(8,128)(2,1)}, bf16[256,1024]{1,0:T(8,128)(2,1)}, u32[]{:S(2)}, u32[]{:S(2)}) collective-permute-start(bf16[256,1024]{1,0:T(8,128)(2,1)} %get-tuple-element.243.refs_2_), channel_id=1, source_target_pairs={{0,8},{2,10},{4,12},{6,14},{8,0},{10,2},{12,4},{14,6},{16,24},{18,... | collective-permute-start | bytes 1572872 | tf_op jit(solution)/shard_map/ppermute | solution.py:561
  418.5 5.8 %copy-start.9 = (bf16[256,1024]{1,0:T(8,128)(2,1)S(1)}, bf16[256,1024]{1,0:T(8,128)(2,1)}, u32[]{:S(2)}) copy-start(bf16[256,1024]{1,0:T(8,128)(2,1)} %get-tuple-element.238.refs_4_) | copy-start | bytes 1572868
  418.5 19.7 %copy-start.5 = (bf16[256,1536]{1,0:T(8,128)(2,1)S(1)}, bf16[256,1536]{1,0:T(8,128)(2,1)}, u32[]{:S(2)}) copy-start(bf16[256,1536]{1,0:T(8,128)(2,1)} %get-tuple-element.236.refs_0_) | copy-start | bytes 2359300
  418.5 27.1 %copy-start.6 = (bf16[256,1536]{1,0:T(8,128)(2,1)S(1)}, bf16[256,1536]{1,0:T(8,128)(2,1)}, u32[]{:S(2)}) copy-start(bf16[256,1536]{1,0:T(8,128)(2,1)} %get-tuple-element.237.refs_2_) | copy-start | bytes 2359300
  418.5 1.0 copy-start
  424.3 28.9 %copy-start.3 = (bf16[256,1536]{1,0:T(8,128)(2,1)S(1)}, bf16[256,1536]{1,0:T(8,128)(2,1)}, u32[]{:S(2)}) copy-start(bf16[256,1536]{1,0:T(8,128)(2,1)} %get-tuple-element.227.refs_0_) | copy-start | bytes 2359300
  424.3 32.6 %copy-start.4 = (bf16[256,1536]{1,0:T(8,128)(2,1)S(1)}, bf16[256,1536]{1,0:T(8,128)(2,1)}, u32[]{:S(2)}) copy-start(bf16[256,1536]{1,0:T(8,128)(2,1)} %get-tuple-element.228.refs_2_) | copy-start | bytes 2359300
  424.3 32.6 %copy-start.10 = (f32[32,1024]{1,0:T(8,128)S(1)}, f32[32,1024]{1,0:T(8,128)}, u32[]{:S(2)}) copy-start(f32[32,1024]{1,0:T(8,128)} %get-tuple-element.240) | copy-start | bytes 393220
  424.3 32.6 %collective-permute-start.10 = (bf16[256,1024]{1,0:T(8,128)(2,1)S(1)}, bf16[256,1024]{1,0:T(8,128)(2,1)}, u32[]{:S(2)}, u32[]{:S(2)}) collective-permute-start(bf16[256,1024]{1,0:T(8,128)(2,1)S(1)} %copy-done.9), channel_id=1, source_target_pairs={{0,8},{2,10},{4,12},{6,14},{8,0},{10,2},{12,4},{14,6},{16,24},{18,... | collective-permute-start | bytes 1572872 | tf_op jit(solution)/shard_map/ppermute | solution.py:561
  438.2 33.4 %collective-permute-start.8 = (bf16[256,1536]{1,0:T(8,128)(2,1)S(1)}, bf16[256,1536]{1,0:T(8,128)(2,1)}, u32[]{:S(2)}, u32[]{:S(2)}) collective-permute-start(bf16[256,1536]{1,0:T(8,128)(2,1)S(1)} %copy-done.5), channel_id=1, source_target_pairs={{0,2},{2,0},{4,6},{6,4},{8,10},{10,8},{12,14},{14,12},{16,18},{18,... | collective-permute-start | bytes 2359304 | tf_op jit(solution)/shard_map/ppermute | solution.py:561
  445.6 26.0 %collective-permute-start.9 = (bf16[256,1536]{1,0:T(8,128)(2,1)S(1)}, bf16[256,1536]{1,0:T(8,128)(2,1)}, u32[]{:S(2)}, u32[]{:S(2)}) collective-permute-start(bf16[256,1536]{1,0:T(8,128)(2,1)S(1)} %copy-done.6), channel_id=1, source_target_pairs={{0,4},{2,6},{4,0},{6,2},{8,12},{10,14},{12,8},{14,10},{16,20},{18,... | collective-permute-start | bytes 2359304 | tf_op jit(solution)/shard_map/ppermute | solution.py:561
  453.2 26.2 %collective-permute-start.2 = (bf16[256,1536]{1,0:T(8,128)(2,1)S(1)}, bf16[256,1536]{1,0:T(8,128)(2,1)}, u32[]{:S(2)}, u32[]{:S(2)}) collective-permute-start(bf16[256,1536]{1,0:T(8,128)(2,1)S(1)} %copy-done.3), channel_id=1, source_target_pairs={{0,2},{2,0},{4,6},{6,4},{8,10},{10,8},{12,14},{14,12},{16,18},{18,... | collective-permute-start | bytes 2359304 | tf_op jit(solution)/shard_map/ppermute | solution.py:561
  456.9 22.5 %collective-permute-start.3 = (bf16[256,1536]{1,0:T(8,128)(2,1)S(1)}, bf16[256,1536]{1,0:T(8,128)(2,1)}, u32[]{:S(2)}, u32[]{:S(2)}) collective-permute-start(bf16[256,1536]{1,0:T(8,128)(2,1)S(1)} %copy-done.4), channel_id=1, source_target_pairs={{0,4},{2,6},{4,0},{6,2},{8,12},{10,14},{12,8},{14,10},{16,20},{18,... | collective-permute-start | bytes 2359304 | tf_op jit(solution)/shard_map/ppermute | solution.py:561
  457.6 21.8 %collective-permute-start.4 = (bf16[256,1024]{1,0:T(8,128)(2,1)}, bf16[256,1024]{1,0:T(8,128)(2,1)}, u32[]{:S(2)}, u32[]{:S(2)}) collective-permute-start(bf16[256,1024]{1,0:T(8,128)(2,1)} %get-tuple-element.229.refs_4_), channel_id=1, source_target_pairs={{0,8},{2,10},{4,12},{6,14},{8,0},{10,2},{12,4},{14,6},{16,24},{18,... | collective-permute-start | bytes 1572872 | tf_op jit(solution)/shard_map/ppermute | solution.py:561
  479.4 7.9 %copy-start.7 = (bf16[288,1024]{1,0:T(8,128)(2,1)S(1)}, bf16[288,1024]{1,0:T(8,128)(2,1)}, u32[]{:S(2)}) copy-start(bf16[288,1024]{1,0:T(8,128)(2,1)} %get-tuple-element.270) | copy-start | bytes 1769476
  479.4 8.7 %copy-start.8 = (bf16[288,1024]{1,0:T(8,128)(2,1)S(1)}, bf16[288,1024]{1,0:T(8,128)(2,1)}, u32[]{:S(2)}) copy-start(bf16[288,1024]{1,0:T(8,128)(2,1)} %get-tuple-element.271) | copy-start | bytes 1769476
